TPU v7x, 256 devices: a whole 4x4x8 slice. The times are simulated.
256 devices in a mesh: frag: 16 (over z, core), grp: 16 (over y, x).
Axes of the slice: x: 4, y: 4, z: 8, core: 2. Of those that a mesh axis runs over, the one named last changes fastest.
Arguments:
- background: float32 [512, 512, 512], P('frag', 'grp'), may hold values from 0.25 to 4
- orbitals: bfloat16 [16, 16, 16, 8192], P(None, None, None, ('frag', 'grp')), may hold values from -3 to 3
- frag_info: int32 [512, 8], P(('frag', 'grp')), may hold values from -1 to 31, as said below
Outputs:
- total_density: float32 [512, 512, 512], P('frag', 'grp')
- frag_potential: float32 [512, 32768], P(('frag', 'grp'))
Inputs may be any that keep to these rules, and one draw needn't show every extreme that they name: `frag_info`: row r belongs to the device r // 2 in the order frag then grp. A fragment's root x cell lies in the block of x cells that its device's frag index holds of total_density. Sizes are 1 or 2; the sign is -1 to the power of the number of sizes equal to 1; count lies between the number of cells of the box and twice it, and every device holds a fragment with count 16. Counting, for each grp block of total_density's second dimension, the fragments of one device that have box rows in it: at most 2, and in every frag group some block gets 2 from every device of the group.
All inputs are finite; a program needn't handle non-finite values.
Results may differ from a plain program's by a relative error of at most 0.0003.
Values sent between devices are 32-bit elements; how exact they have to be, the bound alone decides.
No kernel may reach another device: no remote copies, remote signals or barrier semaphores. Data moves between devices by JAX's collectives and lax.ppermute only.
A program may use at most 128 MiB of HBM per device.

v0:
```python
import math

import jax
import jax.numpy as jnp
from jax import lax
from jax.sharding import PartitionSpec as P

SPACING = 0.2
HIGHEST = lax.Precision.HIGHEST


def passed_along(block, axis, distance):
    devices = range(lax.axis_size(axis))
    route = [((i - distance) % len(devices), i) for i in devices]
    return lax.ppermute(block, axis, route)


def synthesis_tables(span_cells, cell_edge):
    frequency = jnp.arange(cell_edge, dtype=jnp.int32) - cell_edge // 2
    grid_point = jnp.arange(2 * cell_edge, dtype=jnp.int32)
    box_span = span_cells * cell_edge
    residue = jnp.mod(frequency[:, None, None] * grid_point[None, :, None], box_span[None, None, :])
    angle_value = (
        2.0 * math.pi * residue.astype(jnp.float32) / box_span.astype(jnp.float32)[None, None, :]
    )
    quarter = box_span // 4
    live_mask = (
        (frequency[:, None, None] >= -quarter[None, None, :])
        & (frequency[:, None, None] < quarter[None, None, :])
        & (grid_point[None, :, None] < box_span[None, None, :])
    )
    weight = math.sqrt(2.0 / cell_edge) / span_cells.astype(jnp.float32)
    return jnp.where(
        live_mask, (jnp.cos(angle_value) + jnp.sin(angle_value)) * weight[None, None, :], 0.0
    )


def hartley_rows(row_waves, length):
    positions = jnp.arange(length, dtype=jnp.int32)
    residue = jnp.mod(row_waves[:, None] * positions[None, :], length)
    angle_value = 2.0 * math.pi / length * residue.astype(jnp.float32)
    return jnp.cos(angle_value) + jnp.sin(angle_value)


def hartley_table(length):
    return hartley_rows(jnp.arange(length, dtype=jnp.int32), length)


def poisson_kernel(axis_one, axis_two, axis_three, length):

    def folded_square(wave_index):
        lowest = jnp.minimum(wave_index, length - wave_index)
        return lowest * lowest

    square_sum = folded_square(axis_one) + folded_square(axis_two) + folded_square(axis_three)
    factor = (length * SPACING) ** 2 / math.pi
    return jnp.where(square_sum > 0, factor / jnp.maximum(square_sum, 1).astype(jnp.float32), 0.0)


def unit_plan(frag_rows, groups, block_cells, cell_total):
    start_y = frag_rows[:, 1]
    first_owner = start_y // block_cells
    next_owner = jnp.mod(start_y + 1, cell_total) // block_cells
    crossing = (frag_rows[:, 4] == 2) & (next_owner != first_owner)
    owners = jnp.concatenate([first_owner, next_owner])
    usable = jnp.concatenate([jnp.ones_like(crossing), crossing])
    onehot = (
        (owners[:, None] == jnp.arange(groups, dtype=jnp.int32)[None, :]) & usable[:, None]
    ).astype(jnp.int32)
    earlier = jnp.cumsum(onehot, axis=0) - onehot
    places = jnp.sum(earlier * onehot, axis=1)
    return (owners, usable, places)


def unit_root(frag_rows, owners, cell_edge, x_block, y_block, grid_len, frag_pos):
    rows_twice = jnp.concatenate([frag_rows, frag_rows], 0)
    root_x = rows_twice[:, 0] * cell_edge - frag_pos * x_block
    root_y = (
        jnp.mod(rows_twice[:, 1] * cell_edge - owners * y_block + cell_edge, grid_len) - cell_edge
    )
    root_z = rows_twice[:, 2] * cell_edge
    return jnp.stack([root_x, root_y, root_z], axis=1)


def body(background, orbitals, frag_info):
    x_block, y_block, grid_len = background.shape
    cell_edge = orbitals.shape[0]
    box_len = 2 * cell_edge
    box_points = box_len * box_len * box_len
    frag_count = frag_info.shape[0]
    most_orbs = orbitals.shape[3] // frag_count
    groups = lax.axis_size("grp")
    frag_pos = lax.axis_index("frag")
    grp_pos = lax.axis_index("grp")
    cell_total = grid_len // cell_edge
    block_cells = y_block // cell_edge
    capacity = 2 * ((frag_count + groups - 1) // groups)
    per_block = min(frag_count, 4)

    def block_density(block_pos):
        coeffs = orbitals
        coeffs = coeffs.astype(jnp.float32).reshape(
            cell_edge, cell_edge, cell_edge, per_block, most_orbs
        )
        table_x = synthesis_tables(frag_info[:, 3], cell_edge)
        table_y = synthesis_tables(frag_info[:, 4], cell_edge)
        table_z = synthesis_tables(frag_info[:, 5], cell_edge)
        partial_value = jnp.einsum("abcfm,czf->abzfm", coeffs, table_z, precision=HIGHEST)
        partial_value = jnp.einsum("abzfm,byf->ayzfm", partial_value, table_y, precision=HIGHEST)
        partial_value = jnp.einsum("ayzfm,axf->xyzfm", partial_value, table_x, precision=HIGHEST)
        occupied = (jnp.arange(most_orbs, dtype=jnp.int32)[None, :] < frag_info[:, 7:8]).astype(
            jnp.float32
        )
        return 2.0 * jnp.sum(partial_value * partial_value * occupied, axis=4)

    blocks = lax.map(block_density, jnp.arange(frag_count // per_block, dtype=jnp.int32))
    density = jnp.transpose(blocks, (0, 4, 1, 2, 3)).reshape(frag_count, box_len, box_len, box_len)
    signed = frag_info[:, 6].astype(jnp.float32)[:, None, None, None] * density
    owners, usable, places = unit_plan(frag_info, groups, block_cells, cell_total)
    rows_twice = jnp.concatenate([frag_info, frag_info], 0)
    steps_box = jnp.arange(box_len, dtype=jnp.int32)
    row_owner = jnp.mod(rows_twice[:, 1:2] * cell_edge + steps_box[None, :], grid_len) // y_block
    row_mask = ((row_owner == owners[:, None]) & usable[:, None]).astype(jnp.float32)
    pieces = (jnp.concatenate([signed, signed], 0) * row_mask[:, None, :, None]).reshape(
        2 * frag_count, box_points
    )
    column = owners * capacity + places
    select = (
        (column[:, None] == jnp.arange(groups * capacity, dtype=jnp.int32)[None, :])
        & usable[:, None]
    ).astype(jnp.float32)
    outgoing = jnp.dot(
        select.T, pieces, precision=HIGHEST, preferred_element_type=jnp.float32
    ).reshape(groups, capacity, box_points)
    incoming = lax.all_to_all(outgoing, "grp", split_axis=0, concat_axis=0, tiled=True)
    every_rows = lax.all_gather(frag_info, "grp", axis=0, tiled=True).reshape(groups, frag_count, 8)

    def slot_roots(source_rows):
        source_owners, source_usable, source_places = unit_plan(
            source_rows, groups, block_cells, cell_total
        )
        roots = unit_root(
            source_rows, source_owners, cell_edge, x_block, y_block, grid_len, frag_pos
        )
        landing = source_usable & (source_owners == grp_pos)
        picking = (
            landing[:, None]
            & (source_places[:, None] == jnp.arange(capacity, dtype=jnp.int32)[None, :])
        ).astype(jnp.int32)
        return jnp.sum(picking[:, :, None] * roots[:, None, :], axis=0)

    slot_places = jax.vmap(slot_roots)(every_rows).reshape(groups * capacity, 3)
    incoming = incoming.reshape(groups * capacity, box_len, box_len, box_len)
    anchors = slot_places + jnp.array([0, 1, 0], dtype=jnp.int32)[None, :] * cell_edge
    region = jnp.zeros(
        (x_block + cell_edge, y_block + 2 * cell_edge, grid_len + cell_edge), jnp.float32
    )

    def place_slot(slot, current):
        corner = (anchors[slot, 0], anchors[slot, 1], anchors[slot, 2])
        window = lax.dynamic_slice(current, corner, (box_len, box_len, box_len))
        return lax.dynamic_update_slice(current, window + incoming[slot], corner)

    region = lax.fori_loop(0, groups * capacity, place_slot, region)
    region = region[:, cell_edge : cell_edge + y_block, :]
    region = region[:, :, :grid_len].at[:, :, :cell_edge].add(region[:, :, grid_len:])
    spilled = passed_along(region[x_block:], "frag", 1)
    deposit = region[:x_block].at[:cell_edge].add(spilled)
    total_density = background + deposit
    hartley = hartley_table(grid_len)
    spectrum = jnp.einsum("xyz,zk->xky", total_density, hartley, precision=HIGHEST)
    spectrum = lax.all_to_all(spectrum, "grp", split_axis=1, concat_axis=2, tiled=True)
    spectrum = jnp.einsum("xky,yl->lkx", spectrum, hartley, precision=HIGHEST)
    spectrum = lax.all_to_all(spectrum, "frag", split_axis=0, concat_axis=2, tiled=True)
    spectrum = jnp.einsum("lkx,xm->lkm", spectrum, hartley, precision=HIGHEST)
    rows_len, depth_len = (spectrum.shape[0], spectrum.shape[1])
    rows_wave = frag_pos * rows_len + jnp.arange(rows_len, dtype=jnp.int32)
    depth_wave = grp_pos * depth_len + jnp.arange(depth_len, dtype=jnp.int32)
    cols_wave = jnp.arange(grid_len, dtype=jnp.int32)
    kernel = poisson_kernel(
        rows_wave[:, None, None], depth_wave[None, :, None], cols_wave[None, None, :], grid_len
    )
    spectrum = spectrum * kernel
    inverse = jnp.einsum("lkm,mx->lkx", spectrum, hartley, precision=HIGHEST)
    inverse = lax.all_to_all(inverse, "frag", split_axis=2, concat_axis=0, tiled=True)
    inverse = jnp.einsum("lkx,ly->xky", inverse, hartley, precision=HIGHEST)
    inverse = lax.all_to_all(inverse, "grp", split_axis=2, concat_axis=1, tiled=True)
    inverse = jnp.einsum("xky,kz->xyz", inverse, hartley, precision=HIGHEST)
    potential = inverse * (1.0 / float(grid_len) ** 3)
    upper = passed_along(potential[:cell_edge], "frag", -1)
    widened = jnp.concatenate([potential, upper], 0)
    widened = jnp.pad(widened, ((0, 0), (cell_edge, cell_edge), (0, 0)))
    widened = jnp.concatenate([widened, widened[:, :, :cell_edge]], 2)

    def read_slot(corner):
        return lax.dynamic_slice(
            widened, (corner[0], corner[1], corner[2]), (box_len, box_len, box_len)
        )

    outgoing_back = lax.map(read_slot, anchors).reshape(groups, capacity, box_points)
    returned = lax.all_to_all(
        outgoing_back, "grp", split_axis=0, concat_axis=0, tiled=True
    ).reshape(groups * capacity, box_points)
    picked = jnp.dot(select, returned, precision=HIGHEST, preferred_element_type=jnp.float32)
    merged = (picked[:frag_count] + picked[frag_count:]).reshape(
        frag_count, box_len, box_len, box_len
    )
    extent = frag_info[:, 3:6] * cell_edge
    inside = (
        (steps_box[None, :, None, None] < extent[:, 0][:, None, None, None])
        & (steps_box[None, None, :, None] < extent[:, 1][:, None, None, None])
        & (steps_box[None, None, None, :] < extent[:, 2][:, None, None, None])
    )
    frag_potential = jnp.where(inside, merged, 0.0).reshape(frag_count, box_points)
    return (total_density, frag_potential)


def solution(mesh):
    return jax.shard_map(
        body,
        mesh=mesh,
        in_specs=(
            P("frag", "grp", None),
            P(None, None, None, ("frag", "grp")),
            P(("frag", "grp"), None),
        ),
        out_specs=(P("frag", "grp", None), P(("frag", "grp"), None)),
        check_vma=False,
    )
```

profile of v0, /device:TPU:1, one launch (start us, length us, event | category | flops | bytes accessed | tf_op | source)
XLA Modules:
  0.0 1674.8 jit_solution(17378869445778703779)
XLA Ops:
  11.3 8.0 fusion.4
  19.3 22.8 %multiply_reduce_fusion = f32[2,32,32,32]{3,1,2,0:T(8,128)S(1)} fusion(f32[16,32,32,2,16]{2,1,4,0,3:T(8,128)S(1)} %fusion.4, f32[2,16]{1,0:T(2,128)S(1)} %compare_convert_fusion, s32[2]{0:T(128)S(1)} %get-tuple-element.208, s32[16,32]{1,0:T(8,128)S(1)} %multiply_bitcast_fusion.1, f32[2]{0:T(128)S(1)} %get-tuple-element.154, f32[2]{0:T(128)S(1)} %get-tuple-element.199, ...), kind=kOutput, calls=%fused_computation.6 | convolution fusion | flops 204421120 | bytes 2361594 | tf_op jit(solution)/shard_map/while/body/eval_jaxpr/ayzfm,axf->xyzfm/dot_general | solution.py:110
  52.9 7.8 all-to-all-start
  60.7 71.4 %all-gather = s32[16,2,8]{2,1,0:T(2,128)S(1)} all-gather(s32[1,2,8]{2,1,0:T(2,128)S(1)} %bitcast.185), channel_id=1, replica_groups=mesh['frag'=16,'grp'=16] {'grp'}, dimensions={0}, use_global_device_ids=true | all-gather | bytes 1088 | tf_op jit(solution)/shard_map/all_gather | solution.py:136
  133.4 15.4 reshape.893
  152.8 490.9 %while.29 = (s32[]{:T(128)}, f32[48,64,528]{2,1,0:T(8,128)}, s32[32,3]{0,1:T(4,128)S(1)}, f32[32,32,32,32]{3,2,1,0:T(8,128)}, s32[]{:T(128)}, /*index=5*/s32[]{:T(128)}, s32[]{:T(128)}, s32[]{:T(128)}, s32[]{:T(128)}) while((s32[]{:T(128)}, f32[48,64,528]{2,1,0:T(8,128)}, s32[32,3]{0,1:T(4,128)S(1)}, f32[32,32,32,32]{3,2,1,0:T(8,128)}, ...), condition=%wide.region_7.9_spmd, body=%wide.region_6.8_spmd.sunk | while | flops 32779 | bytes 655603 | solution.py:164
  247.2 14.0 dynamic_update_slice.17
  398.7 13.9 dynamic_update_slice.17
  492.6 14.0 dynamic_update_slice.17
  529.1 14.0 dynamic_update_slice.17
  652.8 11.5 collective-permute-done
  666.5 8.6 convolution_bitcast_fusion.2
  690.3 235.7 %all_to_all.82 = f32[16,1,32768]{2,1,0:T(1,128)} all-to-all(f32[16,1,32768]{2,1,0:T(1,128)S(1)} %reshape.926), channel_id=1, replica_groups=mesh['frag'=16,'grp'=16] {'grp'}, dimensions={0} | all-to-all | bytes 4194304 | tf_op jit(solution)/shard_map/all_to_all | solution.py:172
  938.5 11.4 copy.135
  956.6 8.6 convolution_bitcast_fusion.1
  965.2 8.4 copy.117
  973.6 8.6 reshape.928
  988.2 48.8 %all-to-all-done.2 = f32[16,1,32768]{2,1,0:T(1,128)} async-done(((f32[16,1,32768]{2,1,0:T(1,128)}), f32[16,1,32768]{2,1,0:T(1,128)}, u32[]{:S(2)}, u32[]{:S(2)}) %all-to-all-start.2) | async-done | bytes 2097184 | tf_op jit(solution)/shard_map/all_to_all | solution.py:174
  1049.0 9.0 copy.118
  1064.3 8.9 fusion.21
  1073.2 8.2 fusion.11
  1096.5 56.3 %all_to_all.83 = f32[16,1,32768]{2,1,0:T(1,128)} all-to-all(f32[16,1,32768]{2,1,0:T(1,128)S(1)} %reshape.930), channel_id=1, replica_groups=mesh['frag'=16,'grp'=16] {'frag'}, dimensions={0} | all-to-all | bytes 4194304 | tf_op jit(solution)/shard_map/all_to_all | solution.py:185
  1164.8 9.1 copy.120
  1180.2 8.8 fusion.39
  1189.0 8.4 copy.121
  1204.8 31.6 %all_to_all.84 = f32[16,1,32768]{2,1,0:T(1,128)} all-to-all(f32[16,1,32768]{2,1,0:T(1,128)S(1)} %reshape.932), channel_id=1, replica_groups=mesh['frag'=16,'grp'=16] {'grp'}, dimensions={0} | all-to-all | bytes 4194304 | tf_op jit(solution)/shard_map/all_to_all | solution.py:187
  1248.4 9.1 copy.122
  1264.8 10.4 convolution_multiply_fusion
  1276.3 14.4 collective-permute-done.1
  1295.9 284.5 %while.30 = (s32[]{:T(128)}, f32[32,32,32,32]{3,2,1,0:T(8,128)}, s32[32,3]{0,1:T(4,128)S(1)}, f32[48,64,528]{2,1,0:T(8,128)}, s32[]{:T(128)}, /*index=5*/s32[]{:T(128)}, s32[]{:T(128)}, s32[]{:T(128)}, s32[]{:T(128)}) while((s32[]{:T(128)}, f32[32,32,32,32]{3,2,1,0:T(8,128)}, s32[32,3]{0,1:T(4,128)S(1)}, f32[48,64,528]{2,1,0:T(8,128)}, ...), condition=%wide.region_9.11_spmd, body=%wide.region_8.10_spmd.sunk | while | flops 11 | bytes 1049347 | solution.py:200
  1580.4 16.7 reshape.894
  1603.0 60.7 %all-to-all-done.5 = f32[16,2,32768]{2,1,0:T(2,128)} async-done(((f32[16,2,32768]{2,1,0:T(2,128)}), f32[16,2,32768]{2,1,0:T(2,128)}, u32[]{:S(2)}, u32[]{:S(2)}) %all-to-all-start.5) | async-done | bytes 4194336 | tf_op jit(solution)/shard_map/all_to_all | solution.py:201
  (297 shorter events, 529.3 us)
Async XLA Ops:
  52.9 7.8 copy-start.2
  52.9 80.4 %copy-start.3 = (s32[3]{0:T(128)S(1)}, s32[3]{0:T(128)}, u32[]{:S(2)}) copy-start(s32[3]{0:T(128)} %constant.328) | copy-start | bytes 40
  52.9 80.4 %all-to-all-start = ((f32[16,2,32768]{2,1,0:T(2,128)}), f32[16,2,32768]{2,1,0:T(2,128)}, u32[]{:S(2)}, u32[]{:S(2)}) async-start(f32[16,2,32768]{2,1,0:T(2,128)} %copy.114), calls=%async_computation | async-start | bytes 8388608 | tf_op jit(solution)/shard_map/all_to_all | solution.py:135
  652.6 11.8 collective-permute-start
  652.8 11.8 copy-start
  665.2 1.3 copy-start.1
  982.2 54.8 %all-to-all-start.2 = ((f32[16,1,32768]{2,1,0:T(1,128)}), f32[16,1,32768]{2,1,0:T(1,128)}, u32[]{:S(2)}, u32[]{:S(2)}) async-start(f32[16,1,32768]{2,1,0:T(1,128)} %reshape.928), calls=%async_computation.2 | async-start | bytes 4194304 | tf_op jit(solution)/shard_map/all_to_all | solution.py:174
  1276.3 14.4 collective-permute-start.1
  1597.0 66.6 %all-to-all-start.5 = ((f32[16,2,32768]{2,1,0:T(2,128)}), f32[16,2,32768]{2,1,0:T(2,128)}, u32[]{:S(2)}, u32[]{:S(2)}) async-start(f32[16,2,32768]{2,1,0:T(2,128)} %reshape.894), calls=%async_computation.5 | async-start | bytes 8388608 | tf_op jit(solution)/shard_map/all_to_all | solution.py:201
where the time goes:
time: 1700 us; the launch traced here: 1670 us
  local copies, waits for them, and re-layouts  562 us (33%)
  blocking collectives  395 us (23%)
  loops' own time  369 us (22%)
  waiting for transfers between devices  135 us (8%)
  other arithmetic  101 us (6%)
  matrix products  92.6 us (5%)
  starting transfers between devices  18.2 us (1%)
    all_to_all x1, blocking collectives, body(): lax.all_to_all(spectrum, 'grp', split_axis=1, concat_axis=2, tiled=True)  236 us
    dynamic_update_slice x32, local copies, waits for them, and re-layouts, place_slot(): return lax.dynamic_update_slice(current, window + incoming[slot], corner)  232 us
    another operation x1, loops' own time, body(): lax.map(read_slot, anchors).reshape(groups, capacity, box_points)  187 us
    another operation x1, loops' own time, body(): region = lax.fori_loop(0, groups * capacity, place_slot, region)  183 us
    dynamic_update_slice x32, local copies, waits for them, and re-layouts, body(): lax.map(read_slot, anchors).reshape(groups, capacity, box_points)  76.4 us
    all_gather x1, blocking collectives, body(): lax.all_gather(frag_info, 'grp', axis=0, tiled=True)  71.4 us
    all_to_all x1, waiting for transfers between devices, body(): lax.all_to_all(outgoing_back, 'grp', split_axis=0, concat_axis=0, tiled=T...  60.7 us
    unnamed x17, local copies, waits for them, and re-layouts  57.5 us
  transfers between devices with their start and end apart: 5, of which 4 were waited for; matrix products, arithmetic and copies ran while one was open for 0% of the time, Pallas kernels for 0%

commit v1 on v0

v1 whole, which is shorter than its diff:
```python
import math

import jax
import jax.numpy as jnp
import ml_dtypes
import numpy as np
from jax import lax
from jax.experimental import pallas as pl
from jax.experimental.pallas import tpu as pltpu
from jax.sharding import PartitionSpec as P

NG = 512
SPACING = 0.2
F32 = jnp.float32
BF16 = jnp.bfloat16
BOTH = ("frag", "grp")
VMEM_LIMIT = 56 * 1024 * 1024


def halves(table):
    high = table.astype(ml_dtypes.bfloat16)
    low = (table - high.astype(np.float64)).astype(ml_dtypes.bfloat16)
    return np.stack([high, low])


def synthesis_table(span):
    frequency = np.arange(16)[:, None] - 8
    point = np.arange(32)[None, :]
    angle = 2.0 * math.pi * np.mod(frequency * point, span * 16) / (span * 16)
    live = (frequency >= -4 * span) & (frequency < 4 * span) & (point < 16 * span)
    return np.where(live, (np.cos(angle) + np.sin(angle)) * math.sqrt(2.0 / 16) / span, 0.0)


def plane_tables():
    tables = []
    for span_y in (1, 2):
        for span_z in (1, 2):
            table_y = synthesis_table(span_y).reshape(16, 2, 16)
            table_z = synthesis_table(span_z)
            full = np.einsum("brg,cz->bcgrz", table_y, table_z)
            tables.append(halves(full.reshape(256, 1024)))
    return np.stack(tables)


def depth_tables():
    tables = []
    for span in (1, 2):
        full = np.einsum("ax,mn->mxan", synthesis_table(span), np.eye(16))
        tables.append(halves(full.reshape(512, 256)))
    return np.stack(tables)


def hartley():
    index = np.arange(NG)
    angle = 2.0 * math.pi / NG * np.mod(index[:, None] * index[None, :], NG)
    return np.cos(angle) + np.sin(angle)


def row_order():
    block, low, high = np.meshgrid(np.arange(16), np.arange(4), np.arange(8), indexing="ij")
    return (block * 32 + high * 4 + low).reshape(-1)


def cyclic_order():
    residue, cell = np.meshgrid(np.arange(16), np.arange(32), indexing="ij")
    return (cell * 16 + residue).reshape(-1)


def split(value):
    high = value.astype(BF16)
    return high, (value - high.astype(F32)).astype(BF16)


def product(left, right, dims):
    dims = (dims, ((), ()))
    total = lax.dot_general(left[0], right[1], dims, preferred_element_type=F32)
    total += lax.dot_general(left[1], right[0], dims, preferred_element_type=F32)
    return total + lax.dot_general(left[0], right[0], dims, preferred_element_type=F32)


NN = ((1,), (0,))
NT = ((1,), (1,))
TN = ((0,), (0,))


def lanes_of(shape):
    return lax.broadcasted_iota(jnp.int32, shape, len(shape) - 1)


def exchange(parts):
    lane = lanes_of(parts[0].shape)
    low = lane < 64
    even = (lane & 32) == 0
    v0, v1, v2, v3 = parts
    a0 = jnp.where(low, v0, pltpu.roll(v2, 64, 1))
    a1 = jnp.where(low, v1, pltpu.roll(v3, 64, 1))
    a2 = jnp.where(low, pltpu.roll(v0, 64, 1), v2)
    a3 = jnp.where(low, pltpu.roll(v1, 64, 1), v3)
    return (
        jnp.where(even, a0, pltpu.roll(a1, 32, 1)),
        jnp.where(even, pltpu.roll(a0, 96, 1), a1),
        jnp.where(even, a2, pltpu.roll(a3, 32, 1)),
        jnp.where(even, pltpu.roll(a2, 96, 1), a3),
    )


def density_kernel(info_ref, coeff_ref, plane_ref, depth_ref, note_ref, out_ref):
    f = pl.program_id(0)
    count = info_ref[f, 7]
    scale = 2.0 * info_ref[f, 6].astype(F32)
    coeffs = coeff_ref[:, pl.ds(pl.multiple_of(f * 16, 16), 16), :].reshape(256, 256)
    for part in range(4):
        columns = slice(part * 256, (part + 1) * 256)
        flat = jnp.dot(coeffs, plane_ref[0, 1, :, columns], preferred_element_type=F32)
        flat += jnp.dot(coeffs, plane_ref[0, 0, :, columns], preferred_element_type=F32)
        psi = product((depth_ref[0, 0], depth_ref[0, 1]), split(flat), NN)
        total = jnp.zeros((32, 256), F32)
        for m in range(16):
            orbital = psi[m * 32 : (m + 1) * 32]
            total += orbital * orbital * (m < count).astype(F32)
        total = total * scale
        for tile in range(2):
            here = total[:, tile * 128 : (tile + 1) * 128]
            turned = pltpu.roll(here, 64, 1)
            owner = 2 * (2 * part + tile)
            low = lanes_of(here.shape) < 64

            @pl.when(f == 0)
            def _():
                out_ref[owner, 0:32, :] = here
                out_ref[owner + 1, 0:32, :] = turned

            @pl.when(f == 1)
            def _():
                out_ref[owner, 0:32, :] = jnp.where(low, out_ref[owner, 0:32, :], turned)
                out_ref[owner + 1, 0:32, :] = jnp.where(low, out_ref[owner + 1, 0:32, :], here)

    for owner in range(16):
        out_ref[owner, 32:40, :] = note_ref[...]


def densities(info, coeffs, note):
    planes = jnp.asarray(plane_tables())
    depths = jnp.asarray(depth_tables())
    return pl.pallas_call(
        density_kernel,
        grid_spec=pltpu.PrefetchScalarGridSpec(
            num_scalar_prefetch=1,
            grid=(2,),
            in_specs=[
                pl.BlockSpec((16, 32, 256), lambda f, info: (0, 0, 0)),
                pl.BlockSpec(
                    (1, 2, 256, 1024), lambda f, info: (2 * info[f, 4] + info[f, 5] - 3, 0, 0, 0)
                ),
                pl.BlockSpec((1, 2, 512, 256), lambda f, info: (info[f, 3] - 1, 0, 0, 0)),
                pl.BlockSpec((8, 128), lambda f, info: (0, 0)),
            ],
            out_specs=pl.BlockSpec((16, 40, 128), lambda f, info: (0, 0, 0)),
        ),
        out_shape=jax.ShapeDtypeStruct((16, 40, 128), F32),
        compiler_params=pltpu.CompilerParams(vmem_limit_bytes=VMEM_LIMIT),
        name="densities",
    )(info, coeffs, planes, depths, note)


def deposit_kernel(info_ref, own_ref, past_ref, out_ref):
    out_ref[...] = jnp.zeros(out_ref.shape, F32)

    def source(s, carry):
        own = own_ref[s, 0:32, :]
        past = past_ref[s, 0:16, :]
        lane = lanes_of((16, 128))
        for f in range(2):
            for first, piece in ((0, own), (32, past)):
                number = first + 2 * s + f
                odd = info_ref[number, 0] & 1
                cell_z = info_ref[number, 2]
                tile = cell_z >> 3
                offset = (cell_z & 7) * 16
                inside = (lane >= offset) & (lane < offset + 32)
                beyond = lane < offset - 96
                for r in range(2):
                    row = (info_ref[number, 1] + r) & 31
                    turned = pltpu.roll(piece, (offset + 128 - (64 * f + 32 * r)) & 127, 1)
                    if first:
                        kept = (odd == 1).astype(F32)
                        moves = ((0, turned * kept),)
                    else:
                        kept = (odd == 0).astype(F32)
                        start = pl.multiple_of(odd * 16, 16)
                        moves = ((start, turned[0:16]), (16, turned[16:32] * kept))
                    for at, value in moves:
                        out_ref[row, tile, pl.ds(at, 16), :] += jnp.where(inside, value, 0.0)

                    @pl.when(offset == 112)
                    def _():
                        after = (tile + 1) & 3
                        for at, value in moves:
                            out_ref[row, after, pl.ds(at, 16), :] += jnp.where(beyond, value, 0.0)

        return carry

    lax.fori_loop(0, 16, source, 0)


def deposits(info, own, past):
    return pl.pallas_call(
        deposit_kernel,
        in_specs=[
            pl.BlockSpec(memory_space=pltpu.SMEM),
            pl.BlockSpec(memory_space=pltpu.VMEM),
            pl.BlockSpec(memory_space=pltpu.VMEM),
        ],
        out_specs=pl.BlockSpec(memory_space=pltpu.VMEM),
        out_shape=jax.ShapeDtypeStruct((32, 4, 32, 128), F32),
        compiler_params=pltpu.CompilerParams(vmem_limit_bytes=VMEM_LIMIT),
        name="deposits",
    )(info, own, past)


def forward_kernel(back_ref, held_ref, table_ref, total_ref, out_ref):
    table = (table_ref[0], table_ref[1])

    def block(b, carry):
        for x in range(8):
            plane = b * 8 + x
            for jj in range(2):
                for half in range(2):
                    rows = slice(jj * 16 + half * 8, jj * 16 + half * 8 + 8)
                    for tile in range(4):
                        start = half * 2048 + jj * 128 + tile * 32 + plane
                        columns = slice(tile * 128, (tile + 1) * 128)
                        total_ref[plane, rows, columns] = (
                            back_ref[plane, rows, columns]
                            + held_ref[pl.ds(start, 8, stride=256), :]
                        )
        total = total_ref[pl.ds(pl.multiple_of(b * 8, 8), 8), :, :].reshape(256, 512)
        waves = product(table, split(total), NT)
        for tile in range(2):
            out_ref[pl.ds(2 * b + tile, 512, stride=8), :] = waves[
                :, tile * 128 : (tile + 1) * 128
            ]
        return carry

    lax.fori_loop(0, 4, block, 0)


def forward_z(background, held, table):
    return pl.pallas_call(
        forward_kernel,
        in_specs=[pl.BlockSpec(memory_space=pltpu.VMEM)] * 3,
        out_specs=[pl.BlockSpec(memory_space=pltpu.VMEM)] * 2,
        out_shape=[
            jax.ShapeDtypeStruct((32, 32, 512), F32),
            jax.ShapeDtypeStruct((4096, 128), F32),
        ],
        compiler_params=pltpu.CompilerParams(vmem_limit_bytes=VMEM_LIMIT),
        name="forward_z",
    )(background, held, table)


def planes_kernel(place_ref, in_ref, side_ref, rows_ref, back_ref, cyclic_ref, out_ref, grid_ref):
    side = (side_ref[0], side_ref[1])
    rows = (rows_ref[0], rows_ref[1])
    back = (back_ref[0], back_ref[1])
    cyclic = (cyclic_ref[0], cyclic_ref[1])

    def plane(kk, carry):
        for quad in range(4):
            parts = [in_ref[:, 4 * quad + i, kk].reshape(128, 128) for i in range(4)]
            for i, part in enumerate(exchange(parts)):
                grid_ref[:, i, :, quad * 128 : (quad + 1) * 128] = part.reshape(16, 8, 128)
        value = product(split(grid_ref[...].reshape(512, 512)), side, NN)
        value = product(rows, split(value), NN)

        def folded(index):
            lowest = jnp.minimum(index, NG - index)
            return lowest * lowest

        wave = 2 * place_ref[0] + kk
        square = (
            folded(lax.broadcasted_iota(jnp.int32, (NG, 1), 0))
            + folded(lax.broadcasted_iota(jnp.int32, (1, NG), 1))
            + folded(wave)
        )
        factor = (NG * SPACING) ** 2 / math.pi / float(NG) ** 3
        value = value * jnp.where(
            square > 0, factor / jnp.maximum(square, 1).astype(F32), 0.0
        )
        value = product(back, split(value), NN)
        grid_ref[...] = product(split(value), cyclic, NN).reshape(16, 4, 8, 512)
        for quad in range(4):
            columns = slice(quad * 128, (quad + 1) * 128)
            parts = [grid_ref[:, i, :, columns].reshape(128, 128) for i in range(4)]
            for i, part in enumerate(exchange(parts)):
                out_ref[:, 4 * quad + i, kk] = part.reshape(16, 8, 128)
        return carry

    lax.fori_loop(0, 2, plane, 0)


def solve_planes(place, waves, tables):
    return pl.pallas_call(
        planes_kernel,
        in_specs=[pl.BlockSpec(memory_space=pltpu.SMEM)]
        + [pl.BlockSpec(memory_space=pltpu.VMEM)] * 5,
        out_specs=pl.BlockSpec(memory_space=pltpu.VMEM),
        out_shape=jax.ShapeDtypeStruct((16, 16, 2, 8, 128), F32),
        scratch_shapes=[pltpu.VMEM((16, 4, 8, 512), F32)],
        compiler_params=pltpu.CompilerParams(vmem_limit_bytes=VMEM_LIMIT),
        name="solve_planes",
    )(place, waves, *tables)


def boxes_kernel(info_ref, in_ref, table_ref, own_ref, past_ref, grid_ref):
    table = (table_ref[0], table_ref[1])

    def block(b, carry):
        waves = in_ref[pl.ds(b, 512, stride=8), :]
        value = product(split(waves), table, TN)
        for tile in range(4):
            grid_ref[tile, pl.ds(pl.multiple_of(b * 128, 128), 128), :] = value[
                :, tile * 128 : (tile + 1) * 128
            ]
        return carry

    lax.fori_loop(0, 8, block, 0)

    def source(s, carry):
        lane = lanes_of((16, 128))
        group = lane >> 5
        first_half = jnp.zeros((16, 128), F32)
        second_half = jnp.zeros((16, 128), F32)
        past_half = jnp.zeros((16, 128), F32)
        for f in range(2):
            for first in (0, 32):
                number = first + 2 * s + f
                odd = info_ref[number, 0] & 1
                cell_z = info_ref[number, 2]
                tile = cell_z >> 3
                after = (tile + 1) & 3
                offset = (cell_z & 7) * 16
                for r in range(2):
                    row = (info_ref[number, 1] + r) & 31
                    shift = (64 * f + 32 * r + 128 - offset) & 127
                    wanted = group == 2 * f + r

                    def rows_at(start):
                        value = jnp.where(
                            lane >= offset,
                            grid_ref[tile, pl.ds(start, 16, stride=32), :],
                            grid_ref[after, pl.ds(start, 16, stride=32), :],
                        )
                        return jnp.where(wanted, pltpu.roll(value, shift, 1), 0.0)

                    if first:
                        past_half += rows_at(row) * (odd == 1).astype(F32)
                    else:
                        first_half += rows_at(odd * 512 + row)
                        second_half += rows_at(512 + row) * (odd == 0).astype(F32)
        own_ref[s, 0:16, :] = first_half
        own_ref[s, 16:32, :] = second_half
        past_ref[s] = past_half
        return carry

    lax.fori_loop(0, 16, source, 0)


def boxes(info, waves, table):
    return pl.pallas_call(
        boxes_kernel,
        in_specs=[
            pl.BlockSpec(memory_space=pltpu.SMEM),
            pl.BlockSpec(memory_space=pltpu.VMEM),
            pl.BlockSpec(memory_space=pltpu.VMEM),
        ],
        out_specs=[pl.BlockSpec(memory_space=pltpu.VMEM)] * 2,
        out_shape=[
            jax.ShapeDtypeStruct((16, 32, 128), F32),
            jax.ShapeDtypeStruct((16, 16, 128), F32),
        ],
        scratch_shapes=[pltpu.VMEM((4, 1024, 128), F32)],
        compiler_params=pltpu.CompilerParams(vmem_limit_bytes=VMEM_LIMIT),
        name="boxes",
    )(info, waves, table)


def layout_kernel(info_ref, in_ref, out_ref):
    row = lax.broadcasted_iota(jnp.int32, (32, 128), 0)
    lane = lanes_of((32, 128))
    for quad in range(4):
        parts = exchange([in_ref[4 * quad + i] for i in range(4)])
        for f in range(2):
            for r in range(2):
                inside = (
                    (row < info_ref[f, 3] * 16)
                    & (16 * r + 4 * quad + (lane >> 5) < info_ref[f, 4] * 16)
                    & ((lane & 31) < info_ref[f, 5] * 16)
                )
                out_ref[pl.ds((4 * r + quad) * 2 + f, 32, stride=16), :] = jnp.where(
                    inside, parts[2 * f + r], 0.0
                )


def lay_out(info, pieces):
    return pl.pallas_call(
        layout_kernel,
        in_specs=[
            pl.BlockSpec(memory_space=pltpu.SMEM),
            pl.BlockSpec(memory_space=pltpu.VMEM),
        ],
        out_specs=pl.BlockSpec(memory_space=pltpu.VMEM),
        out_shape=jax.ShapeDtypeStruct((512, 128), F32),
        compiler_params=pltpu.CompilerParams(vmem_limit_bytes=VMEM_LIMIT),
        name="lay_out",
    )(info, pieces)


def along_frag(block, distance):
    devices = range(lax.axis_size("frag"))
    route = [(i, (i + distance) % len(devices)) for i in devices]
    return lax.ppermute(block, "frag", route)


def traded(block, axis):
    return lax.all_to_all(block, axis, split_axis=0, concat_axis=0, tiled=True)


def body(background, orbitals, frag_info):
    waves = hartley()
    straight = jnp.asarray(halves(waves))
    order = row_order()
    rows = jnp.asarray(halves(waves[:, order]))
    back = jnp.asarray(halves(waves[order, :]))
    cyclic = jnp.asarray(halves(waves[:, cyclic_order()]))
    place = (lax.axis_index("frag") * 16 + lax.axis_index("grp")).astype(jnp.int32).reshape(1)

    coeffs = jnp.transpose(orbitals.reshape(16, 256, 32), (0, 2, 1))
    note = jnp.pad(frag_info.astype(F32).reshape(1, 16), ((0, 7), (0, 112)))
    own = traded(densities(frag_info, coeffs, note), "grp")
    past = along_frag(own[:, 16:40, :], 1)
    info = jnp.concatenate([own[:, 32, :16], past[:, 16, :16]]).astype(jnp.int32).reshape(64, 8)
    region = deposits(info, own, past)
    held = traded(region.reshape(16, 256, 128), "grp").reshape(4096, 128)
    total_density, spectrum = forward_z(background, held, straight)
    spectrum = traded(spectrum.reshape(256, 16, 128), BOTH).reshape(16, 16, 2, 8, 128)
    spectrum = solve_planes(place, spectrum, (straight, rows, back, cyclic))
    spectrum = traded(spectrum.reshape(256, 16, 128), BOTH).reshape(4096, 128)
    pieces, beyond = boxes(info, spectrum, straight)
    beyond = along_frag(beyond, -1)
    pieces = pieces + jnp.pad(beyond, ((0, 0), (16, 0), (0, 0)))
    pieces = lay_out(frag_info, traded(pieces, "grp"))
    frag_potential = pieces.reshape(256, 2, 128).transpose(1, 0, 2).reshape(2, 32768)
    return total_density, frag_potential


def solution(mesh):
    return jax.shard_map(
        body,
        mesh=mesh,
        in_specs=(
            P("frag", "grp", None),
            P(None, None, None, ("frag", "grp")),
            P(("frag", "grp"), None),
        ),
        out_specs=(P("frag", "grp", None), P(("frag", "grp"), None)),
        check_vma=False,
    )
```

time: 1700 us -> 261 us (0.15); the launches traced: 1670 us -> 261 us
  local copies, waits for them, and re-layouts: 562 us -> 4.99 us
  loops' own time: 369 us -> 0 us
  blocking collectives: 395 us -> 118 us
  other arithmetic: 101 us -> 1.67 us
  matrix products: 92.6 us -> 0 us
  waiting for transfers between devices: 135 us -> 58.7 us
  Pallas kernels: 0 us -> 57 us
    another operation x2 -> x0, loops' own time: 369 us -> none  [the longest x1 187 us: body(): lax.map(read_slot, anchors).reshape(groups, capacity, box_points)]
    dynamic_update_slice x64 -> x0, local copies, waits for them, and re-layouts: 308 us -> none  [the longest x32 232 us: place_slot(): return lax.dynamic_update_slice(current, window + incoming[slot], corner)]
    all_to_all x3 -> x4, blocking collectives: 324 us -> 118 us  [traded(): return lax.all_to_all(block, axis, split_axis=0, concat_axis=0, tiled=True)]
    dot_general x10 -> x0, matrix products: 83.8 us -> none  [the longest x1 22.8 us: block_density(): jnp.einsum('ayzfm,axf->xyzfm', partial_value, table_x, precision=HIGHEST)]
    all_gather x1 -> x0, blocking collectives: 71.4 us -> none  [body(): lax.all_gather(frag_info, 'grp', axis=0, tiled=True)]
    all_to_all x8 -> x0, local copies, waits for them, and re-layouts: 59.3 us -> none  [the longest x3 18.6 us: body(): lax.all_to_all(spectrum, 'grp', split_axis=1, concat_axis=2, tiled=True)]
    add x37 -> x1, other arithmetic: 59.1 us -> 0.98 us  [body(): pieces = pieces + jnp.pad(beyond, ((0, 0), (16, 0), (0, 0)))]
    all_to_all x3 -> x1, waiting for transfers between devices: 109 us -> 52.2 us  [traded(): return lax.all_to_all(block, axis, split_axis=0, concat_axis=0, tiled=True)]
  transfers between devices with their start and end apart: 5 -> 3, of which waited for: 4 -> 3; matrix products, arithmetic and copies ran while one was open for 0% -> 0% of each run, Pallas kernels for 0% -> 0%
where the time goes in v1:
time: 261 us
  blocking collectives  118 us (45%)
  waiting for transfers between devices  58.7 us (22%)
  Pallas kernels  57 us (22%)
  starting transfers between devices  19.1 us (7%)
  local copies, waits for them, and re-layouts  4.99 us (2%)
    all_to_all x4, blocking collectives, traded(): return lax.all_to_all(block, axis, split_axis=0, concat_axis=0, tiled=True)  118 us
    all_to_all x1, waiting for transfers between devices, traded(): return lax.all_to_all(block, axis, split_axis=0, concat_axis=0, tiled=True)  52.2 us
    all_to_all x1, starting transfers between devices, traded(): return lax.all_to_all(block, axis, split_axis=0, concat_axis=0, tiled=True)  14.3 us
    pallas_call x1, Pallas kernels, solve_planes(): pl.pallas_call(planes_kernel, in_specs=[pl.BlockSpec(memory_space=pltpu.S...  13.6 us
    pallas_call x1, Pallas kernels, deposits(): pl.pallas_call(deposit_kernel, in_specs=[pl.BlockSpec(memory_space=pltpu....  12.3 us
    pallas_call x1, Pallas kernels, boxes(): pl.pallas_call(boxes_kernel, in_specs=[pl.BlockSpec(memory_space=pltpu.SM...  10.6 us
    pallas_call x1, Pallas kernels, densities(): pl.pallas_call(density_kernel, grid_spec=pltpu.PrefetchScalarGridSpec(num...  10.3 us
    pallas_call x1, Pallas kernels, forward_z(): pl.pallas_call(forward_kernel, in_specs=[pl.BlockSpec(memory_space=pltpu....  8.25 us
  transfers between devices with their start and end apart: 3, of which 3 were waited for; matrix products, arithmetic and copies ran while one was open for 0% of the time, Pallas kernels for 0%

profile of v1, /device:TPU:1, one launch (start us, length us, event | category | flops | bytes accessed | tf_op | source)
XLA Modules:
  0.0 260.6 jit_solution(6633912843388130951)
XLA Ops:
  0.6 2.2 copy.21
  2.9 0.7 convert_element_type.14
  3.6 0.1 reshape.41
  3.6 0.6 pad.8.note_ref
  4.2 10.3 %densities.1 = f32[16,40,128]{2,1,0:T(8,128)} custom-call(s32[2,8]{1,0:T(2,128)} %info_ref.3, bf16[16,32,256]{2,1,0:T(8,128)(2,1)} %bitcast.24, bf16[4,2,256,1024]{3,2,1,0:T(8,128)(2,1)} %constant.28.clone.plane_ref, bf16[2,2,512,256]{3,2,1,0:T(8,128)(2,1)} %constant.29.clone.depth_ref, f32[8,128]{1,0:T(8,128)} %pad.8.note_ref), custom_call_target="tpu_custom_call" | custom-call | tf_op jit(solution)/shard_map/densities/pallas_call | solution.py:145
  14.5 16.1 %all_to_all.25.own_ref = f32[16,40,128]{2,1,0:T(8,128)S(1)} all-to-all(f32[16,40,128]{2,1,0:T(8,128)} %densities.1), channel_id=1, replica_groups=mesh['frag'=16,'grp'=16] {'grp'}, dimensions={0} | all-to-all | bytes 655360 | tf_op jit(solution)/shard_map/all_to_all | solution.py:426
  30.6 0.0 copy-start.1
  30.6 3.4 %collective-permute-start = (f32[16,24,128]{2,1,0:T(8,128)S(1)}, f32[16,24,128]{2,1,0:T(8,128)S(1)}, u32[]{:S(2)}, u32[]{:S(2)}) collective-permute-start(f32[16,24,128]{2,1,0:T(8,128)S(1)} %slice.13), channel_id=1, source_target_pairs={{0,16},{16,32},{32,48},{48,64},{64,80},{80,96},{96,112},{112,128},... | collective-permute-start | bytes 589832 | tf_op jit(solution)/shard_map/ppermute | solution.py:422
  34.0 2.6 %collective-permute-done.past_ref = f32[16,24,128]{2,1,0:T(8,128)S(1)} collective-permute-done((f32[16,24,128]{2,1,0:T(8,128)S(1)}, f32[16,24,128]{2,1,0:T(8,128)S(1)}, u32[]{:S(2)}, u32[]{:S(2)}) %collective-permute-start) | collective-permute-done | bytes 196640 | tf_op jit(solution)/shard_map/ppermute | solution.py:422
  36.6 0.0 copy-start.2
  36.6 0.7 convert_element_type.16.info_ref
  37.3 0.0 copy-done.1
  37.3 0.0 copy-done.2
  37.3 12.3 %deposits.1 = f32[32,4,32,128]{3,2,1,0:T(8,128)} custom-call(s32[64,8]{1,0:T(8,128)} %convert_element_type.16.info_ref, f32[16,40,128]{2,1,0:T(8,128)} %copy-done.1, f32[16,24,128]{2,1,0:T(8,128)} %copy-done.2), custom_call_target="tpu_custom_call" | custom-call | tf_op jit(solution)/shard_map/deposits/pallas_call | solution.py:207
  49.6 29.4 %all_to_all.26 = f32[16,256,128]{2,1,0:T(8,128)} all-to-all(f32[16,256,128]{2,1,0:T(8,128)} %bitcast.20), channel_id=1, replica_groups=mesh['frag'=16,'grp'=16] {'grp'}, dimensions={0} | all-to-all | bytes 4194304 | tf_op jit(solution)/shard_map/all_to_all | solution.py:426
  79.0 8.3 %forward_z.1 = (f32[32,32,512]{2,1,0:T(8,128)}, f32[4096,128]{1,0:T(8,128)}) custom-call(f32[32,32,512]{2,1,0:T(8,128)} %back_ref.2, f32[4096,128]{1,0:T(8,128)} %bitcast.19, bf16[2,512,512]{2,1,0:T(8,128)(2,1)} %constant.24.clone.table_ref.side_ref), custom_call_target="tpu_custom_call" | custom-call | tf_op jit(solution)/shard_map/forward_z/pallas_call | solution.py:249
  87.3 14.3 %all-to-all-start.2 = ((f32[256,16,128]{2,1,0:T(8,128)}), f32[256,16,128]{2,1,0:T(8,128)S(1)}, u32[]{:S(2)}, u32[]{:S(2)}) async-start(f32[256,16,128]{2,1,0:T(8,128)} %bitcast.23), calls=%async_computation.2 | async-start | bytes 4194304 | tf_op jit(solution)/shard_map/all_to_all | solution.py:426
  101.6 52.2 %all-to-all-done.2 = f32[256,16,128]{2,1,0:T(8,128)S(1)} async-done(((f32[256,16,128]{2,1,0:T(8,128)}), f32[256,16,128]{2,1,0:T(8,128)S(1)}, u32[]{:S(2)}, u32[]{:S(2)}) %all-to-all-start.2) | async-done | bytes 2097184 | tf_op jit(solution)/shard_map/all_to_all | solution.py:426
  153.8 0.0 copy-start
  153.8 1.3 copy-done
  155.1 13.6 %solve_planes.1 = f32[16,16,2,8,128]{4,3,2,1,0:T(8,128)} custom-call(s32[1]{0:T(128)} %bitcast.6.place_ref, f32[16,16,2,8,128]{4,3,2,1,0:T(8,128)} %bitcast.21, bf16[2,512,512]{2,1,0:T(8,128)(2,1)} %constant.24.clone.table_ref.side_ref, bf16[2,512,512]{2,1,0:T(8,128)(2,1)} %constant.25.clone.rows_ref, bf16[2,512,512]{2,1,0:T(8,128)(2,1)} %constant.26.clone.back_ref, ...), custom_call_target="tpu_custom_call" | custom-call | tf_op jit(solution)/shard_map/solve_planes/pallas_call | solution.py:303
  168.7 60.1 %all_to_all.27 = f32[256,16,128]{2,1,0:T(8,128)} all-to-all(f32[256,16,128]{2,1,0:T(8,128)} %bitcast.22), channel_id=1, replica_groups=mesh['frag'=16,'grp'=16] {'frag','grp'}, dimensions={0} | all-to-all | bytes 4194304 | tf_op jit(solution)/shard_map/all_to_all | solution.py:426
  228.8 10.6 %boxes.1 = (f32[16,32,128]{2,1,0:T(8,128)}, f32[16,16,128]{2,1,0:T(8,128)}) custom-call(s32[64,8]{1,0:T(8,128)} %convert_element_type.16.info_ref, f32[4096,128]{1,0:T(8,128)} %bitcast.18, bf16[2,512,512]{2,1,0:T(8,128)(2,1)} %constant.24.clone.table_ref.side_ref), custom_call_target="tpu_custom_call" | custom-call | tf_op jit(solution)/shard_map/boxes/pallas_call | solution.py:370
  239.4 1.4 collective-permute-start.1
  240.8 3.9 %collective-permute-done.1 = f32[16,16,128]{2,1,0:T(8,128)S(1)} collective-permute-done((f32[16,16,128]{2,1,0:T(8,128)}, f32[16,16,128]{2,1,0:T(8,128)S(1)}, u32[]{:S(2)}, u32[]{:S(2)}) %collective-permute-start.1) | collective-permute-done | bytes 131104 | tf_op jit(solution)/shard_map/ppermute | solution.py:422
  244.7 1.0 pad_add_fusion
  245.6 12.9 %all_to_all.28.in_ref = f32[16,32,128]{2,1,0:T(8,128)} all-to-all(f32[16,32,128]{2,1,0:T(8,128)S(1)} %pad_add_fusion), channel_id=1, replica_groups=mesh['frag'=16,'grp'=16] {'grp'}, dimensions={0} | all-to-all | bytes 524288 | tf_op jit(solution)/shard_map/all_to_all | solution.py:426
  258.6 2.0 lay_out.1
  (4 shorter events, 0.0 us)
Async XLA Ops:
  30.6 6.7 %copy-start.1 = (f32[16,40,128]{2,1,0:T(8,128)}, f32[16,40,128]{2,1,0:T(8,128)S(1)}, u32[]{:S(2)}) copy-start(f32[16,40,128]{2,1,0:T(8,128)S(1)} %all_to_all.25.own_ref) | copy-start | bytes 983044
  30.6 6.0 %collective-permute-start = (f32[16,24,128]{2,1,0:T(8,128)S(1)}, f32[16,24,128]{2,1,0:T(8,128)S(1)}, u32[]{:S(2)}, u32[]{:S(2)}) collective-permute-start(f32[16,24,128]{2,1,0:T(8,128)S(1)} %slice.13), channel_id=1, source_target_pairs={{0,16},{16,32},{32,48},{48,64},{64,80},{80,96},{96,112},{112,128},... | collective-permute-start | bytes 589832 | tf_op jit(solution)/shard_map/ppermute | solution.py:422
  36.6 0.7 copy-start.2
  87.3 66.5 %all-to-all-start.2 = ((f32[256,16,128]{2,1,0:T(8,128)}), f32[256,16,128]{2,1,0:T(8,128)S(1)}, u32[]{:S(2)}, u32[]{:S(2)}) async-start(f32[256,16,128]{2,1,0:T(8,128)} %bitcast.23), calls=%async_computation.2 | async-start | bytes 4194304 | tf_op jit(solution)/shard_map/all_to_all | solution.py:426
  153.8 1.3 copy-start
  239.4 5.3 %collective-permute-start.1 = (f32[16,16,128]{2,1,0:T(8,128)}, f32[16,16,128]{2,1,0:T(8,128)S(1)}, u32[]{:S(2)}, u32[]{:S(2)}) collective-permute-start(f32[16,16,128]{2,1,0:T(8,128)} %get-tuple-element.9), channel_id=1, source_target_pairs={{0,240},{16,0},{32,16},{48,32},{64,48},{80,64},{96,80},{112,96},{1... | collective-permute-start | bytes 393224 | tf_op jit(solution)/shard_map/ppermute | solution.py:422

commit v2 on v1

v2 whole, which is shorter than its diff:
```python
import math

import jax
import jax.numpy as jnp
import ml_dtypes
import numpy as np
from jax import lax
from jax.experimental import pallas as pl
from jax.experimental.pallas import tpu as pltpu
from jax.sharding import PartitionSpec as P

NG = 512
SPACING = 0.2
F32 = jnp.float32
BF16 = jnp.bfloat16
BOTH = ("frag", "grp")
VMEM_LIMIT = 24 * 1024 * 1024


def halves(table):
    high = table.astype(ml_dtypes.bfloat16)
    low = (table - high.astype(np.float64)).astype(ml_dtypes.bfloat16)
    return np.stack([high, low])


def synthesis_table(span):
    frequency = np.arange(16)[:, None] - 8
    point = np.arange(32)[None, :]
    angle = 2.0 * math.pi * np.mod(frequency * point, span * 16) / (span * 16)
    live = (frequency >= -4 * span) & (frequency < 4 * span) & (point < 16 * span)
    return np.where(live, (np.cos(angle) + np.sin(angle)) * math.sqrt(2.0 / 16) / span, 0.0)


def plane_tables():
    tables = []
    for span_y in (1, 2):
        for span_z in (1, 2):
            table_y = synthesis_table(span_y).reshape(16, 2, 16)
            table_z = synthesis_table(span_z)
            full = np.einsum("brg,cz->bcgrz", table_y, table_z)
            tables.append(halves(full.reshape(256, 1024)))
    return np.stack(tables)


def depth_tables():
    tables = []
    for span in (1, 2):
        full = np.einsum("ax,mn->mxan", synthesis_table(span), np.eye(16))
        tables.append(halves(full.reshape(512, 256)))
    return np.stack(tables)


def cas(rows, columns):
    angle = 2.0 * math.pi / NG * np.mod(rows[:, None] * columns[None, :], NG)
    return np.cos(angle) + np.sin(angle)


def row_order():
    block, low, high = np.meshgrid(np.arange(16), np.arange(4), np.arange(8), indexing="ij")
    return (block * 32 + high * 4 + low).reshape(-1)


def cyclic_order(parity):
    residue, cell = np.meshgrid(np.arange(parity, 16, 2), np.arange(32), indexing="ij")
    return (cell * 16 + residue).reshape(-1)


def wave_tables():
    start = np.arange(256)
    even, odd = 2 * start, 2 * start + 1
    rows = row_order()[:256]
    low = np.concatenate([even[:128], odd[:128]])
    tables = [
        cas(even, start),
        cas(odd, start),
        cas(start, odd),
        cas(even, rows),
        cas(odd, rows),
        cas(rows, even),
        cas(rows, odd),
        cas(low, cyclic_order(0)),
        cas(low, cyclic_order(1)),
    ]
    return np.concatenate([halves(table) for table in tables])


def split(value):
    high = value.astype(BF16)
    return high, (value - high.astype(F32)).astype(BF16)


def product(left, right, dims):
    dims = (dims, ((), ()))
    total = lax.dot_general(left[0], right[1], dims, preferred_element_type=F32)
    total += lax.dot_general(left[1], right[0], dims, preferred_element_type=F32)
    return total + lax.dot_general(left[0], right[0], dims, preferred_element_type=F32)


NN = ((1,), (0,))
NT = ((1,), (1,))
TN = ((0,), (0,))


def lanes_of(shape):
    return lax.broadcasted_iota(jnp.int32, shape, len(shape) - 1)


def exchange(parts):
    lane = lanes_of(parts[0].shape)
    low = lane < 64
    even = (lane & 32) == 0
    v0, v1, v2, v3 = parts
    a0 = jnp.where(low, v0, pltpu.roll(v2, 64, 1))
    a1 = jnp.where(low, v1, pltpu.roll(v3, 64, 1))
    a2 = jnp.where(low, pltpu.roll(v0, 64, 1), v2)
    a3 = jnp.where(low, pltpu.roll(v1, 64, 1), v3)
    return (
        jnp.where(even, a0, pltpu.roll(a1, 32, 1)),
        jnp.where(even, pltpu.roll(a0, 96, 1), a1),
        jnp.where(even, a2, pltpu.roll(a3, 32, 1)),
        jnp.where(even, pltpu.roll(a2, 96, 1), a3),
    )


def density_kernel(
    info_ref, orbitals_ref, planes_ref, depths_ref, out_ref, coeff_ref, plane_ref, depth_ref, sems
):
    copies = []
    for f in range(2):
        pair = 2 * info_ref[f, 4] + info_ref[f, 5] - 3
        copies.append(pltpu.make_async_copy(planes_ref.at[pair], plane_ref.at[f], sems.at[2 * f]))
        copies.append(
            pltpu.make_async_copy(
                depths_ref.at[info_ref[f, 3] - 1], depth_ref.at[f], sems.at[2 * f + 1]
            )
        )
    for copy in copies:
        copy.start()
    for a in range(16):
        coeff_ref[a] = jnp.transpose(orbitals_ref[a].astype(F32)).astype(BF16)
    for f in range(2):
        count = info_ref[f, 7]
        scale = 2.0 * info_ref[f, 6].astype(F32)
        coeffs = coeff_ref[:, 16 * f : 16 * f + 16, :].reshape(256, 256)
        copies[2 * f].wait()
        copies[2 * f + 1].wait()
        for part in range(4):
            columns = slice(part * 256, (part + 1) * 256)
            flat = jnp.dot(coeffs, plane_ref[f, 1, :, columns], preferred_element_type=F32)
            flat += jnp.dot(coeffs, plane_ref[f, 0, :, columns], preferred_element_type=F32)
            psi = product((depth_ref[f, 0], depth_ref[f, 1]), split(flat), NN)
            total = jnp.zeros((32, 256), F32)
            for m in range(16):
                orbital = psi[m * 32 : (m + 1) * 32]
                total += orbital * orbital * (m < count).astype(F32)
            total = total * scale
            for tile in range(2):
                here = total[:, tile * 128 : (tile + 1) * 128]
                turned = pltpu.roll(here, 64, 1)
                owner = 2 * (2 * part + tile)
                low = lanes_of(here.shape) < 64
                if f == 0:
                    out_ref[owner, 0:32, :] = here
                    out_ref[owner + 1, 0:32, :] = turned
                else:
                    out_ref[owner, 0:32, :] = jnp.where(low, out_ref[owner, 0:32, :], turned)
                    out_ref[owner + 1, 0:32, :] = jnp.where(low, out_ref[owner + 1, 0:32, :], here)
    lane = lanes_of((8, 128))
    note = jnp.zeros((8, 128), F32)
    for place in range(16):
        note = jnp.where(lane == place, info_ref[place // 8, place % 8].astype(F32), note)
    for owner in range(16):
        out_ref[owner, 32:40, :] = note


def densities(info, orbitals):
    planes = jnp.asarray(plane_tables())
    depths = jnp.asarray(depth_tables())
    return pl.pallas_call(
        density_kernel,
        in_specs=[
            pl.BlockSpec(memory_space=pltpu.SMEM),
            pl.BlockSpec(memory_space=pltpu.VMEM),
            pl.BlockSpec(memory_space=pl.ANY),
            pl.BlockSpec(memory_space=pl.ANY),
        ],
        out_specs=pl.BlockSpec(memory_space=pltpu.VMEM),
        out_shape=jax.ShapeDtypeStruct((16, 40, 128), F32),
        scratch_shapes=[
            pltpu.VMEM((16, 32, 256), BF16),
            pltpu.VMEM((2, 2, 256, 1024), BF16),
            pltpu.VMEM((2, 2, 512, 256), BF16),
            pltpu.SemaphoreType.DMA((4,)),
        ],
        compiler_params=pltpu.CompilerParams(vmem_limit_bytes=56 * 1024 * 1024),
        name="densities",
    )(info, orbitals, planes, depths)


def deposit_kernel(info_ref, own_ref, past_ref, out_ref):
    out_ref[...] = jnp.zeros(out_ref.shape, F32)

    def source(s, carry):
        own = own_ref[s, 0:32, :]
        past = past_ref[s, 0:16, :]
        lane = lanes_of((16, 128))
        adds = []
        for f in range(2):
            for first, piece in ((0, own), (32, past)):
                number = first + 2 * s + f
                odd = info_ref[number, 0] & 1
                cell_y = info_ref[number, 1]
                cell_z = info_ref[number, 2]
                tile = cell_z >> 3
                after = (tile + 1) & 3
                offset = (cell_z & 7) * 16
                kept = odd == 1 if first else odd == 0
                low = jnp.where(kept, offset, 256)
                part_inside = (lane >= low) & (lane < low + 32)
                part_beyond = lane < jnp.where(kept, offset - 96, 0)
                inside = (lane >= offset) & (lane < offset + 32)
                beyond = lane < offset - 96
                for r in range(2):
                    row = (cell_y + r) & 31
                    turned = pltpu.roll(piece, (offset + 128 - (64 * f + 32 * r)) & 127, 1)
                    if first:
                        adds.append((row, tile, 0, jnp.where(part_inside, turned, 0.0)))
                        adds.append((row, after, 0, jnp.where(part_beyond, turned, 0.0)))
                    else:
                        start = pl.multiple_of(odd * 16, 16)
                        top, rest = turned[0:16], turned[16:32]
                        adds.append((row, tile, start, jnp.where(inside, top, 0.0)))
                        adds.append((row, after, start, jnp.where(beyond, top, 0.0)))
                        adds.append((row, tile, 16, jnp.where(part_inside, rest, 0.0)))
                        adds.append((row, after, 16, jnp.where(part_beyond, rest, 0.0)))
        for row, tile, start, value in adds:
            out_ref[row, tile, pl.ds(start, 16), :] += value
        return carry

    lax.fori_loop(0, 16, source, 0, unroll=2)


def deposits(info, own, past):
    return pl.pallas_call(
        deposit_kernel,
        in_specs=[
            pl.BlockSpec(memory_space=pltpu.SMEM),
            pl.BlockSpec(memory_space=pltpu.VMEM),
            pl.BlockSpec(memory_space=pltpu.VMEM),
        ],
        out_specs=pl.BlockSpec(memory_space=pltpu.VMEM),
        out_shape=jax.ShapeDtypeStruct((32, 4, 32, 128), F32),
        compiler_params=pltpu.CompilerParams(vmem_limit_bytes=VMEM_LIMIT),
        name="deposits",
    )(info, own, past)


def forward_kernel(back_ref, held_ref, table_ref, total_ref, out_ref, turned_ref):
    b = pl.program_id(0)
    for g in range(16):
        for jj in range(2):
            for tile in range(4):
                turned_ref[tile, pl.ds(jj * 16 + g, 8, stride=32), :] = held_ref[
                    (g * 2 + jj) * 4 + tile
                ]
    for tile in range(4):
        columns = slice(tile * 128, (tile + 1) * 128)
        total_ref[:, :, columns] = back_ref[:, :, columns] + turned_ref[tile].reshape(8, 32, 128)
    total = total_ref[...].reshape(256, 512)
    near, far = total[:, :256], total[:, 256:]
    for parity, value in ((0, near + far), (1, near - far)):
        table = (table_ref[2 * parity], table_ref[2 * parity + 1])
        waves = product(table, split(value), NT)
        for tile in range(2):
            place = pl.ds(2048 * parity + 2 * b + tile, 256, stride=8)
            out_ref[place, :] = waves[:, tile * 128 : (tile + 1) * 128]


def forward_z(background, held, table):
    return pl.pallas_call(
        forward_kernel,
        grid=(4,),
        in_specs=[
            pl.BlockSpec((8, 32, 512), lambda b: (b, 0, 0)),
            pl.BlockSpec((128, 8, 128), lambda b: (0, b, 0)),
            pl.BlockSpec((4, 256, 256), lambda b: (0, 0, 0)),
        ],
        out_specs=[
            pl.BlockSpec((8, 32, 512), lambda b: (b, 0, 0)),
            pl.BlockSpec((4096, 128), lambda b: (0, 0)),
        ],
        out_shape=[
            jax.ShapeDtypeStruct((32, 32, 512), F32),
            jax.ShapeDtypeStruct((4096, 128), F32),
        ],
        scratch_shapes=[pltpu.VMEM((4, 256, 128), F32)],
        compiler_params=pltpu.CompilerParams(vmem_limit_bytes=VMEM_LIMIT),
        name="forward_z",
    )(background, held, table)


def planes_kernel(place_ref, in_ref, tables_ref, out_ref, grid_ref):
    kk = pl.program_id(0)

    def table(i):
        return tables_ref[2 * i], tables_ref[2 * i + 1]

    for quad in range(4):
        parts = [in_ref[:, 4 * quad + i, 0].reshape(128, 128) for i in range(4)]
        for i, part in enumerate(exchange(parts)):
            grid_ref[:, i, :, quad * 128 : (quad + 1) * 128] = part.reshape(16, 8, 128)
    grid = grid_ref[...].reshape(512, 512)
    near, far = grid[:, :256], grid[:, 256:]
    value = jnp.concatenate(
        [product(split(near + far), table(0), NN), product(split(near - far), table(2), NN)], 1
    )
    near, far = value[:256], value[256:]
    value = jnp.concatenate(
        [product(table(3), split(near + far), NN), product(table(4), split(near - far), NN)], 0
    )

    def folded(place):
        wave = jnp.where(place < 256, 2 * place, 2 * place - 511)
        lowest = jnp.minimum(wave, NG - wave)
        return lowest * lowest

    square = (
        folded(lax.broadcasted_iota(jnp.int32, (NG, 1), 0))
        + folded(lax.broadcasted_iota(jnp.int32, (1, NG), 1))
        + folded(2 * place_ref[0] + kk)
    )
    factor = (NG * SPACING) ** 2 / math.pi / float(NG) ** 3
    value = value * jnp.where(square > 0, factor / jnp.maximum(square, 1).astype(F32), 0.0)
    even = product(table(5), split(value[:256]), NN)
    odd = product(table(6), split(value[256:]), NN)
    value = jnp.concatenate([even + odd, even - odd], 0)
    near = jnp.concatenate([value[:, 0:128], value[:, 256:384]], 1)
    far = jnp.concatenate([value[:, 128:256], value[:, 384:512]], 1)
    even = product(split(near + far), table(7), NN)
    odd = product(split(near - far), table(8), NN)
    grid_ref[...] = jnp.concatenate([even, odd], 1).reshape(16, 4, 8, 512)
    for quad in range(4):
        columns = slice(quad * 128, (quad + 1) * 128)
        parts = [grid_ref[:, i, :, columns].reshape(128, 128) for i in range(4)]
        for i, part in enumerate(exchange(parts)):
            owner = 2 * (4 * (quad % 2) + i) + quad // 2
            out_ref[:, owner, 0] = part.reshape(16, 8, 128)


def solve_planes(place, waves, tables):
    block = pl.BlockSpec((16, 16, 1, 8, 128), lambda kk: (0, 0, kk, 0, 0))
    return pl.pallas_call(
        planes_kernel,
        grid=(2,),
        in_specs=[
            pl.BlockSpec(memory_space=pltpu.SMEM),
            block,
            pl.BlockSpec(memory_space=pltpu.VMEM),
        ],
        out_specs=block,
        out_shape=jax.ShapeDtypeStruct((16, 16, 2, 8, 128), F32),
        scratch_shapes=[pltpu.VMEM((16, 4, 8, 512), F32)],
        compiler_params=pltpu.CompilerParams(vmem_limit_bytes=VMEM_LIMIT),
        name="solve_planes",
    )(place, waves, tables)


def boxes_kernel(info_ref, in_ref, table_ref, own_ref, past_ref, grid_ref):
    def block(b, carry):
        even = split(in_ref[pl.ds(b, 256, stride=8), :])
        odd = split(in_ref[pl.ds(2048 + b, 256, stride=8), :])
        even = product(even, (table_ref[0], table_ref[1]), TN)
        odd = product(odd, (table_ref[2], table_ref[3]), TN)
        value = jnp.concatenate([even + odd, even - odd], 1)
        for low in range(4):
            for cells in range(4):
                first = low * 32 + cells * 8
                for tile in range(4):
                    place = pl.ds(cells * 256 + 4 * b + low, 8, stride=32)
                    grid_ref[tile, place, :] = value[
                        first : first + 8, tile * 128 : (tile + 1) * 128
                    ]
        return carry

    lax.fori_loop(0, 8, block, 0)

    def source(s, carry):
        lane = lanes_of((16, 128))
        group = lane >> 5
        first_half = jnp.zeros((16, 128), F32)
        second_half = jnp.zeros((16, 128), F32)
        past_half = jnp.zeros((16, 128), F32)
        for f in range(2):
            for first in (0, 32):
                number = first + 2 * s + f
                odd = info_ref[number, 0] & 1
                cell_z = info_ref[number, 2]
                tile = cell_z >> 3
                after = (tile + 1) & 3
                offset = (cell_z & 7) * 16
                for r in range(2):
                    row = (info_ref[number, 1] + r) & 31
                    shift = (64 * f + 32 * r + 128 - offset) & 127
                    wanted = group == 2 * f + r

                    def rows_at(start):
                        place = pl.ds(pl.multiple_of(row * 32 + start, 16), 16)
                        value = jnp.where(
                            lane >= offset, grid_ref[tile, place, :], grid_ref[after, place, :]
                        )
                        return jnp.where(wanted, pltpu.roll(value, shift, 1), 0.0)

                    if first:
                        past_half += rows_at(0) * (odd == 1).astype(F32)
                    else:
                        first_half += rows_at(odd * 16)
                        second_half += rows_at(16) * (odd == 0).astype(F32)
        own_ref[s, 0:16, :] = first_half
        own_ref[s, 16:32, :] = second_half
        past_ref[s] = past_half
        return carry

    lax.fori_loop(0, 16, source, 0, unroll=2)


def boxes(info, waves, table):
    return pl.pallas_call(
        boxes_kernel,
        grid=(1,),
        in_specs=[
            pl.BlockSpec(memory_space=pltpu.SMEM),
            pl.BlockSpec(memory_space=pltpu.VMEM),
            pl.BlockSpec((4, 256, 256), lambda i: (0, 0, 0)),
        ],
        out_specs=[pl.BlockSpec(memory_space=pltpu.VMEM)] * 2,
        out_shape=[
            jax.ShapeDtypeStruct((16, 32, 128), F32),
            jax.ShapeDtypeStruct((16, 16, 128), F32),
        ],
        scratch_shapes=[pltpu.VMEM((4, 1024, 128), F32)],
        compiler_params=pltpu.CompilerParams(vmem_limit_bytes=VMEM_LIMIT),
        name="boxes",
    )(info, waves, table)


def layout_kernel(info_ref, in_ref, out_ref):
    row = lax.broadcasted_iota(jnp.int32, (32, 128), 0)
    lane = lanes_of((32, 128))
    for quad in range(4):
        parts = exchange([in_ref[4 * quad + i] for i in range(4)])
        for f in range(2):
            for r in range(2):
                inside = (
                    (row < info_ref[f, 3] * 16)
                    & (16 * r + 4 * quad + (lane >> 5) < info_ref[f, 4] * 16)
                    & ((lane & 31) < info_ref[f, 5] * 16)
                )
                out_ref[pl.ds((4 * r + quad) * 2 + f, 32, stride=16), :] = jnp.where(
                    inside, parts[2 * f + r], 0.0
                )


def lay_out(info, pieces):
    return pl.pallas_call(
        layout_kernel,
        in_specs=[
            pl.BlockSpec(memory_space=pltpu.SMEM),
            pl.BlockSpec(memory_space=pltpu.VMEM),
        ],
        out_specs=pl.BlockSpec(memory_space=pltpu.VMEM),
        out_shape=jax.ShapeDtypeStruct((512, 128), F32),
        compiler_params=pltpu.CompilerParams(vmem_limit_bytes=VMEM_LIMIT),
        name="lay_out",
    )(info, pieces)


def along_frag(block, distance):
    devices = range(lax.axis_size("frag"))
    route = [(i, (i + distance) % len(devices)) for i in devices]
    return lax.ppermute(block, "frag", route)


def traded(block, axis):
    return lax.all_to_all(block, axis, split_axis=0, concat_axis=0, tiled=True)


def body(background, orbitals, frag_info):
    tables = jnp.asarray(wave_tables())
    place = (lax.axis_index("frag") * 16 + lax.axis_index("grp")).astype(jnp.int32).reshape(1)
    frag_info, place = lax.optimization_barrier((frag_info, place))
    coeffs = orbitals.reshape(16, 256, 32)
    own = traded(densities(frag_info, coeffs), "grp")
    past = along_frag(own[:, 16:40, :], 1)
    info = jnp.concatenate([own[:, 32, :16], past[:, 16, :16]]).astype(jnp.int32).reshape(64, 8)
    region = deposits(info, own, past)
    held = traded(region.reshape(16, 256, 128), "grp").reshape(128, 32, 128)
    total_density, spectrum = forward_z(background, held, tables)
    spectrum = traded(spectrum.reshape(256, 16, 128), BOTH).reshape(16, 16, 2, 8, 128)
    spectrum = solve_planes(place, spectrum, tables)
    spectrum = traded(spectrum.reshape(256, 16, 128), BOTH).reshape(4096, 128)
    pieces, beyond = boxes(info, spectrum, tables)
    beyond = along_frag(beyond, -1)
    pieces = pieces + jnp.pad(beyond, ((0, 0), (16, 0), (0, 0)))
    pieces = lay_out(frag_info, traded(pieces, "grp"))
    frag_potential = pieces.reshape(256, 2, 128).transpose(1, 0, 2).reshape(2, 32768)
    return total_density, frag_potential


def solution(mesh):
    return jax.shard_map(
        body,
        mesh=mesh,
        in_specs=(
            P("frag", "grp", None),
            P(None, None, None, ("frag", "grp")),
            P(("frag", "grp"), None),
        ),
        out_specs=(P("frag", "grp", None), P(("frag", "grp"), None)),
        check_vma=False,
    )
```

time: 261 us -> 223 us (0.85)
  blocking collectives: 118 us -> 182 us
  waiting for transfers between devices: 58.7 us -> 6.29 us
  Pallas kernels: 57 us -> 29.3 us
  starting transfers between devices: 19.1 us -> 4.82 us
  local copies, waits for them, and re-layouts: 4.99 us -> 0.11 us
    all_to_all x4 -> x5, blocking collectives: 118 us -> 182 us  [traded(): return lax.all_to_all(block, axis, split_axis=0, concat_axis=0, tiled=True)]
    all_to_all x1 -> x0, waiting for transfers between devices: 52.2 us -> none  [traded(): return lax.all_to_all(block, axis, split_axis=0, concat_axis=0, tiled=True)]
    pallas_call x4, Pallas kernels: 42.7 us -> 24.6 us  [the longest x1 7.06 us: boxes(): pl.pallas_call(boxes_kernel, grid=(1,), in_specs=[pl.BlockSpec(memory_spa...]
    all_to_all x1 -> x0, starting transfers between devices: 14.3 us -> none  [traded(): return lax.all_to_all(block, axis, split_axis=0, concat_axis=0, tiled=True)]
    pallas_call x1, Pallas kernels: 12.3 us -> 3.1 us  [deposits(): pl.pallas_call(deposit_kernel, in_specs=[pl.BlockSpec(memory_space=pltpu....]
  transfers between devices with their start and end apart: 3 -> 2, of which waited for: 3 -> 2; matrix products, arithmetic and copies ran while one was open for 0% -> 0% of each run, Pallas kernels for 0% -> 0%
where the time goes in v2:
time: 223 us
  blocking collectives  182 us (82%)
  Pallas kernels  29.3 us (13%)
  waiting for transfers between devices  6.29 us (3%)
  starting transfers between devices  4.82 us (2%)
    all_to_all x5, blocking collectives, traded(): return lax.all_to_all(block, axis, split_axis=0, concat_axis=0, tiled=True)  182 us
    pallas_call x1, Pallas kernels, boxes(): pl.pallas_call(boxes_kernel, grid=(1,), in_specs=[pl.BlockSpec(memory_spa...  7.06 us
    pallas_call x1, Pallas kernels, solve_planes(): pl.pallas_call(planes_kernel, grid=(2,), in_specs=[pl.BlockSpec(memory_sp...  6.72 us
    pallas_call x1, Pallas kernels, densities(): pl.pallas_call(density_kernel, in_specs=[pl.BlockSpec(memory_space=pltpu....  6.66 us
    ppermute x2, waiting for transfers between devices, along_frag(): return lax.ppermute(block, 'frag', route)  6.29 us
    ppermute x2, starting transfers between devices, along_frag(): return lax.ppermute(block, 'frag', route)  4.82 us
  transfers between devices with their start and end apart: 2, of which 2 were waited for; matrix products, arithmetic and copies ran while one was open for 0% of the time, Pallas kernels for 0%

profile of v2, /device:TPU:1, one launch (start us, length us, event | category | flops | bytes accessed | tf_op | source)
XLA Modules:
  0.0 223.0 jit_solution(8132261090709169099)
XLA Ops:
  0.6 6.7 %densities.1 = f32[16,40,128]{2,1,0:T(8,128)} custom-call(s32[2,8]{1,0:T(2,128)} %info_ref.1, bf16[16,256,32]{2,1,0:T(8,128)(2,1)} %bitcast.23, bf16[4,2,256,1024]{3,2,1,0:T(8,128)(2,1)} %constant.19.clone.planes_ref, bf16[2,2,512,256]{3,2,1,0:T(8,128)(2,1)} %constant.20.clone.depths_ref), custom_call_target="tpu_custom_call" | custom-call | tf_op jit(solution)/shard_map/densities/pallas_call | solution.py:179
  7.3 16.1 %all_to_all.25.own_ref = f32[16,40,128]{2,1,0:T(8,128)S(1)} all-to-all(f32[16,40,128]{2,1,0:T(8,128)} %densities.1), channel_id=1, replica_groups=mesh['frag'=16,'grp'=16] {'grp'}, dimensions={0} | all-to-all | bytes 655360 | tf_op jit(solution)/shard_map/all_to_all | solution.py:484
  23.4 3.4 %collective-permute-start = (f32[16,24,128]{2,1,0:T(8,128)S(1)}, f32[16,24,128]{2,1,0:T(8,128)S(1)}, u32[]{:S(2)}, u32[]{:S(2)}) collective-permute-start(f32[16,24,128]{2,1,0:T(8,128)S(1)} %slice.13), channel_id=1, source_target_pairs={{0,16},{16,32},{32,48},{48,64},{64,80},{80,96},{96,112},{112,128},... | collective-permute-start | bytes 589832 | tf_op jit(solution)/shard_map/ppermute | solution.py:480
  26.8 2.6 %collective-permute-done.past_ref = f32[16,24,128]{2,1,0:T(8,128)S(1)} collective-permute-done((f32[16,24,128]{2,1,0:T(8,128)S(1)}, f32[16,24,128]{2,1,0:T(8,128)S(1)}, u32[]{:S(2)}, u32[]{:S(2)}) %collective-permute-start) | collective-permute-done | bytes 196640 | tf_op jit(solution)/shard_map/ppermute | solution.py:480
  29.4 0.1 convert_element_type.10.info_ref
  29.5 0.0 copy-start.1
  29.5 3.1 %deposits.1 = f32[32,4,32,128]{3,2,1,0:T(8,128)S(1)} custom-call(s32[64,8]{1,0:T(8,128)S(1)} %convert_element_type.10.info_ref, f32[16,40,128]{2,1,0:T(8,128)S(1)} %all_to_all.25.own_ref, f32[16,24,128]{2,1,0:T(8,128)S(1)} %collective-permute-done.past_ref), custom_call_target="tpu_custom_call" | custom-call | tf_op jit(solution)/shard_map/deposits/pallas_call | solution.py:244
  32.6 0.0 copy-start
  32.6 27.7 %all_to_all.26 = f32[16,256,128]{2,1,0:T(8,128)S(1)} all-to-all(f32[16,256,128]{2,1,0:T(8,128)S(1)} %bitcast.19), channel_id=1, replica_groups=mesh['frag'=16,'grp'=16] {'grp'}, dimensions={0} | all-to-all | bytes 4194304 | tf_op jit(solution)/shard_map/all_to_all | solution.py:484
  60.3 0.0 copy-done.1
  60.3 0.0 copy-done
  60.3 4.2 %forward_z.1 = (f32[32,32,512]{2,1,0:T(8,128)}, f32[4096,128]{1,0:T(8,128)S(1)}) custom-call(f32[32,32,512]{2,1,0:T(8,128)S(1)} %copy-done.1, f32[128,32,128]{2,1,0:T(8,128)S(1)} %bitcast.17, bf16[18,256,256]{2,1,0:T(8,128)(2,1)S(1)} %copy-done), custom_call_target="tpu_custom_call" | custom-call | tf_op jit(solution)/shard_map/forward_z/pallas_call | solution.py:280
  64.5 65.8 %all_to_all.27 = f32[256,16,128]{2,1,0:T(8,128)S(1)} all-to-all(f32[256,16,128]{2,1,0:T(8,128)S(1)} %bitcast.22), channel_id=1, replica_groups=mesh['frag'=16,'grp'=16] {'frag','grp'}, dimensions={0} | all-to-all | bytes 4194304 | tf_op jit(solution)/shard_map/all_to_all | solution.py:484
  130.3 6.7 %solve_planes.1 = f32[16,16,2,8,128]{4,3,2,1,0:T(8,128)S(1)} custom-call(s32[1]{0:T(128)} %bitcast.place_ref, f32[16,16,2,8,128]{4,3,2,1,0:T(8,128)S(1)} %bitcast.20, bf16[18,256,256]{2,1,0:T(8,128)(2,1)S(1)} %copy-done), custom_call_target="tpu_custom_call" | custom-call | tf_op jit(solution)/shard_map/solve_planes/pallas_call | solution.py:352
  137.0 59.6 %all_to_all.28 = f32[256,16,128]{2,1,0:T(8,128)S(1)} all-to-all(f32[256,16,128]{2,1,0:T(8,128)S(1)} %bitcast.21), channel_id=1, replica_groups=mesh['frag'=16,'grp'=16] {'frag','grp'}, dimensions={0} | all-to-all | bytes 4194304 | tf_op jit(solution)/shard_map/all_to_all | solution.py:484
  196.6 0.0 copy-start.2
  196.6 7.1 %boxes.1 = (f32[16,32,128]{2,1,0:T(8,128)S(1)}, f32[16,16,128]{2,1,0:T(8,128)S(1)}) custom-call(s32[64,8]{1,0:T(8,128)S(1)} %convert_element_type.10.info_ref, f32[4096,128]{1,0:T(8,128)S(1)} %bitcast.18, bf16[18,256,256]{2,1,0:T(8,128)(2,1)S(1)} %copy-done), custom_call_target="tpu_custom_call" | custom-call | tf_op jit(solution)/shard_map/boxes/pallas_call | solution.py:427
  203.7 1.4 collective-permute-start.1
  205.1 3.7 %collective-permute-done.1 = f32[16,16,128]{2,1,0:T(8,128)S(1)} collective-permute-done((f32[16,16,128]{2,1,0:T(8,128)S(1)}, f32[16,16,128]{2,1,0:T(8,128)S(1)}, u32[]{:S(2)}, u32[]{:S(2)}) %collective-permute-start.1) | collective-permute-done | bytes 131104 | tf_op jit(solution)/shard_map/ppermute | solution.py:480
  208.8 12.6 %all_to_all.29.in_ref = f32[16,32,128]{2,1,0:T(8,128)S(1)} all-to-all(f32[16,32,128]{2,1,0:T(8,128)S(1)} %pad_add_fusion), channel_id=1, replica_groups=mesh['frag'=16,'grp'=16] {'grp'}, dimensions={0} | all-to-all | bytes 524288 | tf_op jit(solution)/shard_map/all_to_all | solution.py:484
  221.4 0.0 copy-done.2
  221.5 1.6 lay_out.1
  (5 shorter events, 0.1 us)
Async XLA Ops:
  23.4 6.0 %collective-permute-start = (f32[16,24,128]{2,1,0:T(8,128)S(1)}, f32[16,24,128]{2,1,0:T(8,128)S(1)}, u32[]{:S(2)}, u32[]{:S(2)}) collective-permute-start(f32[16,24,128]{2,1,0:T(8,128)S(1)} %slice.13), channel_id=1, source_target_pairs={{0,16},{16,32},{32,48},{48,64},{64,80},{80,96},{96,112},{112,128},... | collective-permute-start | bytes 589832 | tf_op jit(solution)/shard_map/ppermute | solution.py:480
  29.5 30.8 %copy-start.1 = (f32[32,32,512]{2,1,0:T(8,128)S(1)}, f32[32,32,512]{2,1,0:T(8,128)}, u32[]{:S(2)}) copy-start(f32[32,32,512]{2,1,0:T(8,128)} %back_ref.1) | copy-start | bytes 6291460
  32.6 27.7 %copy-start = (bf16[18,256,256]{2,1,0:T(8,128)(2,1)S(1)}, bf16[18,256,256]{2,1,0:T(8,128)(2,1)}, u32[]{:S(2)}) copy-start(bf16[18,256,256]{2,1,0:T(8,128)(2,1)} %constant.18.clone.table_ref.tables_ref) | copy-start | bytes 7077892
  196.6 24.8 %copy-start.2 = (s32[2,8]{1,0:T(2,128)S(1)}, s32[2,8]{1,0:T(2,128)}, u32[]{:S(2)}) copy-start(s32[2,8]{1,0:T(2,128)} %info_ref.1) | copy-start | bytes 196
  203.7 5.1 %collective-permute-start.1 = (f32[16,16,128]{2,1,0:T(8,128)S(1)}, f32[16,16,128]{2,1,0:T(8,128)S(1)}, u32[]{:S(2)}, u32[]{:S(2)}) collective-permute-start(f32[16,16,128]{2,1,0:T(8,128)S(1)} %get-tuple-element.13), channel_id=1, source_target_pairs={{0,240},{16,0},{32,16},{48,32},{64,48},{80,64},{96,80},{112,96},{1... | collective-permute-start | bytes 393224 | tf_op jit(solution)/shard_map/ppermute | solution.py:480

commit v3 on v2

--- a/solution.py
+++ b/solution.py
@@ -14,6 +14,7 @@
 F32 = jnp.float32
 BF16 = jnp.bfloat16
 BOTH = ("frag", "grp")
+PITCH = 40
 VMEM_LIMIT = 24 * 1024 * 1024
 
 
@@ -109,11 +110,13 @@
     lane = lanes_of(parts[0].shape)
     low = lane < 64
     even = (lane & 32) == 0
-    v0, v1, v2, v3 = parts
-    a0 = jnp.where(low, v0, pltpu.roll(v2, 64, 1))
-    a1 = jnp.where(low, v1, pltpu.roll(v3, 64, 1))
-    a2 = jnp.where(low, pltpu.roll(v0, 64, 1), v2)
-    a3 = jnp.where(low, pltpu.roll(v1, 64, 1), v3)
+
+    def swapped(first, second):
+        crossed = pltpu.roll(jnp.where(low, second, first), 64, 1)
+        return jnp.where(low, first, crossed), jnp.where(low, crossed, second)
+
+    a0, a2 = swapped(parts[0], parts[2])
+    a1, a3 = swapped(parts[1], parts[3])
     return (
         jnp.where(even, a0, pltpu.roll(a1, 32, 1)),
         jnp.where(even, pltpu.roll(a0, 96, 1), a1),
@@ -260,12 +263,15 @@
     for g in range(16):
         for jj in range(2):
             for tile in range(4):
-                turned_ref[tile, pl.ds(jj * 16 + g, 8, stride=32), :] = held_ref[
+                turned_ref[tile, pl.ds(jj * 16 + g, 8, stride=PITCH), :] = held_ref[
                     (g * 2 + jj) * 4 + tile
                 ]
     for tile in range(4):
         columns = slice(tile * 128, (tile + 1) * 128)
-        total_ref[:, :, columns] = back_ref[:, :, columns] + turned_ref[tile].reshape(8, 32, 128)
+        for x in range(8):
+            total_ref[x, :, columns] = (
+                back_ref[x, :, columns] + turned_ref[tile, x * PITCH : x * PITCH + 32, :]
+            )
     total = total_ref[...].reshape(256, 512)
     near, far = total[:, :256], total[:, 256:]
     for parity, value in ((0, near + far), (1, near - far)):
@@ -293,7 +299,7 @@
             jax.ShapeDtypeStruct((32, 32, 512), F32),
             jax.ShapeDtypeStruct((4096, 128), F32),
         ],
-        scratch_shapes=[pltpu.VMEM((4, 256, 128), F32)],
+        scratch_shapes=[pltpu.VMEM((4, 8 * PITCH, 128), F32)],
         compiler_params=pltpu.CompilerParams(vmem_limit_bytes=VMEM_LIMIT),
         name="forward_z",
     )(background, held, table)
@@ -376,13 +382,13 @@
             for cells in range(4):
                 first = low * 32 + cells * 8
                 for tile in range(4):
-                    place = pl.ds(cells * 256 + 4 * b + low, 8, stride=32)
+                    place = pl.ds(cells * 8 * PITCH + 4 * b + low, 8, stride=PITCH)
                     grid_ref[tile, place, :] = value[
                         first : first + 8, tile * 128 : (tile + 1) * 128
                     ]
         return carry
 
-    lax.fori_loop(0, 8, block, 0)
+    lax.fori_loop(0, 8, block, 0, unroll=4)
 
     def source(s, carry):
         lane = lanes_of((16, 128))
@@ -404,7 +410,7 @@
                     wanted = group == 2 * f + r
 
                     def rows_at(start):
-                        place = pl.ds(pl.multiple_of(row * 32 + start, 16), 16)
+                        place = pl.ds(pl.multiple_of(row * PITCH + start, 8), 16)
                         value = jnp.where(
                             lane >= offset, grid_ref[tile, place, :], grid_ref[after, place, :]
                         )
@@ -437,7 +443,7 @@
             jax.ShapeDtypeStruct((16, 32, 128), F32),
             jax.ShapeDtypeStruct((16, 16, 128), F32),
         ],
-        scratch_shapes=[pltpu.VMEM((4, 1024, 128), F32)],
+        scratch_shapes=[pltpu.VMEM((4, 32 * PITCH, 128), F32)],
         compiler_params=pltpu.CompilerParams(vmem_limit_bytes=VMEM_LIMIT),
         name="boxes",
     )(info, waves, table)

time: 223 us -> 219 us (0.982)
  Pallas kernels: 29.3 us -> 24.6 us
    pallas_call x1, Pallas kernels: 7.06 us -> 4.1 us  [boxes(): pl.pallas_call(boxes_kernel, grid=(1,), in_specs=[pl.BlockSpec(memory_spa...]
where the time goes in v3:
time: 219 us; the launch traced here: 218 us
  blocking collectives  182 us (83%)
  Pallas kernels  24.6 us (11%)
  waiting for transfers between devices  6.28 us (3%)
  starting transfers between devices  4.83 us (2%)
    all_to_all x5, blocking collectives, traded(): return lax.all_to_all(block, axis, split_axis=0, concat_axis=0, tiled=True)  182 us
    pallas_call x1, Pallas kernels, densities(): pl.pallas_call(density_kernel, in_specs=[pl.BlockSpec(memory_space=pltpu....  6.66 us
    ppermute x2, waiting for transfers between devices, along_frag(): return lax.ppermute(block, 'frag', route)  6.28 us
    pallas_call x1, Pallas kernels, solve_planes(): pl.pallas_call(planes_kernel, grid=(2,), in_specs=[pl.BlockSpec(memory_sp...  6.28 us
    ppermute x2, starting transfers between devices, along_frag(): return lax.ppermute(block, 'frag', route)  4.83 us
  transfers between devices with their start and end apart: 2, of which 2 were waited for; matrix products, arithmetic and copies ran while one was open for 0% of the time, Pallas kernels for 0%

profile of v3, /device:TPU:1, one launch (start us, length us, event | category | flops | bytes accessed | tf_op | source)
XLA Modules:
  0.0 218.2 jit_solution(14827527864789234033)
XLA Ops:
  0.6 6.7 %densities.1 = f32[16,40,128]{2,1,0:T(8,128)} custom-call(s32[2,8]{1,0:T(2,128)} %info_ref.1, bf16[16,256,32]{2,1,0:T(8,128)(2,1)} %bitcast.23, bf16[4,2,256,1024]{3,2,1,0:T(8,128)(2,1)} %constant.19.clone.planes_ref, bf16[2,2,512,256]{3,2,1,0:T(8,128)(2,1)} %constant.20.clone.depths_ref), custom_call_target="tpu_custom_call" | custom-call | tf_op jit(solution)/shard_map/densities/pallas_call | solution.py:182
  7.3 16.1 %all_to_all.25.own_ref = f32[16,40,128]{2,1,0:T(8,128)S(1)} all-to-all(f32[16,40,128]{2,1,0:T(8,128)} %densities.1), channel_id=1, replica_groups=mesh['frag'=16,'grp'=16] {'grp'}, dimensions={0} | all-to-all | bytes 655360 | tf_op jit(solution)/shard_map/all_to_all | solution.py:490
  23.4 3.4 %collective-permute-start = (f32[16,24,128]{2,1,0:T(8,128)S(1)}, f32[16,24,128]{2,1,0:T(8,128)S(1)}, u32[]{:S(2)}, u32[]{:S(2)}) collective-permute-start(f32[16,24,128]{2,1,0:T(8,128)S(1)} %slice.13), channel_id=1, source_target_pairs={{0,16},{16,32},{32,48},{48,64},{64,80},{80,96},{96,112},{112,128},... | collective-permute-start | bytes 589832 | tf_op jit(solution)/shard_map/ppermute | solution.py:486
  26.8 2.6 %collective-permute-done.past_ref = f32[16,24,128]{2,1,0:T(8,128)S(1)} collective-permute-done((f32[16,24,128]{2,1,0:T(8,128)S(1)}, f32[16,24,128]{2,1,0:T(8,128)S(1)}, u32[]{:S(2)}, u32[]{:S(2)}) %collective-permute-start) | collective-permute-done | bytes 196640 | tf_op jit(solution)/shard_map/ppermute | solution.py:486
  29.4 0.1 convert_element_type.10.info_ref
  29.5 0.0 copy-start.1
  29.5 3.1 %deposits.1 = f32[32,4,32,128]{3,2,1,0:T(8,128)S(1)} custom-call(s32[64,8]{1,0:T(8,128)S(1)} %convert_element_type.10.info_ref, f32[16,40,128]{2,1,0:T(8,128)S(1)} %all_to_all.25.own_ref, f32[16,24,128]{2,1,0:T(8,128)S(1)} %collective-permute-done.past_ref), custom_call_target="tpu_custom_call" | custom-call | tf_op jit(solution)/shard_map/deposits/pallas_call | solution.py:247
  32.6 0.0 copy-start
  32.6 27.7 %all_to_all.26 = f32[16,256,128]{2,1,0:T(8,128)S(1)} all-to-all(f32[16,256,128]{2,1,0:T(8,128)S(1)} %bitcast.19), channel_id=1, replica_groups=mesh['frag'=16,'grp'=16] {'grp'}, dimensions={0} | all-to-all | bytes 4194304 | tf_op jit(solution)/shard_map/all_to_all | solution.py:490
  60.3 0.0 copy-done.1
  60.3 0.0 copy-done
  60.3 2.9 %forward_z.1 = (f32[32,32,512]{2,1,0:T(8,128)}, f32[4096,128]{1,0:T(8,128)S(1)}) custom-call(f32[32,32,512]{2,1,0:T(8,128)S(1)} %copy-done.1, f32[128,32,128]{2,1,0:T(8,128)S(1)} %bitcast.17, bf16[18,256,256]{2,1,0:T(8,128)(2,1)S(1)} %copy-done), custom_call_target="tpu_custom_call" | custom-call | tf_op jit(solution)/shard_map/forward_z/pallas_call | solution.py:286
  63.2 65.8 %all_to_all.27 = f32[256,16,128]{2,1,0:T(8,128)S(1)} all-to-all(f32[256,16,128]{2,1,0:T(8,128)S(1)} %bitcast.22), channel_id=1, replica_groups=mesh['frag'=16,'grp'=16] {'frag','grp'}, dimensions={0} | all-to-all | bytes 4194304 | tf_op jit(solution)/shard_map/all_to_all | solution.py:490
  129.0 6.3 %solve_planes.1 = f32[16,16,2,8,128]{4,3,2,1,0:T(8,128)S(1)} custom-call(s32[1]{0:T(128)} %bitcast.place_ref, f32[16,16,2,8,128]{4,3,2,1,0:T(8,128)S(1)} %bitcast.20, bf16[18,256,256]{2,1,0:T(8,128)(2,1)S(1)} %copy-done), custom_call_target="tpu_custom_call" | custom-call | tf_op jit(solution)/shard_map/solve_planes/pallas_call | solution.py:358
  135.3 59.6 %all_to_all.28 = f32[256,16,128]{2,1,0:T(8,128)S(1)} all-to-all(f32[256,16,128]{2,1,0:T(8,128)S(1)} %bitcast.21), channel_id=1, replica_groups=mesh['frag'=16,'grp'=16] {'frag','grp'}, dimensions={0} | all-to-all | bytes 4194304 | tf_op jit(solution)/shard_map/all_to_all | solution.py:490
  194.9 0.0 copy-start.2
  194.9 4.1 %boxes.1 = (f32[16,32,128]{2,1,0:T(8,128)S(1)}, f32[16,16,128]{2,1,0:T(8,128)S(1)}) custom-call(s32[64,8]{1,0:T(8,128)S(1)} %convert_element_type.10.info_ref, f32[4096,128]{1,0:T(8,128)S(1)} %bitcast.18, bf16[18,256,256]{2,1,0:T(8,128)(2,1)S(1)} %copy-done), custom_call_target="tpu_custom_call" | custom-call | tf_op jit(solution)/shard_map/boxes/pallas_call | solution.py:433
  199.0 1.4 collective-permute-start.1
  200.4 3.7 %collective-permute-done.1 = f32[16,16,128]{2,1,0:T(8,128)S(1)} collective-permute-done((f32[16,16,128]{2,1,0:T(8,128)S(1)}, f32[16,16,128]{2,1,0:T(8,128)S(1)}, u32[]{:S(2)}, u32[]{:S(2)}) %collective-permute-start.1) | collective-permute-done | bytes 131104 | tf_op jit(solution)/shard_map/ppermute | solution.py:486
  204.1 12.6 %all_to_all.29.in_ref = f32[16,32,128]{2,1,0:T(8,128)S(1)} all-to-all(f32[16,32,128]{2,1,0:T(8,128)S(1)} %pad_add_fusion), channel_id=1, replica_groups=mesh['frag'=16,'grp'=16] {'grp'}, dimensions={0} | all-to-all | bytes 524288 | tf_op jit(solution)/shard_map/all_to_all | solution.py:490
  216.7 0.0 copy-done.2
  216.7 1.5 lay_out.1
  (5 shorter events, 0.1 us)
Async XLA Ops:
  23.4 6.0 %collective-permute-start = (f32[16,24,128]{2,1,0:T(8,128)S(1)}, f32[16,24,128]{2,1,0:T(8,128)S(1)}, u32[]{:S(2)}, u32[]{:S(2)}) collective-permute-start(f32[16,24,128]{2,1,0:T(8,128)S(1)} %slice.13), channel_id=1, source_target_pairs={{0,16},{16,32},{32,48},{48,64},{64,80},{80,96},{96,112},{112,128},... | collective-permute-start | bytes 589832 | tf_op jit(solution)/shard_map/ppermute | solution.py:486
  29.5 30.8 %copy-start.1 = (f32[32,32,512]{2,1,0:T(8,128)S(1)}, f32[32,32,512]{2,1,0:T(8,128)}, u32[]{:S(2)}) copy-start(f32[32,32,512]{2,1,0:T(8,128)} %back_ref.1) | copy-start | bytes 6291460
  32.6 27.7 %copy-start = (bf16[18,256,256]{2,1,0:T(8,128)(2,1)S(1)}, bf16[18,256,256]{2,1,0:T(8,128)(2,1)}, u32[]{:S(2)}) copy-start(bf16[18,256,256]{2,1,0:T(8,128)(2,1)} %constant.18.clone.table_ref.tables_ref) | copy-start | bytes 7077892
  194.9 21.9 %copy-start.2 = (s32[2,8]{1,0:T(2,128)S(1)}, s32[2,8]{1,0:T(2,128)}, u32[]{:S(2)}) copy-start(s32[2,8]{1,0:T(2,128)} %info_ref.1) | copy-start | bytes 196
  199.0 5.1 %collective-permute-start.1 = (f32[16,16,128]{2,1,0:T(8,128)S(1)}, f32[16,16,128]{2,1,0:T(8,128)S(1)}, u32[]{:S(2)}, u32[]{:S(2)}) collective-permute-start(f32[16,16,128]{2,1,0:T(8,128)S(1)} %get-tuple-element.13), channel_id=1, source_target_pairs={{0,240},{16,0},{32,16},{48,32},{64,48},{80,64},{96,80},{112,96},{1... | collective-permute-start | bytes 393224 | tf_op jit(solution)/shard_map/ppermute | solution.py:486

commit v4 on v3

--- a/solution.py
+++ b/solution.py
@@ -61,28 +61,23 @@
     return (block * 32 + high * 4 + low).reshape(-1)
 
 
-def cyclic_order(parity):
-    residue, cell = np.meshgrid(np.arange(parity, 16, 2), np.arange(32), indexing="ij")
-    return (cell * 16 + residue).reshape(-1)
-
-
 def wave_tables():
     start = np.arange(256)
     even, odd = 2 * start, 2 * start + 1
     rows = row_order()[:256]
-    low = np.concatenate([even[:128], odd[:128]])
     tables = [
         cas(even, start),
         cas(odd, start),
         cas(start, odd),
         cas(even, rows),
         cas(odd, rows),
-        cas(rows, even),
-        cas(rows, odd),
-        cas(low, cyclic_order(0)),
-        cas(low, cyclic_order(1)),
     ]
     return np.concatenate([halves(table) for table in tables])
+
+
+def window_table():
+    waves = np.concatenate([np.arange(0, NG, 2), np.arange(1, NG, 2)])
+    return halves(cas(np.arange(NG + 64) % NG, waves))
 
 
 def split(value):
@@ -200,7 +195,21 @@
     )(info, orbitals, planes, depths)
 
 
-def deposit_kernel(info_ref, own_ref, past_ref, out_ref):
+def first_cell(info_ref):
+    def touched(number):
+        cell = info_ref[number, 1]
+        return cell >> 1, ((cell + info_ref[number, 4] - 1) & 31) >> 1
+
+    first, last = touched(0)
+    shared = jnp.int32(1)
+    for number in range(1, 32):
+        one, other = touched(number)
+        shared = shared * ((one == first) | (other == first)).astype(jnp.int32)
+    return (2 * jnp.where(shared == 1, first, last) + 31) & 31
+
+
+def deposit_kernel(info_ref, own_ref, past_ref, out_ref, cell_ref):
+    cell_ref[...] = jnp.full((8, 128), first_cell(info_ref).astype(F32))
     out_ref[...] = jnp.zeros(out_ref.shape, F32)
 
     def source(s, carry):
@@ -251,8 +260,11 @@
             pl.BlockSpec(memory_space=pltpu.VMEM),
             pl.BlockSpec(memory_space=pltpu.VMEM),
         ],
-        out_specs=pl.BlockSpec(memory_space=pltpu.VMEM),
-        out_shape=jax.ShapeDtypeStruct((32, 4, 32, 128), F32),
+        out_specs=[pl.BlockSpec(memory_space=pltpu.VMEM)] * 2,
+        out_shape=[
+            jax.ShapeDtypeStruct((32, 4, 32, 128), F32),
+            jax.ShapeDtypeStruct((8, 128), F32),
+        ],
         compiler_params=pltpu.CompilerParams(vmem_limit_bytes=VMEM_LIMIT),
         name="deposits",
     )(info, own, past)
@@ -305,7 +317,7 @@
     )(background, held, table)
 
 
-def planes_kernel(place_ref, in_ref, tables_ref, out_ref, grid_ref):
+def planes_kernel(place_ref, cells_ref, in_ref, tables_ref, window_ref, out_ref, grid_ref, wave_ref):
     kk = pl.program_id(0)
 
     def table(i):
@@ -337,93 +349,79 @@
     )
     factor = (NG * SPACING) ** 2 / math.pi / float(NG) ** 3
     value = value * jnp.where(square > 0, factor / jnp.maximum(square, 1).astype(F32), 0.0)
-    even = product(table(5), split(value[:256]), NN)
-    odd = product(table(6), split(value[256:]), NN)
-    value = jnp.concatenate([even + odd, even - odd], 0)
-    near = jnp.concatenate([value[:, 0:128], value[:, 256:384]], 1)
-    far = jnp.concatenate([value[:, 128:256], value[:, 384:512]], 1)
-    even = product(split(near + far), table(7), NN)
-    odd = product(split(near - far), table(8), NN)
-    grid_ref[...] = jnp.concatenate([even, odd], 1).reshape(16, 4, 8, 512)
-    for quad in range(4):
-        columns = slice(quad * 128, (quad + 1) * 128)
-        parts = [grid_ref[:, i, :, columns].reshape(128, 128) for i in range(4)]
-        for i, part in enumerate(exchange(parts)):
-            owner = 2 * (4 * (quad % 2) + i) + quad // 2
-            out_ref[:, owner, 0] = part.reshape(16, 8, 128)
-
-
-def solve_planes(place, waves, tables):
-    block = pl.BlockSpec((16, 16, 1, 8, 128), lambda kk: (0, 0, kk, 0, 0))
+    even = product(table(0), split(value[:256]), NN)
+    odd = product(table(2), split(value[256:]), NN)
+    for i, value in enumerate(split(jnp.concatenate([even + odd, even - odd, even[:32] + odd[:32]]))):
+        wave_ref[i] = value
+    lane = lanes_of((16, 128))
+    for group in range(16):
+        place = pl.ds(pl.multiple_of(cells_ref[group] * 16, 16), 64)
+        window = (window_ref[0, place, :], window_ref[1, place, :])
+        rows = slice(group * 32, group * 32 + 64)
+        value = product(window, (wave_ref[0, rows, :], wave_ref[1, rows, :]), NT)
+        for half in range(2):
+            joined = jnp.zeros((16, 128), F32)
+            for cell in range(4):
+                piece = jnp.concatenate([value[16 * cell : 16 * cell + 16]] * 2, 1)
+                piece = pltpu.roll(piece, (32 * (cell - half)) % 128, 1)
+                joined = jnp.where((lane >> 5) == cell, piece, joined)
+            out_ref[pl.ds(group * 64 + 2 * kk + half, 16, stride=4), :] = joined
+
+
+def solve_planes(place, cells, waves, tables, window):
     return pl.pallas_call(
         planes_kernel,
         grid=(2,),
         in_specs=[
             pl.BlockSpec(memory_space=pltpu.SMEM),
-            block,
-            pl.BlockSpec(memory_space=pltpu.VMEM),
-        ],
-        out_specs=block,
-        out_shape=jax.ShapeDtypeStruct((16, 16, 2, 8, 128), F32),
-        scratch_shapes=[pltpu.VMEM((16, 4, 8, 512), F32)],
+            pl.BlockSpec(memory_space=pltpu.SMEM),
+            pl.BlockSpec((16, 16, 1, 8, 128), lambda kk: (0, 0, kk, 0, 0)),
+            pl.BlockSpec(memory_space=pltpu.VMEM),
+            pl.BlockSpec(memory_space=pltpu.VMEM),
+        ],
+        out_specs=pl.BlockSpec((1024, 128), lambda kk: (0, 0)),
+        out_shape=jax.ShapeDtypeStruct((1024, 128), F32),
+        scratch_shapes=[pltpu.VMEM((16, 4, 8, 512), F32), pltpu.VMEM((2, 544, 512), BF16)],
         compiler_params=pltpu.CompilerParams(vmem_limit_bytes=VMEM_LIMIT),
         name="solve_planes",
-    )(place, waves, tables)
-
-
-def boxes_kernel(info_ref, in_ref, table_ref, own_ref, past_ref, grid_ref):
-    def block(b, carry):
-        even = split(in_ref[pl.ds(b, 256, stride=8), :])
-        odd = split(in_ref[pl.ds(2048 + b, 256, stride=8), :])
+    )(place, cells, waves, tables, window)
+
+
+def boxes_kernel(info_ref, in_ref, table_ref, out_ref, grid_ref):
+    for half in range(2):
+        even = split(in_ref[pl.ds(half, 256, stride=2), :])
+        odd = split(in_ref[pl.ds(512 + half, 256, stride=2), :])
         even = product(even, (table_ref[0], table_ref[1]), TN)
         odd = product(odd, (table_ref[2], table_ref[3]), TN)
-        value = jnp.concatenate([even + odd, even - odd], 1)
-        for low in range(4):
-            for cells in range(4):
-                first = low * 32 + cells * 8
-                for tile in range(4):
-                    place = pl.ds(cells * 8 * PITCH + 4 * b + low, 8, stride=PITCH)
-                    grid_ref[tile, place, :] = value[
-                        first : first + 8, tile * 128 : (tile + 1) * 128
-                    ]
-        return carry
-
-    lax.fori_loop(0, 8, block, 0, unroll=4)
+        for cell in range(4):
+            first = 32 * cell
+            for tile in range(4):
+                columns = slice(tile % 2 * 128, tile % 2 * 128 + 128)
+                near, far = even[first : first + 32, columns], odd[first : first + 32, columns]
+                place = slice(64 * cell + 32 * half, 64 * cell + 32 * half + 32)
+                grid_ref[tile, place, :] = near + far if tile < 2 else near - far
+    base = first_cell(info_ref)
 
     def source(s, carry):
-        lane = lanes_of((16, 128))
+        lane = lanes_of((32, 128))
         group = lane >> 5
-        first_half = jnp.zeros((16, 128), F32)
-        second_half = jnp.zeros((16, 128), F32)
-        past_half = jnp.zeros((16, 128), F32)
+        total = jnp.zeros((32, 128), F32)
         for f in range(2):
-            for first in (0, 32):
-                number = first + 2 * s + f
-                odd = info_ref[number, 0] & 1
-                cell_z = info_ref[number, 2]
-                tile = cell_z >> 3
-                after = (tile + 1) & 3
-                offset = (cell_z & 7) * 16
-                for r in range(2):
-                    row = (info_ref[number, 1] + r) & 31
-                    shift = (64 * f + 32 * r + 128 - offset) & 127
-                    wanted = group == 2 * f + r
-
-                    def rows_at(start):
-                        place = pl.ds(pl.multiple_of(row * PITCH + start, 8), 16)
-                        value = jnp.where(
-                            lane >= offset, grid_ref[tile, place, :], grid_ref[after, place, :]
-                        )
-                        return jnp.where(wanted, pltpu.roll(value, shift, 1), 0.0)
-
-                    if first:
-                        past_half += rows_at(0) * (odd == 1).astype(F32)
-                    else:
-                        first_half += rows_at(odd * 16)
-                        second_half += rows_at(16) * (odd == 0).astype(F32)
-        own_ref[s, 0:16, :] = first_half
-        own_ref[s, 16:32, :] = second_half
-        past_ref[s] = past_half
+            number = 2 * s + f
+            start = (info_ref[number, 0] & 1) * 16
+            cell_z = info_ref[number, 2]
+            tile = cell_z >> 3
+            after = (tile + 1) & 3
+            offset = (cell_z & 7) * 16
+            for r in range(2):
+                cell = (info_ref[number, 1] + r - base) & 3
+                place = pl.ds(pl.multiple_of(cell * 64 + start, 16), 32)
+                value = jnp.where(
+                    lane >= offset, grid_ref[tile, place, :], grid_ref[after, place, :]
+                )
+                value = pltpu.roll(value, (64 * f + 32 * r + 128 - offset) & 127, 1)
+                total = jnp.where(group == 2 * f + r, value, total)
+        out_ref[s] = total
         return carry
 
     lax.fori_loop(0, 16, source, 0, unroll=2)
@@ -438,12 +436,9 @@
             pl.BlockSpec(memory_space=pltpu.VMEM),
             pl.BlockSpec((4, 256, 256), lambda i: (0, 0, 0)),
         ],
-        out_specs=[pl.BlockSpec(memory_space=pltpu.VMEM)] * 2,
-        out_shape=[
-            jax.ShapeDtypeStruct((16, 32, 128), F32),
-            jax.ShapeDtypeStruct((16, 16, 128), F32),
-        ],
-        scratch_shapes=[pltpu.VMEM((4, 32 * PITCH, 128), F32)],
+        out_specs=pl.BlockSpec(memory_space=pltpu.VMEM),
+        out_shape=jax.ShapeDtypeStruct((16, 32, 128), F32),
+        scratch_shapes=[pltpu.VMEM((4, 256, 128), F32)],
         compiler_params=pltpu.CompilerParams(vmem_limit_bytes=VMEM_LIMIT),
         name="boxes",
     )(info, waves, table)
@@ -491,22 +486,21 @@
 
 
 def body(background, orbitals, frag_info):
-    tables = jnp.asarray(wave_tables())
+    tables, window = jnp.asarray(wave_tables()), jnp.asarray(window_table())
     place = (lax.axis_index("frag") * 16 + lax.axis_index("grp")).astype(jnp.int32).reshape(1)
     frag_info, place = lax.optimization_barrier((frag_info, place))
     coeffs = orbitals.reshape(16, 256, 32)
     own = traded(densities(frag_info, coeffs), "grp")
     past = along_frag(own[:, 16:40, :], 1)
     info = jnp.concatenate([own[:, 32, :16], past[:, 16, :16]]).astype(jnp.int32).reshape(64, 8)
-    region = deposits(info, own, past)
+    region, cell = deposits(info, own, past)
+    cells = lax.all_gather(cell, BOTH, axis=0, tiled=True)[::128, 0].astype(jnp.int32)
     held = traded(region.reshape(16, 256, 128), "grp").reshape(128, 32, 128)
     total_density, spectrum = forward_z(background, held, tables)
     spectrum = traded(spectrum.reshape(256, 16, 128), BOTH).reshape(16, 16, 2, 8, 128)
-    spectrum = solve_planes(place, spectrum, tables)
-    spectrum = traded(spectrum.reshape(256, 16, 128), BOTH).reshape(4096, 128)
-    pieces, beyond = boxes(info, spectrum, tables)
-    beyond = along_frag(beyond, -1)
-    pieces = pieces + jnp.pad(beyond, ((0, 0), (16, 0), (0, 0)))
+    spectrum = solve_planes(place, cells, spectrum, tables, window)
+    spectrum = traded(spectrum.reshape(256, 4, 128), BOTH).reshape(1024, 128)
+    pieces = boxes(info, spectrum, tables)
     pieces = lay_out(frag_info, traded(pieces, "grp"))
     frag_potential = pieces.reshape(256, 2, 128).transpose(1, 0, 2).reshape(2, 32768)
     return total_density, frag_potential

time: 219 us -> 260 us (1.19)
  waiting for transfers between devices: 6.28 us -> 115 us
  blocking collectives: 182 us -> 85.1 us
  between operations: 0.68 us -> 14.1 us
  starting transfers between devices: 4.83 us -> 17.2 us
  local copies, waits for them, and re-layouts: 0.11 us -> 3.95 us
    all_gather x0 -> x1, waiting for transfers between devices: none -> 112 us  [body(): lax.all_gather(cell, BOTH, axis=0, tiled=True)[::128, 0].astype(jnp.int32)]
    all_to_all x5 -> x4, blocking collectives: 182 us -> 85.1 us  [traded(): return lax.all_to_all(block, axis, split_axis=0, concat_axis=0, tiled=True)]
    all_to_all x0 -> x1, starting transfers between devices: none -> 13.8 us  [traded(): return lax.all_to_all(block, axis, split_axis=0, concat_axis=0, tiled=True)]
    ppermute x2 -> x1, waiting for transfers between devices: 6.28 us -> 2.61 us  [along_frag(): return lax.ppermute(block, 'frag', route)]
  transfers between devices with their start and end apart: 2 -> 3, of which waited for: 2 -> 2; matrix products, arithmetic and copies ran while one was open for 0% -> 1% of each run, Pallas kernels for 0% -> 0%
where the time goes in v4:
time: 260 us; the launch traced here: 259 us
  waiting for transfers between devices  115 us (44%)
  blocking collectives  85.1 us (33%)
  Pallas kernels  24.2 us (9%)
  starting transfers between devices  17.2 us (7%)
  between operations  14.1 us (5%)
  local copies, waits for them, and re-layouts  3.95 us (2%)
    all_gather x1, waiting for transfers between devices, body(): lax.all_gather(cell, BOTH, axis=0, tiled=True)[::128, 0].astype(jnp.int32)  112 us
    all_to_all x4, blocking collectives, traded(): return lax.all_to_all(block, axis, split_axis=0, concat_axis=0, tiled=True)  85.1 us
    all_to_all x1, starting transfers between devices, traded(): return lax.all_to_all(block, axis, split_axis=0, concat_axis=0, tiled=True)  13.8 us
    pallas_call x1, Pallas kernels, solve_planes(): pl.pallas_call(planes_kernel, grid=(2,), in_specs=[pl.BlockSpec(memory_sp...  7.12 us
    pallas_call x1, Pallas kernels, densities(): pl.pallas_call(density_kernel, in_specs=[pl.BlockSpec(memory_space=pltpu....  6.66 us
  transfers between devices with their start and end apart: 3, of which 2 were waited for; matrix products, arithmetic and copies ran while one was open for 1% of the time, Pallas kernels for 0%

profile of v4, /device:TPU:1, one launch (start us, length us, event | category | flops | bytes accessed | tf_op | source)
XLA Modules:
  0.0 259.4 jit_solution(9724858136126822898)
XLA Ops:
  7.2 6.7 %densities.1 = f32[16,40,128]{2,1,0:T(8,128)} custom-call(s32[2,8]{1,0:T(2,128)} %info_ref.1, bf16[16,256,32]{2,1,0:T(8,128)(2,1)} %bitcast.23, bf16[4,2,256,1024]{3,2,1,0:T(8,128)(2,1)} %constant.19.clone.planes_ref, bf16[2,2,512,256]{3,2,1,0:T(8,128)(2,1)} %constant.20.clone.depths_ref), custom_call_target="tpu_custom_call" | custom-call | tf_op jit(solution)/shard_map/densities/pallas_call | solution.py:177
  13.8 16.1 %all_to_all.25.own_ref = f32[16,40,128]{2,1,0:T(8,128)S(1)} all-to-all(f32[16,40,128]{2,1,0:T(8,128)} %densities.1), channel_id=1, replica_groups=mesh['frag'=16,'grp'=16] {'grp'}, dimensions={0} | all-to-all | bytes 655360 | tf_op jit(solution)/shard_map/all_to_all | solution.py:485
  29.9 3.4 %collective-permute-start = (f32[16,24,128]{2,1,0:T(8,128)S(1)}, f32[16,24,128]{2,1,0:T(8,128)S(1)}, u32[]{:S(2)}, u32[]{:S(2)}) collective-permute-start(f32[16,24,128]{2,1,0:T(8,128)S(1)} %slice.17), channel_id=1, source_target_pairs={{0,16},{16,32},{32,48},{48,64},{64,80},{80,96},{96,112},{112,128},... | collective-permute-start | bytes 589832 | tf_op jit(solution)/shard_map/ppermute | solution.py:481
  33.3 2.6 %collective-permute-done.past_ref = f32[16,24,128]{2,1,0:T(8,128)S(1)} collective-permute-done((f32[16,24,128]{2,1,0:T(8,128)S(1)}, f32[16,24,128]{2,1,0:T(8,128)S(1)}, u32[]{:S(2)}, u32[]{:S(2)}) %collective-permute-start) | collective-permute-done | bytes 196640 | tf_op jit(solution)/shard_map/ppermute | solution.py:481
  36.0 0.1 convert_element_type.13.info_ref
  36.0 3.7 %deposits.1 = (f32[32,4,32,128]{3,2,1,0:T(8,128)S(1)}, f32[8,128]{1,0:T(8,128)}) custom-call(s32[64,8]{1,0:T(8,128)S(1)} %convert_element_type.13.info_ref, f32[16,40,128]{2,1,0:T(8,128)S(1)} %all_to_all.25.own_ref, f32[16,24,128]{2,1,0:T(8,128)S(1)} %collective-permute-done.past_ref), custom_call_target="tpu_custom_call" | custom-call | tf_op jit(solution)/shard_map/deposits/pallas_call | solution.py:256
  39.7 0.0 copy-start
  39.7 0.0 copy-start.1
  39.7 27.8 %all_to_all.26 = f32[16,256,128]{2,1,0:T(8,128)S(1)} all-to-all(f32[16,256,128]{2,1,0:T(8,128)S(1)} %bitcast.20), channel_id=1, replica_groups=mesh['frag'=16,'grp'=16] {'grp'}, dimensions={0} | all-to-all | bytes 4194304 | tf_op jit(solution)/shard_map/all_to_all | solution.py:485
  67.6 0.0 copy-done
  67.6 0.0 copy-done.1
  67.6 2.9 %forward_z.1 = (f32[32,32,512]{2,1,0:T(8,128)}, f32[4096,128]{1,0:T(8,128)S(1)}) custom-call(f32[32,32,512]{2,1,0:T(8,128)S(1)} %copy-done.1, f32[128,32,128]{2,1,0:T(8,128)S(1)} %bitcast.18, bf16[10,256,256]{2,1,0:T(8,128)(2,1)S(1)} %copy-done), custom_call_target="tpu_custom_call" | custom-call | tf_op jit(solution)/shard_map/forward_z/pallas_call | solution.py:298
  70.4 0.0 copy-start.2
  70.4 1.3 copy-done.2
  71.8 13.8 %all-to-all-start.2 = ((f32[256,16,128]{2,1,0:T(8,128)}), f32[256,16,128]{2,1,0:T(8,128)S(1)}, u32[]{:S(2)}, u32[]{:S(2)}) async-start(f32[256,16,128]{2,1,0:T(8,128)} %bitcast.19), calls=%async_computation.2 | async-start | bytes 4194304 | tf_op jit(solution)/shard_map/all_to_all | solution.py:485
  85.5 0.0 all-gather.2.cloned.1.call-start
  85.6 0.7 all-gather.2.cloned.1.call-update
  86.3 111.5 %all-gather.2.cloned.1.call-done = f32[2048,128]{1,0:T(8,128)} async-done(((f32[8,128]{1,0:T(8,128)}), f32[2048,128]{1,0:T(8,128)}) %all-gather.2.cloned.1.call-update) | async-done | bytes 1048592 | tf_op jit(solution)/shard_map/all_gather | solution.py:497
  197.8 1.2 slice.15
  199.0 0.1 convert_reduce_fusion.cells_ref
  199.1 0.0 all-to-all-done.2
  199.1 0.0 copy-start.3
  199.2 1.3 copy-done.3
  200.4 7.1 %solve_planes.1 = f32[1024,128]{1,0:T(8,128)S(1)} custom-call(s32[1]{0:T(128)} %bitcast.place_ref, s32[16]{0:T(128)S(1)} %convert_reduce_fusion.cells_ref, f32[16,16,2,8,128]{4,3,2,1,0:T(8,128)S(1)} %bitcast.17, bf16[10,256,256]{2,1,0:T(8,128)(2,1)S(1)} %copy-done, bf16[2,576,512]{2,1,0:T(8,128)(2,1)S(1)} %copy-done.3), custom_call_target="tpu_custom_call" | custom-call | tf_op jit(solution)/shard_map/solve_planes/pallas_call | solution.py:372
  207.5 0.0 copy-start.4
  207.6 31.0 %all_to_all.27 = f32[256,4,128]{2,1,0:T(4,128)S(1)} all-to-all(f32[256,4,128]{2,1,0:T(4,128)S(1)} %bitcast.22), channel_id=1, replica_groups=mesh['frag'=16,'grp'=16] {'frag','grp'}, dimensions={0} | all-to-all | bytes 1048576 | tf_op jit(solution)/shard_map/all_to_all | solution.py:485
  238.6 2.4 boxes.1
  240.9 10.1 %all_to_all.28.in_ref = f32[16,32,128]{2,1,0:T(8,128)S(1)} all-to-all(f32[16,32,128]{2,1,0:T(8,128)S(1)} %boxes.1), channel_id=1, replica_groups=mesh['frag'=16,'grp'=16] {'grp'}, dimensions={0} | all-to-all | bytes 524288 | tf_op jit(solution)/shard_map/all_to_all | solution.py:485
  251.1 0.0 copy-done.4
  251.1 1.5 lay_out.1
  (4 shorter events, 0.0 us)
Async XLA Ops:
  29.9 6.0 %collective-permute-start = (f32[16,24,128]{2,1,0:T(8,128)S(1)}, f32[16,24,128]{2,1,0:T(8,128)S(1)}, u32[]{:S(2)}, u32[]{:S(2)}) collective-permute-start(f32[16,24,128]{2,1,0:T(8,128)S(1)} %slice.17), channel_id=1, source_target_pairs={{0,16},{16,32},{32,48},{48,64},{64,80},{80,96},{96,112},{112,128},... | collective-permute-start | bytes 589832 | tf_op jit(solution)/shard_map/ppermute | solution.py:481
  39.7 27.8 %copy-start = (bf16[10,256,256]{2,1,0:T(8,128)(2,1)S(1)}, bf16[10,256,256]{2,1,0:T(8,128)(2,1)}, u32[]{:S(2)}) copy-start(bf16[10,256,256]{2,1,0:T(8,128)(2,1)} %constant.17.clone.table_ref.tables_ref) | copy-start | bytes 3932164
  39.7 27.8 %copy-start.1 = (f32[32,32,512]{2,1,0:T(8,128)S(1)}, f32[32,32,512]{2,1,0:T(8,128)}, u32[]{:S(2)}) copy-start(f32[32,32,512]{2,1,0:T(8,128)} %back_ref.1) | copy-start | bytes 6291460
  70.4 1.3 copy-start.2
  71.8 127.4 %all-to-all-start.2 = ((f32[256,16,128]{2,1,0:T(8,128)}), f32[256,16,128]{2,1,0:T(8,128)S(1)}, u32[]{:S(2)}, u32[]{:S(2)}) async-start(f32[256,16,128]{2,1,0:T(8,128)} %bitcast.19), calls=%async_computation.2 | async-start | bytes 4194304 | tf_op jit(solution)/shard_map/all_to_all | solution.py:485
  85.5 112.2 %all-gather.2.cloned.1.call-start = ((), (), s32[]{:S(2)}) async-start(), calls=%async_computation.5 | async-start | bytes 1052672 | tf_op jit(solution)/shard_map/all_gather | solution.py:497
  199.1 1.3 copy-start.3
  207.5 43.5 %copy-start.4 = (s32[2,8]{1,0:T(2,128)S(1)}, s32[2,8]{1,0:T(2,128)}, u32[]{:S(2)}) copy-start(s32[2,8]{1,0:T(2,128)} %info_ref.1) | copy-start | bytes 196
Sparse Core Ops, SparseCore 0:
  90.7 107.0 all-gather.1

commit v5 on v4

--- a/solution.py
+++ b/solution.py
@@ -270,8 +270,13 @@
     )(info, own, past)
 
 
-def forward_kernel(back_ref, held_ref, table_ref, total_ref, out_ref, turned_ref):
+def forward_kernel(back_ref, held_ref, table_ref, cell_ref, total_ref, out_ref, turned_ref):
     b = pl.program_id(0)
+
+    @pl.when(b == 0)
+    def _():
+        out_ref[pl.ds(16, 256, stride=17), :] = jnp.broadcast_to(cell_ref[0:1, :], (256, 128))
+
     for g in range(16):
         for jj in range(2):
             for tile in range(4):
@@ -290,11 +295,11 @@
         table = (table_ref[2 * parity], table_ref[2 * parity + 1])
         waves = product(table, split(value), NT)
         for tile in range(2):
-            place = pl.ds(2048 * parity + 2 * b + tile, 256, stride=8)
+            place = pl.ds(8 * parity + 2 * b + tile, 256, stride=17)
             out_ref[place, :] = waves[:, tile * 128 : (tile + 1) * 128]
 
 
-def forward_z(background, held, table):
+def forward_z(background, held, table, cell):
     return pl.pallas_call(
         forward_kernel,
         grid=(4,),
@@ -302,29 +307,46 @@
             pl.BlockSpec((8, 32, 512), lambda b: (b, 0, 0)),
             pl.BlockSpec((128, 8, 128), lambda b: (0, b, 0)),
             pl.BlockSpec((4, 256, 256), lambda b: (0, 0, 0)),
+            pl.BlockSpec((8, 128), lambda b: (0, 0)),
         ],
         out_specs=[
             pl.BlockSpec((8, 32, 512), lambda b: (b, 0, 0)),
-            pl.BlockSpec((4096, 128), lambda b: (0, 0)),
+            pl.BlockSpec((4352, 128), lambda b: (0, 0)),
         ],
         out_shape=[
             jax.ShapeDtypeStruct((32, 32, 512), F32),
-            jax.ShapeDtypeStruct((4096, 128), F32),
+            jax.ShapeDtypeStruct((4352, 128), F32),
         ],
         scratch_shapes=[pltpu.VMEM((4, 8 * PITCH, 128), F32)],
         compiler_params=pltpu.CompilerParams(vmem_limit_bytes=VMEM_LIMIT),
         name="forward_z",
-    )(background, held, table)
-
-
-def planes_kernel(place_ref, cells_ref, in_ref, tables_ref, window_ref, out_ref, grid_ref, wave_ref):
+    )(background, held, table, cell)
+
+
+def planes_kernel(
+    place_ref, in_ref, tables_ref, window_ref, out_ref, grid_ref, wave_ref, cells_ref
+):
     kk = pl.program_id(0)
+
+    @pl.when(kk == 0)
+    def _():
+        for group in range(16):
+            row = group * 272 + 16
+            cells_ref[group] = jnp.max(in_ref[row : row + 1, :]).astype(jnp.int32)
 
     def table(i):
         return tables_ref[2 * i], tables_ref[2 * i + 1]
 
     for quad in range(4):
-        parts = [in_ref[:, 4 * quad + i, 0].reshape(128, 128) for i in range(4)]
+        parts = [
+            jnp.concatenate(
+                [
+                    in_ref[pl.ds((group * 16 + 4 * quad + i) * 17 + 8 * kk, 8), :]
+                    for group in range(16)
+                ]
+            )
+            for i in range(4)
+        ]
         for i, part in enumerate(exchange(parts)):
             grid_ref[:, i, :, quad * 128 : (quad + 1) * 128] = part.reshape(16, 8, 128)
     grid = grid_ref[...].reshape(512, 512)
@@ -337,14 +359,16 @@
         [product(table(3), split(near + far), NN), product(table(4), split(near - far), NN)], 0
     )
 
-    def folded(place):
-        wave = jnp.where(place < 256, 2 * place, 2 * place - 511)
+    def folded(wave):
         lowest = jnp.minimum(wave, NG - wave)
         return lowest * lowest
 
+    def ordered(place):
+        return jnp.where(place < 256, 2 * place, 2 * place - 511)
+
     square = (
-        folded(lax.broadcasted_iota(jnp.int32, (NG, 1), 0))
-        + folded(lax.broadcasted_iota(jnp.int32, (1, NG), 1))
+        folded(ordered(lax.broadcasted_iota(jnp.int32, (NG, 1), 0)))
+        + folded(ordered(lax.broadcasted_iota(jnp.int32, (1, NG), 1)))
         + folded(2 * place_ref[0] + kk)
     )
     factor = (NG * SPACING) ** 2 / math.pi / float(NG) ** 3
@@ -368,29 +392,32 @@
             out_ref[pl.ds(group * 64 + 2 * kk + half, 16, stride=4), :] = joined
 
 
-def solve_planes(place, cells, waves, tables, window):
+def solve_planes(place, waves, tables, window):
     return pl.pallas_call(
         planes_kernel,
         grid=(2,),
         in_specs=[
             pl.BlockSpec(memory_space=pltpu.SMEM),
-            pl.BlockSpec(memory_space=pltpu.SMEM),
-            pl.BlockSpec((16, 16, 1, 8, 128), lambda kk: (0, 0, kk, 0, 0)),
+            pl.BlockSpec(memory_space=pltpu.VMEM),
             pl.BlockSpec(memory_space=pltpu.VMEM),
             pl.BlockSpec(memory_space=pltpu.VMEM),
         ],
         out_specs=pl.BlockSpec((1024, 128), lambda kk: (0, 0)),
         out_shape=jax.ShapeDtypeStruct((1024, 128), F32),
-        scratch_shapes=[pltpu.VMEM((16, 4, 8, 512), F32), pltpu.VMEM((2, 544, 512), BF16)],
+        scratch_shapes=[
+            pltpu.VMEM((16, 4, 8, 512), F32),
+            pltpu.VMEM((2, 544, 512), BF16),
+            pltpu.SMEM((16,), jnp.int32),
+        ],
         compiler_params=pltpu.CompilerParams(vmem_limit_bytes=VMEM_LIMIT),
         name="solve_planes",
-    )(place, cells, waves, tables, window)
+    )(place, waves, tables, window)
 
 
 def boxes_kernel(info_ref, in_ref, table_ref, out_ref, grid_ref):
     for half in range(2):
-        even = split(in_ref[pl.ds(half, 256, stride=2), :])
-        odd = split(in_ref[pl.ds(512 + half, 256, stride=2), :])
+        even = split(in_ref[pl.ds(half, 256, stride=4), :])
+        odd = split(in_ref[pl.ds(2 + half, 256, stride=4), :])
         even = product(even, (table_ref[0], table_ref[1]), TN)
         odd = product(odd, (table_ref[2], table_ref[3]), TN)
         for cell in range(4):
@@ -494,11 +521,10 @@
     past = along_frag(own[:, 16:40, :], 1)
     info = jnp.concatenate([own[:, 32, :16], past[:, 16, :16]]).astype(jnp.int32).reshape(64, 8)
     region, cell = deposits(info, own, past)
-    cells = lax.all_gather(cell, BOTH, axis=0, tiled=True)[::128, 0].astype(jnp.int32)
     held = traded(region.reshape(16, 256, 128), "grp").reshape(128, 32, 128)
-    total_density, spectrum = forward_z(background, held, tables)
-    spectrum = traded(spectrum.reshape(256, 16, 128), BOTH).reshape(16, 16, 2, 8, 128)
-    spectrum = solve_planes(place, cells, spectrum, tables, window)
+    total_density, spectrum = forward_z(background, held, tables, cell)
+    spectrum = traded(spectrum.reshape(256, 1, 2176), BOTH).reshape(4352, 128)
+    spectrum = solve_planes(place, spectrum, tables, window)
     spectrum = traded(spectrum.reshape(256, 4, 128), BOTH).reshape(1024, 128)
     pieces = boxes(info, spectrum, tables)
     pieces = lay_out(frag_info, traded(pieces, "grp"))

time: 260 us -> 181 us (0.70)
  waiting for transfers between devices: 115 us -> 2.61 us
  blocking collectives: 85.1 us -> 151 us
  starting transfers between devices: 17.2 us -> 3.4 us
  between operations: 14.1 us -> 0.69 us
  local copies, waits for them, and re-layouts: 3.95 us -> 0.12 us
    all_gather x1 -> x0, waiting for transfers between devices: 112 us -> none  [body(): lax.all_gather(cell, BOTH, axis=0, tiled=True)[::128, 0].astype(jnp.int32)]
    all_to_all x4 -> x5, blocking collectives: 85.1 us -> 151 us  [traded(): return lax.all_to_all(block, axis, split_axis=0, concat_axis=0, tiled=True)]
    all_to_all x1 -> x0, starting transfers between devices: 13.8 us -> none  [traded(): return lax.all_to_all(block, axis, split_axis=0, concat_axis=0, tiled=True)]
  transfers between devices with their start and end apart: 3 -> 1, of which waited for: 2 -> 1; matrix products, arithmetic and copies ran while one was open for 1% -> 0% of each run, Pallas kernels for 0% -> 0%
where the time goes in v5:
time: 181 us
  blocking collectives  151 us (83%)
  Pallas kernels  23.3 us (13%)
  starting transfers between devices  3.4 us (2%)
  waiting for transfers between devices  2.61 us (1%)
    all_to_all x5, blocking collectives, traded(): return lax.all_to_all(block, axis, split_axis=0, concat_axis=0, tiled=True)  151 us
    pallas_call x1, Pallas kernels, solve_planes(): pl.pallas_call(planes_kernel, grid=(2,), in_specs=[pl.BlockSpec(memory_sp...  6.73 us
    pallas_call x1, Pallas kernels, densities(): pl.pallas_call(density_kernel, in_specs=[pl.BlockSpec(memory_space=pltpu....  6.66 us
  transfers between devices with their start and end apart: 1, of which 1 were waited for; matrix products, arithmetic and copies ran while one was open for 0% of the time, Pallas kernels for 0%

profile of v5, /device:TPU:1, one launch (start us, length us, event | category | flops | bytes accessed | tf_op | source)
XLA Modules:
  0.0 180.9 jit_solution(10639835382620533978)
XLA Ops:
  0.6 6.7 %densities.1 = f32[16,40,128]{2,1,0:T(8,128)} custom-call(s32[2,8]{1,0:T(2,128)} %info_ref.1, bf16[16,256,32]{2,1,0:T(8,128)(2,1)} %bitcast.23, bf16[4,2,256,1024]{3,2,1,0:T(8,128)(2,1)} %constant.19.clone.planes_ref, bf16[2,2,512,256]{3,2,1,0:T(8,128)(2,1)} %constant.20.clone.depths_ref), custom_call_target="tpu_custom_call" | custom-call | tf_op jit(solution)/shard_map/densities/pallas_call | solution.py:177
  7.3 16.1 %all_to_all.25.own_ref = f32[16,40,128]{2,1,0:T(8,128)S(1)} all-to-all(f32[16,40,128]{2,1,0:T(8,128)} %densities.1), channel_id=1, replica_groups=mesh['frag'=16,'grp'=16] {'grp'}, dimensions={0} | all-to-all | bytes 655360 | tf_op jit(solution)/shard_map/all_to_all | solution.py:512
  23.4 3.4 %collective-permute-start = (f32[16,24,128]{2,1,0:T(8,128)S(1)}, f32[16,24,128]{2,1,0:T(8,128)S(1)}, u32[]{:S(2)}, u32[]{:S(2)}) collective-permute-start(f32[16,24,128]{2,1,0:T(8,128)S(1)} %slice.13), channel_id=1, source_target_pairs={{0,16},{16,32},{32,48},{48,64},{64,80},{80,96},{96,112},{112,128},... | collective-permute-start | bytes 589832 | tf_op jit(solution)/shard_map/ppermute | solution.py:508
  26.8 2.6 %collective-permute-done.past_ref = f32[16,24,128]{2,1,0:T(8,128)S(1)} collective-permute-done((f32[16,24,128]{2,1,0:T(8,128)S(1)}, f32[16,24,128]{2,1,0:T(8,128)S(1)}, u32[]{:S(2)}, u32[]{:S(2)}) %collective-permute-start) | collective-permute-done | bytes 196640 | tf_op jit(solution)/shard_map/ppermute | solution.py:508
  29.4 0.1 convert_element_type.8.info_ref
  29.5 3.1 %deposits.1 = (f32[32,4,32,128]{3,2,1,0:T(8,128)S(1)}, f32[8,128]{1,0:T(8,128)S(1)}) custom-call(s32[64,8]{1,0:T(8,128)S(1)} %convert_element_type.8.info_ref, f32[16,40,128]{2,1,0:T(8,128)S(1)} %all_to_all.25.own_ref, f32[16,24,128]{2,1,0:T(8,128)S(1)} %collective-permute-done.past_ref), custom_call_target="tpu_custom_call" | custom-call | tf_op jit(solution)/shard_map/deposits/pallas_call | solution.py:256
  32.6 0.0 copy-start
  32.6 0.0 copy-start.1
  32.6 27.8 %all_to_all.26 = f32[16,256,128]{2,1,0:T(8,128)S(1)} all-to-all(f32[16,256,128]{2,1,0:T(8,128)S(1)} %bitcast.20), channel_id=1, replica_groups=mesh['frag'=16,'grp'=16] {'grp'}, dimensions={0} | all-to-all | bytes 4194304 | tf_op jit(solution)/shard_map/all_to_all | solution.py:512
  60.5 0.0 copy-done
  60.5 0.0 copy-done.1
  60.5 2.9 %forward_z.1 = (f32[32,32,512]{2,1,0:T(8,128)}, f32[4352,128]{1,0:T(8,128)S(1)}) custom-call(f32[32,32,512]{2,1,0:T(8,128)S(1)} %copy-done.1, f32[128,32,128]{2,1,0:T(8,128)S(1)} %bitcast.18, bf16[10,256,256]{2,1,0:T(8,128)(2,1)S(1)} %copy-done, f32[8,128]{1,0:T(8,128)S(1)} %get-tuple-element.10.cell_ref), custom_call_target="tpu_custom_call" | custom-call | tf_op jit(solution)/shard_map/forward_z/pallas_call | solution.py:303
  63.4 0.0 copy-start.2
  63.4 68.5 %all_to_all.27 = f32[256,1,2176]{2,1,0:T(1,128)S(1)} all-to-all(f32[256,1,2176]{2,1,0:T(1,128)S(1)} %bitcast.19), channel_id=1, replica_groups=mesh['frag'=16,'grp'=16] {'frag','grp'}, dimensions={0} | all-to-all | bytes 4456448 | tf_op jit(solution)/shard_map/all_to_all | solution.py:512
  131.9 0.0 copy-done.2
  131.9 6.7 %solve_planes.1 = f32[1024,128]{1,0:T(8,128)S(1)} custom-call(s32[1]{0:T(128)} %bitcast.place_ref, f32[4352,128]{1,0:T(8,128)S(1)} %bitcast.17, bf16[10,256,256]{2,1,0:T(8,128)(2,1)S(1)} %copy-done, bf16[2,576,512]{2,1,0:T(8,128)(2,1)S(1)} %copy-done.2), custom_call_target="tpu_custom_call" | custom-call | tf_op jit(solution)/shard_map/solve_planes/pallas_call | solution.py:396
  138.7 0.0 copy-start.3
  138.7 28.2 %all_to_all.28 = f32[256,4,128]{2,1,0:T(4,128)S(1)} all-to-all(f32[256,4,128]{2,1,0:T(4,128)S(1)} %bitcast.22), channel_id=1, replica_groups=mesh['frag'=16,'grp'=16] {'frag','grp'}, dimensions={0} | all-to-all | bytes 1048576 | tf_op jit(solution)/shard_map/all_to_all | solution.py:512
  166.9 2.3 %boxes.1 = f32[16,32,128]{2,1,0:T(8,128)S(1)} custom-call(s32[64,8]{1,0:T(8,128)S(1)} %convert_element_type.8.info_ref, f32[1024,128]{1,0:T(8,128)S(1)} %bitcast.21, bf16[10,256,256]{2,1,0:T(8,128)(2,1)S(1)} %copy-done), custom_call_target="tpu_custom_call" | custom-call | tf_op jit(solution)/shard_map/boxes/pallas_call | solution.py:458
  169.2 10.1 %all_to_all.29.in_ref = f32[16,32,128]{2,1,0:T(8,128)S(1)} all-to-all(f32[16,32,128]{2,1,0:T(8,128)S(1)} %boxes.1), channel_id=1, replica_groups=mesh['frag'=16,'grp'=16] {'grp'}, dimensions={0} | all-to-all | bytes 524288 | tf_op jit(solution)/shard_map/all_to_all | solution.py:512
  179.4 0.0 copy-done.3
  179.4 1.5 lay_out.1
  (4 shorter events, 0.0 us)
Async XLA Ops:
  23.4 6.0 %collective-permute-start = (f32[16,24,128]{2,1,0:T(8,128)S(1)}, f32[16,24,128]{2,1,0:T(8,128)S(1)}, u32[]{:S(2)}, u32[]{:S(2)}) collective-permute-start(f32[16,24,128]{2,1,0:T(8,128)S(1)} %slice.13), channel_id=1, source_target_pairs={{0,16},{16,32},{32,48},{48,64},{64,80},{80,96},{96,112},{112,128},... | collective-permute-start | bytes 589832 | tf_op jit(solution)/shard_map/ppermute | solution.py:508
  32.6 27.9 %copy-start = (bf16[10,256,256]{2,1,0:T(8,128)(2,1)S(1)}, bf16[10,256,256]{2,1,0:T(8,128)(2,1)}, u32[]{:S(2)}) copy-start(bf16[10,256,256]{2,1,0:T(8,128)(2,1)} %constant.17.clone.table_ref.tables_ref) | copy-start | bytes 3932164
  32.6 27.9 %copy-start.1 = (f32[32,32,512]{2,1,0:T(8,128)S(1)}, f32[32,32,512]{2,1,0:T(8,128)}, u32[]{:S(2)}) copy-start(f32[32,32,512]{2,1,0:T(8,128)} %back_ref.1) | copy-start | bytes 6291460
  63.4 68.5 %copy-start.2 = (bf16[2,576,512]{2,1,0:T(8,128)(2,1)S(1)}, bf16[2,576,512]{2,1,0:T(8,128)(2,1)}, u32[]{:S(2)}) copy-start(bf16[2,576,512]{2,1,0:T(8,128)(2,1)} %constant.18.clone.window_ref) | copy-start | bytes 3538948
  138.7 40.7 %copy-start.3 = (s32[2,8]{1,0:T(2,128)S(1)}, s32[2,8]{1,0:T(2,128)}, u32[]{:S(2)}) copy-start(s32[2,8]{1,0:T(2,128)} %info_ref.1) | copy-start | bytes 196

commit v6 on v5

--- a/solution.py
+++ b/solution.py
@@ -158,17 +158,18 @@
                 owner = 2 * (2 * part + tile)
                 low = lanes_of(here.shape) < 64
                 if f == 0:
-                    out_ref[owner, 0:32, :] = here
-                    out_ref[owner + 1, 0:32, :] = turned
+                    out_ref[33 * owner : 33 * owner + 32, :] = here
+                    out_ref[33 * owner + 33 : 33 * owner + 65, :] = turned
                 else:
-                    out_ref[owner, 0:32, :] = jnp.where(low, out_ref[owner, 0:32, :], turned)
-                    out_ref[owner + 1, 0:32, :] = jnp.where(low, out_ref[owner + 1, 0:32, :], here)
-    lane = lanes_of((8, 128))
-    note = jnp.zeros((8, 128), F32)
+                    for first, value in ((33 * owner, turned), (33 * owner + 33, here)):
+                        place = slice(first, first + 32)
+                        out_ref[place, :] = jnp.where(low, out_ref[place, :], value)
+    lane = lanes_of((1, 128))
+    note = jnp.zeros((1, 128), F32)
     for place in range(16):
         note = jnp.where(lane == place, info_ref[place // 8, place % 8].astype(F32), note)
     for owner in range(16):
-        out_ref[owner, 32:40, :] = note
+        out_ref[33 * owner + 32 : 33 * owner + 33, :] = note
 
 
 def densities(info, orbitals):
@@ -183,7 +184,7 @@
             pl.BlockSpec(memory_space=pl.ANY),
         ],
         out_specs=pl.BlockSpec(memory_space=pltpu.VMEM),
-        out_shape=jax.ShapeDtypeStruct((16, 40, 128), F32),
+        out_shape=jax.ShapeDtypeStruct((528, 128), F32),
         scratch_shapes=[
             pltpu.VMEM((16, 32, 256), BF16),
             pltpu.VMEM((2, 2, 256, 1024), BF16),
@@ -213,8 +214,8 @@
     out_ref[...] = jnp.zeros(out_ref.shape, F32)
 
     def source(s, carry):
-        own = own_ref[s, 0:32, :]
-        past = past_ref[s, 0:16, :]
+        own = own_ref[pl.ds(s * 33, 32), :]
+        past = past_ref[pl.ds(s * 17, 16), :]
         lane = lanes_of((16, 128))
         adds = []
         for f in range(2):
@@ -383,13 +384,24 @@
         window = (window_ref[0, place, :], window_ref[1, place, :])
         rows = slice(group * 32, group * 32 + 64)
         value = product(window, (wave_ref[0, rows, :], wave_ref[1, rows, :]), NT)
-        for half in range(2):
-            joined = jnp.zeros((16, 128), F32)
-            for cell in range(4):
-                piece = jnp.concatenate([value[16 * cell : 16 * cell + 16]] * 2, 1)
-                piece = pltpu.roll(piece, (32 * (cell - half)) % 128, 1)
-                joined = jnp.where((lane >> 5) == cell, piece, joined)
-            out_ref[pl.ds(group * 64 + 2 * kk + half, 16, stride=4), :] = joined
+        joined = jnp.zeros((16, 128), F32)
+        spare = jnp.zeros((16, 128), F32)
+        for cell in range(4):
+            piece = jnp.concatenate([value[16 * cell : 16 * cell + 16]] * 2, 1)
+            here = pltpu.roll(piece, 32 * cell, 1) if cell else piece
+            joined = jnp.where((lane >> 5) == cell, here, joined)
+            here = pltpu.roll(piece, (16 * cell + 96) % 128, 1)
+            spare = jnp.where(((lane >> 4) & 3) == cell, here, spare)
+        out_ref[pl.ds(group * 48 + kk, 16, stride=3), :] = joined
+        place = pl.ds(group * 48 + 2, 16, stride=3)
+
+        @pl.when(kk == 0)
+        def _():
+            out_ref[place, :] = spare
+
+        @pl.when(kk == 1)
+        def _():
+            out_ref[place, :] = jnp.where(lane < 64, out_ref[place, :], pltpu.roll(spare, 64, 1))
 
 
 def solve_planes(place, waves, tables, window):
@@ -402,8 +414,8 @@
             pl.BlockSpec(memory_space=pltpu.VMEM),
             pl.BlockSpec(memory_space=pltpu.VMEM),
         ],
-        out_specs=pl.BlockSpec((1024, 128), lambda kk: (0, 0)),
-        out_shape=jax.ShapeDtypeStruct((1024, 128), F32),
+        out_specs=pl.BlockSpec((768, 128), lambda kk: (0, 0)),
+        out_shape=jax.ShapeDtypeStruct((768, 128), F32),
         scratch_shapes=[
             pltpu.VMEM((16, 4, 8, 512), F32),
             pltpu.VMEM((2, 544, 512), BF16),
@@ -415,18 +427,21 @@
 
 
 def boxes_kernel(info_ref, in_ref, table_ref, out_ref, grid_ref):
-    for half in range(2):
-        even = split(in_ref[pl.ds(half, 256, stride=4), :])
-        odd = split(in_ref[pl.ds(2 + half, 256, stride=4), :])
-        even = product(even, (table_ref[0], table_ref[1]), TN)
-        odd = product(odd, (table_ref[2], table_ref[3]), TN)
-        for cell in range(4):
-            first = 32 * cell
-            for tile in range(4):
-                columns = slice(tile % 2 * 128, tile % 2 * 128 + 128)
-                near, far = even[first : first + 32, columns], odd[first : first + 32, columns]
-                place = slice(64 * cell + 32 * half, 64 * cell + 32 * half + 32)
-                grid_ref[tile, place, :] = near + far if tile < 2 else near - far
+    even = product(split(in_ref[pl.ds(0, 256, stride=3), :]), (table_ref[0], table_ref[1]), TN)
+    odd = product(split(in_ref[pl.ds(1, 256, stride=3), :]), (table_ref[2], table_ref[3]), TN)
+    spare = split(in_ref[pl.ds(2, 256, stride=3), :])
+    spare_even = product(spare, (table_ref[0], table_ref[1]), TN)
+    spare_odd = product(spare, (table_ref[2], table_ref[3]), TN)
+    for cell in range(4):
+        for tile in range(4):
+            columns = slice(tile % 2 * 128, tile % 2 * 128 + 128)
+            rows = slice(32 * cell, 32 * cell + 32)
+            near, far = even[rows, columns], odd[rows, columns]
+            grid_ref[tile, 48 * cell : 48 * cell + 32, :] = near + far if tile < 2 else near - far
+            near = spare_even[16 * cell : 16 * cell + 16, columns]
+            far = spare_odd[64 + 16 * cell : 80 + 16 * cell, columns]
+            place = slice(48 * cell + 32, 48 * cell + 48)
+            grid_ref[tile, place, :] = near + far if tile < 2 else near - far
     base = first_cell(info_ref)
 
     def source(s, carry):
@@ -442,7 +457,7 @@
             offset = (cell_z & 7) * 16
             for r in range(2):
                 cell = (info_ref[number, 1] + r - base) & 3
-                place = pl.ds(pl.multiple_of(cell * 64 + start, 16), 32)
+                place = pl.ds(pl.multiple_of(cell * 48 + start, 16), 32)
                 value = jnp.where(
                     lane >= offset, grid_ref[tile, place, :], grid_ref[after, place, :]
                 )
@@ -465,7 +480,7 @@
         ],
         out_specs=pl.BlockSpec(memory_space=pltpu.VMEM),
         out_shape=jax.ShapeDtypeStruct((16, 32, 128), F32),
-        scratch_shapes=[pltpu.VMEM((4, 256, 128), F32)],
+        scratch_shapes=[pltpu.VMEM((4, 192, 128), F32)],
         compiler_params=pltpu.CompilerParams(vmem_limit_bytes=VMEM_LIMIT),
         name="boxes",
     )(info, waves, table)
@@ -517,15 +532,17 @@
     place = (lax.axis_index("frag") * 16 + lax.axis_index("grp")).astype(jnp.int32).reshape(1)
     frag_info, place = lax.optimization_barrier((frag_info, place))
     coeffs = orbitals.reshape(16, 256, 32)
-    own = traded(densities(frag_info, coeffs), "grp")
-    past = along_frag(own[:, 16:40, :], 1)
-    info = jnp.concatenate([own[:, 32, :16], past[:, 16, :16]]).astype(jnp.int32).reshape(64, 8)
+    own = traded(densities(frag_info, coeffs).reshape(16, 1, 4224), "grp")
+    past = along_frag(own[:, :, 2048:], 1)
+    info = jnp.concatenate([own[:, 0, 4096:4112], past[:, 0, 2048:2064]])
+    info = info.astype(jnp.int32).reshape(64, 8)
+    own, past = own.reshape(528, 128), past.reshape(272, 128)
     region, cell = deposits(info, own, past)
     held = traded(region.reshape(16, 256, 128), "grp").reshape(128, 32, 128)
     total_density, spectrum = forward_z(background, held, tables, cell)
     spectrum = traded(spectrum.reshape(256, 1, 2176), BOTH).reshape(4352, 128)
     spectrum = solve_planes(place, spectrum, tables, window)
-    spectrum = traded(spectrum.reshape(256, 4, 128), BOTH).reshape(1024, 128)
+    spectrum = traded(spectrum.reshape(256, 1, 384), BOTH).reshape(768, 128)
     pieces = boxes(info, spectrum, tables)
     pieces = lay_out(frag_info, traded(pieces, "grp"))
     frag_potential = pieces.reshape(256, 2, 128).transpose(1, 0, 2).reshape(2, 32768)

time: 181 us -> 189 us (1.044)
  Pallas kernels: 23.3 us -> 33.8 us
  blocking collectives: 151 us -> 148 us
    pallas_call x1, Pallas kernels: 6.73 us -> 17.3 us  [solve_planes(): pl.pallas_call(planes_kernel, grid=(2,), in_specs=[pl.BlockSpec(memory_sp...]
    all_to_all x5, blocking collectives: 151 us -> 148 us  [traded(): return lax.all_to_all(block, axis, split_axis=0, concat_axis=0, tiled=True)]
where the time goes in v6:
time: 189 us; the launch traced here: 188 us
  blocking collectives  148 us (78%)
  Pallas kernels  33.8 us (18%)
  starting transfers between devices  3.66 us (2%)
  waiting for transfers between devices  2.02 us (1%)
    all_to_all x5, blocking collectives, traded(): return lax.all_to_all(block, axis, split_axis=0, concat_axis=0, tiled=True)  148 us
    pallas_call x1, Pallas kernels, solve_planes(): pl.pallas_call(planes_kernel, grid=(2,), in_specs=[pl.BlockSpec(memory_sp...  17.3 us
    pallas_call x1, Pallas kernels, densities(): pl.pallas_call(density_kernel, in_specs=[pl.BlockSpec(memory_space=pltpu....  6.64 us
  transfers between devices with their start and end apart: 1, of which 1 were waited for; matrix products, arithmetic and copies ran while one was open for 0% of the time, Pallas kernels for 0%

profile of v6, /device:TPU:1, one launch (start us, length us, event | category | flops | bytes accessed | tf_op | source)
XLA Modules:
  0.0 188.3 jit_solution(9966315289340111457)
XLA Ops:
  0.6 6.6 %densities.1 = f32[528,128]{1,0:T(8,128)} custom-call(s32[2,8]{1,0:T(2,128)} %info_ref.1, bf16[16,256,32]{2,1,0:T(8,128)(2,1)} %bitcast.29, bf16[4,2,256,1024]{3,2,1,0:T(8,128)(2,1)} %constant.19.clone.planes_ref, bf16[2,2,512,256]{3,2,1,0:T(8,128)(2,1)} %constant.20.clone.depths_ref), custom_call_target="tpu_custom_call" | custom-call | tf_op jit(solution)/shard_map/densities/pallas_call | solution.py:178
  7.3 15.2 %all_to_all.25 = f32[16,1,4224]{2,1,0:T(1,128)S(1)} all-to-all(f32[16,1,4224]{2,1,0:T(1,128)} %bitcast.28), channel_id=1, replica_groups=mesh['frag'=16,'grp'=16] {'grp'}, dimensions={0} | all-to-all | bytes 540672 | tf_op jit(solution)/shard_map/all_to_all | solution.py:527
  22.5 3.7 %collective-permute-start = (f32[16,1,2176]{2,1,0:T(1,128)S(1)}, f32[16,1,2176]{2,1,0:T(1,128)S(1)}, u32[]{:S(2)}, u32[]{:S(2)}) collective-permute-start(f32[16,1,2176]{2,1,0:T(1,128)S(1)} %slice.13), channel_id=1, source_target_pairs={{0,16},{16,32},{32,48},{48,64},{64,80},{80,96},{96,112},{112,128},... | collective-permute-start | bytes 417800 | tf_op jit(solution)/shard_map/ppermute | solution.py:523
  26.2 2.0 %collective-permute-done = f32[16,1,2176]{2,1,0:T(1,128)S(1)} collective-permute-done((f32[16,1,2176]{2,1,0:T(1,128)S(1)}, f32[16,1,2176]{2,1,0:T(1,128)S(1)}, u32[]{:S(2)}, u32[]{:S(2)}) %collective-permute-start) | collective-permute-done | bytes 139296 | tf_op jit(solution)/shard_map/ppermute | solution.py:523
  28.2 0.1 convert_element_type.8.info_ref
  28.3 3.1 %deposits.1 = (f32[32,4,32,128]{3,2,1,0:T(8,128)S(1)}, f32[8,128]{1,0:T(8,128)S(1)}) custom-call(s32[64,8]{1,0:T(8,128)S(1)} %convert_element_type.8.info_ref, f32[528,128]{1,0:T(8,128)S(1)} %bitcast.24, f32[272,128]{1,0:T(8,128)S(1)} %bitcast.27), custom_call_target="tpu_custom_call" | custom-call | tf_op jit(solution)/shard_map/deposits/pallas_call | solution.py:257
  31.4 0.0 copy-start
  31.4 0.0 copy-start.1
  31.4 27.6 %all_to_all.26 = f32[16,256,128]{2,1,0:T(8,128)S(1)} all-to-all(f32[16,256,128]{2,1,0:T(8,128)S(1)} %bitcast.23), channel_id=1, replica_groups=mesh['frag'=16,'grp'=16] {'grp'}, dimensions={0} | all-to-all | bytes 4194304 | tf_op jit(solution)/shard_map/all_to_all | solution.py:527
  59.0 0.0 copy-done
  59.0 0.0 copy-done.1
  59.0 3.0 %forward_z.1 = (f32[32,32,512]{2,1,0:T(8,128)}, f32[4352,128]{1,0:T(8,128)S(1)}) custom-call(f32[32,32,512]{2,1,0:T(8,128)S(1)} %copy-done.1, f32[128,32,128]{2,1,0:T(8,128)S(1)} %bitcast.21, bf16[10,256,256]{2,1,0:T(8,128)(2,1)S(1)} %copy-done, f32[8,128]{1,0:T(8,128)S(1)} %get-tuple-element.10.cell_ref), custom_call_target="tpu_custom_call" | custom-call | tf_op jit(solution)/shard_map/forward_z/pallas_call | solution.py:304
  61.9 0.0 copy-start.2
  61.9 68.8 %all_to_all.27 = f32[256,1,2176]{2,1,0:T(1,128)S(1)} all-to-all(f32[256,1,2176]{2,1,0:T(1,128)S(1)} %bitcast.22), channel_id=1, replica_groups=mesh['frag'=16,'grp'=16] {'frag','grp'}, dimensions={0} | all-to-all | bytes 4456448 | tf_op jit(solution)/shard_map/all_to_all | solution.py:527
  130.7 0.0 copy-done.2
  130.7 17.3 %solve_planes.1 = f32[768,128]{1,0:T(8,128)S(1)} custom-call(s32[1]{0:T(128)} %bitcast.place_ref, f32[4352,128]{1,0:T(8,128)S(1)} %bitcast.20, bf16[10,256,256]{2,1,0:T(8,128)(2,1)S(1)} %copy-done, bf16[2,576,512]{2,1,0:T(8,128)(2,1)S(1)} %copy-done.2), custom_call_target="tpu_custom_call" | custom-call | tf_op jit(solution)/shard_map/solve_planes/pallas_call | solution.py:408
  148.0 0.0 copy-start.3
  148.0 25.8 %all_to_all.28 = f32[256,1,384]{2,1,0:T(1,128)S(1)} all-to-all(f32[256,1,384]{2,1,0:T(1,128)S(1)} %bitcast.26), channel_id=1, replica_groups=mesh['frag'=16,'grp'=16] {'frag','grp'}, dimensions={0} | all-to-all | bytes 786432 | tf_op jit(solution)/shard_map/all_to_all | solution.py:527
  173.9 2.3 %boxes.1 = f32[16,32,128]{2,1,0:T(8,128)S(1)} custom-call(s32[64,8]{1,0:T(8,128)S(1)} %convert_element_type.8.info_ref, f32[768,128]{1,0:T(8,128)S(1)} %bitcast.25, bf16[10,256,256]{2,1,0:T(8,128)(2,1)S(1)} %copy-done), custom_call_target="tpu_custom_call" | custom-call | tf_op jit(solution)/shard_map/boxes/pallas_call | solution.py:473
  176.2 10.6 %all_to_all.29.in_ref = f32[16,32,128]{2,1,0:T(8,128)S(1)} all-to-all(f32[16,32,128]{2,1,0:T(8,128)S(1)} %boxes.1), channel_id=1, replica_groups=mesh['frag'=16,'grp'=16] {'grp'}, dimensions={0} | all-to-all | bytes 524288 | tf_op jit(solution)/shard_map/all_to_all | solution.py:527
  186.8 0.0 copy-done.3
  186.8 1.5 lay_out.1
  (4 shorter events, 0.0 us)
Async XLA Ops:
  22.5 5.7 %collective-permute-start = (f32[16,1,2176]{2,1,0:T(1,128)S(1)}, f32[16,1,2176]{2,1,0:T(1,128)S(1)}, u32[]{:S(2)}, u32[]{:S(2)}) collective-permute-start(f32[16,1,2176]{2,1,0:T(1,128)S(1)} %slice.13), channel_id=1, source_target_pairs={{0,16},{16,32},{32,48},{48,64},{64,80},{80,96},{96,112},{112,128},... | collective-permute-start | bytes 417800 | tf_op jit(solution)/shard_map/ppermute | solution.py:523
  31.4 27.6 %copy-start = (bf16[10,256,256]{2,1,0:T(8,128)(2,1)S(1)}, bf16[10,256,256]{2,1,0:T(8,128)(2,1)}, u32[]{:S(2)}) copy-start(bf16[10,256,256]{2,1,0:T(8,128)(2,1)} %constant.17.clone.table_ref.tables_ref) | copy-start | bytes 3932164
  31.4 27.6 %copy-start.1 = (f32[32,32,512]{2,1,0:T(8,128)S(1)}, f32[32,32,512]{2,1,0:T(8,128)}, u32[]{:S(2)}) copy-start(f32[32,32,512]{2,1,0:T(8,128)} %back_ref.1) | copy-start | bytes 6291460
  61.9 68.8 %copy-start.2 = (bf16[2,576,512]{2,1,0:T(8,128)(2,1)S(1)}, bf16[2,576,512]{2,1,0:T(8,128)(2,1)}, u32[]{:S(2)}) copy-start(bf16[2,576,512]{2,1,0:T(8,128)(2,1)} %constant.18.clone.window_ref) | copy-start | bytes 3538948
  148.0 38.8 %copy-start.3 = (s32[2,8]{1,0:T(2,128)S(1)}, s32[2,8]{1,0:T(2,128)}, u32[]{:S(2)}) copy-start(s32[2,8]{1,0:T(2,128)} %info_ref.1) | copy-start | bytes 196

commit v7 on v6

--- a/solution.py
+++ b/solution.py
@@ -121,8 +121,19 @@
 
 
 def density_kernel(
-    info_ref, orbitals_ref, planes_ref, depths_ref, out_ref, coeff_ref, plane_ref, depth_ref, sems
+    info_ref,
+    source_ref,
+    planes_ref,
+    depths_ref,
+    out_ref,
+    orbitals_ref,
+    coeff_ref,
+    plane_ref,
+    depth_ref,
+    sems,
 ):
+    orbitals_copy = pltpu.make_async_copy(source_ref, orbitals_ref, sems.at[4])
+    orbitals_copy.start()
     copies = []
     for f in range(2):
         pair = 2 * info_ref[f, 4] + info_ref[f, 5] - 3
@@ -132,8 +143,9 @@
                 depths_ref.at[info_ref[f, 3] - 1], depth_ref.at[f], sems.at[2 * f + 1]
             )
         )
-    for copy in copies:
-        copy.start()
+    copies[0].start()
+    copies[1].start()
+    orbitals_copy.wait()
     for a in range(16):
         coeff_ref[a] = jnp.transpose(orbitals_ref[a].astype(F32)).astype(BF16)
     for f in range(2):
@@ -142,6 +154,9 @@
         coeffs = coeff_ref[:, 16 * f : 16 * f + 16, :].reshape(256, 256)
         copies[2 * f].wait()
         copies[2 * f + 1].wait()
+        if f == 0:
+            copies[2].start()
+            copies[3].start()
         for part in range(4):
             columns = slice(part * 256, (part + 1) * 256)
             flat = jnp.dot(coeffs, plane_ref[f, 1, :, columns], preferred_element_type=F32)
@@ -179,17 +194,18 @@
         density_kernel,
         in_specs=[
             pl.BlockSpec(memory_space=pltpu.SMEM),
-            pl.BlockSpec(memory_space=pltpu.VMEM),
+            pl.BlockSpec(memory_space=pl.ANY),
             pl.BlockSpec(memory_space=pl.ANY),
             pl.BlockSpec(memory_space=pl.ANY),
         ],
         out_specs=pl.BlockSpec(memory_space=pltpu.VMEM),
         out_shape=jax.ShapeDtypeStruct((528, 128), F32),
         scratch_shapes=[
+            pltpu.VMEM((16, 256, 32), BF16),
             pltpu.VMEM((16, 32, 256), BF16),
             pltpu.VMEM((2, 2, 256, 1024), BF16),
             pltpu.VMEM((2, 2, 512, 256), BF16),
-            pltpu.SemaphoreType.DMA((4,)),
+            pltpu.SemaphoreType.DMA((5,)),
         ],
         compiler_params=pltpu.CompilerParams(vmem_limit_bytes=56 * 1024 * 1024),
         name="densities",
@@ -250,7 +266,7 @@
             out_ref[row, tile, pl.ds(start, 16), :] += value
         return carry
 
-    lax.fori_loop(0, 16, source, 0, unroll=2)
+    lax.fori_loop(0, 16, source, 0, unroll=4)
 
 
 def deposits(info, own, past):
@@ -394,14 +410,7 @@
             spare = jnp.where(((lane >> 4) & 3) == cell, here, spare)
         out_ref[pl.ds(group * 48 + kk, 16, stride=3), :] = joined
         place = pl.ds(group * 48 + 2, 16, stride=3)
-
-        @pl.when(kk == 0)
-        def _():
-            out_ref[place, :] = spare
-
-        @pl.when(kk == 1)
-        def _():
-            out_ref[place, :] = jnp.where(lane < 64, out_ref[place, :], pltpu.roll(spare, 64, 1))
+        out_ref[place, :] = jnp.where((lane >> 6) == kk, spare, out_ref[place, :])
 
 
 def solve_planes(place, waves, tables, window):
@@ -466,7 +475,7 @@
         out_ref[s] = total
         return carry
 
-    lax.fori_loop(0, 16, source, 0, unroll=2)
+    lax.fori_loop(0, 16, source, 0, unroll=4)
 
 
 def boxes(info, waves, table):

time: 189 us -> 178 us (0.942)
  Pallas kernels: 33.8 us -> 22.7 us
    pallas_call x1, Pallas kernels: 17.3 us -> 6.76 us  [solve_planes(): pl.pallas_call(planes_kernel, grid=(2,), in_specs=[pl.BlockSpec(memory_sp...]
where the time goes in v7:
time: 178 us; the launch traced here: 177 us
  blocking collectives  148 us (83%)
  Pallas kernels  22.7 us (13%)
  starting transfers between devices  3.65 us (2%)
  waiting for transfers between devices  2.02 us (1%)
    all_to_all x5, blocking collectives, traded(): return lax.all_to_all(block, axis, split_axis=0, concat_axis=0, tiled=True)  148 us
    pallas_call x1, Pallas kernels, solve_planes(): pl.pallas_call(planes_kernel, grid=(2,), in_specs=[pl.BlockSpec(memory_sp...  6.76 us
    pallas_call x1, Pallas kernels, densities(): pl.pallas_call(density_kernel, in_specs=[pl.BlockSpec(memory_space=pltpu....  6.41 us
    ppermute x1, starting transfers between devices, along_frag(): return lax.ppermute(block, 'frag', route)  3.65 us
  transfers between devices with their start and end apart: 1, of which 1 were waited for; matrix products, arithmetic and copies ran while one was open for 0% of the time, Pallas kernels for 0%

profile of v7, /device:TPU:1, one launch (start us, length us, event | category | flops | bytes accessed | tf_op | source)
XLA Modules:
  0.0 177.2 jit_solution(14032556202518957211)
XLA Ops:
  0.6 6.4 %densities.1 = f32[528,128]{1,0:T(8,128)} custom-call(s32[2,8]{1,0:T(2,128)} %info_ref.1, bf16[16,256,32]{2,1,0:T(8,128)(2,1)} %bitcast.29, bf16[4,2,256,1024]{3,2,1,0:T(8,128)(2,1)} %constant.19.clone.planes_ref, bf16[2,2,512,256]{3,2,1,0:T(8,128)(2,1)} %constant.20.clone.depths_ref), custom_call_target="tpu_custom_call" | custom-call | tf_op jit(solution)/shard_map/densities/pallas_call | solution.py:193
  7.1 15.2 %all_to_all.25 = f32[16,1,4224]{2,1,0:T(1,128)S(1)} all-to-all(f32[16,1,4224]{2,1,0:T(1,128)} %bitcast.28), channel_id=1, replica_groups=mesh['frag'=16,'grp'=16] {'grp'}, dimensions={0} | all-to-all | bytes 540672 | tf_op jit(solution)/shard_map/all_to_all | solution.py:536
  22.3 3.7 %collective-permute-start = (f32[16,1,2176]{2,1,0:T(1,128)S(1)}, f32[16,1,2176]{2,1,0:T(1,128)S(1)}, u32[]{:S(2)}, u32[]{:S(2)}) collective-permute-start(f32[16,1,2176]{2,1,0:T(1,128)S(1)} %slice.13), channel_id=1, source_target_pairs={{0,16},{16,32},{32,48},{48,64},{64,80},{80,96},{96,112},{112,128},... | collective-permute-start | bytes 417800 | tf_op jit(solution)/shard_map/ppermute | solution.py:532
  25.9 2.0 %collective-permute-done = f32[16,1,2176]{2,1,0:T(1,128)S(1)} collective-permute-done((f32[16,1,2176]{2,1,0:T(1,128)S(1)}, f32[16,1,2176]{2,1,0:T(1,128)S(1)}, u32[]{:S(2)}, u32[]{:S(2)}) %collective-permute-start) | collective-permute-done | bytes 139296 | tf_op jit(solution)/shard_map/ppermute | solution.py:532
  28.0 0.1 convert_element_type.8.info_ref
  28.0 2.9 %deposits.1 = (f32[32,4,32,128]{3,2,1,0:T(8,128)S(1)}, f32[8,128]{1,0:T(8,128)S(1)}) custom-call(s32[64,8]{1,0:T(8,128)S(1)} %convert_element_type.8.info_ref, f32[528,128]{1,0:T(8,128)S(1)} %bitcast.24, f32[272,128]{1,0:T(8,128)S(1)} %bitcast.27), custom_call_target="tpu_custom_call" | custom-call | tf_op jit(solution)/shard_map/deposits/pallas_call | solution.py:273
  31.0 0.0 copy-start
  31.0 0.0 copy-start.1
  31.0 27.6 %all_to_all.26 = f32[16,256,128]{2,1,0:T(8,128)S(1)} all-to-all(f32[16,256,128]{2,1,0:T(8,128)S(1)} %bitcast.23), channel_id=1, replica_groups=mesh['frag'=16,'grp'=16] {'grp'}, dimensions={0} | all-to-all | bytes 4194304 | tf_op jit(solution)/shard_map/all_to_all | solution.py:536
  58.6 0.0 copy-done
  58.6 0.0 copy-done.1
  58.6 3.0 %forward_z.1 = (f32[32,32,512]{2,1,0:T(8,128)}, f32[4352,128]{1,0:T(8,128)S(1)}) custom-call(f32[32,32,512]{2,1,0:T(8,128)S(1)} %copy-done.1, f32[128,32,128]{2,1,0:T(8,128)S(1)} %bitcast.21, bf16[10,256,256]{2,1,0:T(8,128)(2,1)S(1)} %copy-done, f32[8,128]{1,0:T(8,128)S(1)} %get-tuple-element.10.cell_ref), custom_call_target="tpu_custom_call" | custom-call | tf_op jit(solution)/shard_map/forward_z/pallas_call | solution.py:320
  61.5 0.0 copy-start.2
  61.5 68.8 %all_to_all.27 = f32[256,1,2176]{2,1,0:T(1,128)S(1)} all-to-all(f32[256,1,2176]{2,1,0:T(1,128)S(1)} %bitcast.22), channel_id=1, replica_groups=mesh['frag'=16,'grp'=16] {'frag','grp'}, dimensions={0} | all-to-all | bytes 4456448 | tf_op jit(solution)/shard_map/all_to_all | solution.py:536
  130.3 0.0 copy-done.2
  130.3 6.8 %solve_planes.1 = f32[768,128]{1,0:T(8,128)S(1)} custom-call(s32[1]{0:T(128)} %bitcast.place_ref, f32[4352,128]{1,0:T(8,128)S(1)} %bitcast.20, bf16[10,256,256]{2,1,0:T(8,128)(2,1)S(1)} %copy-done, bf16[2,576,512]{2,1,0:T(8,128)(2,1)S(1)} %copy-done.2), custom_call_target="tpu_custom_call" | custom-call | tf_op jit(solution)/shard_map/solve_planes/pallas_call | solution.py:417
  137.1 0.0 copy-start.3
  137.1 25.9 %all_to_all.28 = f32[256,1,384]{2,1,0:T(1,128)S(1)} all-to-all(f32[256,1,384]{2,1,0:T(1,128)S(1)} %bitcast.26), channel_id=1, replica_groups=mesh['frag'=16,'grp'=16] {'frag','grp'}, dimensions={0} | all-to-all | bytes 786432 | tf_op jit(solution)/shard_map/all_to_all | solution.py:536
  163.0 2.1 %boxes.1 = f32[16,32,128]{2,1,0:T(8,128)S(1)} custom-call(s32[64,8]{1,0:T(8,128)S(1)} %convert_element_type.8.info_ref, f32[768,128]{1,0:T(8,128)S(1)} %bitcast.25, bf16[10,256,256]{2,1,0:T(8,128)(2,1)S(1)} %copy-done), custom_call_target="tpu_custom_call" | custom-call | tf_op jit(solution)/shard_map/boxes/pallas_call | solution.py:482
  165.0 10.6 %all_to_all.29.in_ref = f32[16,32,128]{2,1,0:T(8,128)S(1)} all-to-all(f32[16,32,128]{2,1,0:T(8,128)S(1)} %boxes.1), channel_id=1, replica_groups=mesh['frag'=16,'grp'=16] {'grp'}, dimensions={0} | all-to-all | bytes 524288 | tf_op jit(solution)/shard_map/all_to_all | solution.py:536
  175.6 0.0 copy-done.3
  175.6 1.5 lay_out.1
  (4 shorter events, 0.0 us)
Async XLA Ops:
  22.3 5.7 %collective-permute-start = (f32[16,1,2176]{2,1,0:T(1,128)S(1)}, f32[16,1,2176]{2,1,0:T(1,128)S(1)}, u32[]{:S(2)}, u32[]{:S(2)}) collective-permute-start(f32[16,1,2176]{2,1,0:T(1,128)S(1)} %slice.13), channel_id=1, source_target_pairs={{0,16},{16,32},{32,48},{48,64},{64,80},{80,96},{96,112},{112,128},... | collective-permute-start | bytes 417800 | tf_op jit(solution)/shard_map/ppermute | solution.py:532
  31.0 27.6 %copy-start = (bf16[10,256,256]{2,1,0:T(8,128)(2,1)S(1)}, bf16[10,256,256]{2,1,0:T(8,128)(2,1)}, u32[]{:S(2)}) copy-start(bf16[10,256,256]{2,1,0:T(8,128)(2,1)} %constant.17.clone.table_ref.tables_ref) | copy-start | bytes 3932164
  31.0 27.6 %copy-start.1 = (f32[32,32,512]{2,1,0:T(8,128)S(1)}, f32[32,32,512]{2,1,0:T(8,128)}, u32[]{:S(2)}) copy-start(f32[32,32,512]{2,1,0:T(8,128)} %back_ref.1) | copy-start | bytes 6291460
  61.5 68.8 %copy-start.2 = (bf16[2,576,512]{2,1,0:T(8,128)(2,1)S(1)}, bf16[2,576,512]{2,1,0:T(8,128)(2,1)}, u32[]{:S(2)}) copy-start(bf16[2,576,512]{2,1,0:T(8,128)(2,1)} %constant.18.clone.window_ref) | copy-start | bytes 3538948
  137.1 38.6 %copy-start.3 = (s32[2,8]{1,0:T(2,128)S(1)}, s32[2,8]{1,0:T(2,128)}, u32[]{:S(2)}) copy-start(s32[2,8]{1,0:T(2,128)} %info_ref.1) | copy-start | bytes 196

commit v8 on v7

--- a/solution.py
+++ b/solution.py
@@ -225,66 +225,95 @@
     return (2 * jnp.where(shared == 1, first, last) + 31) & 31
 
 
-def deposit_kernel(info_ref, own_ref, past_ref, out_ref, cell_ref):
+def landing(info_ref, number):
+    cell_z = info_ref[number, 2]
+    tile = cell_z >> 3
+    return info_ref[number, 1], tile, (tile + 1) & 3, (cell_z & 7) * 16, info_ref[number, 0] & 1
+
+
+def own_kernel(info_ref, own_ref, out_ref, cell_ref):
     cell_ref[...] = jnp.full((8, 128), first_cell(info_ref).astype(F32))
     out_ref[...] = jnp.zeros(out_ref.shape, F32)
 
     def source(s, carry):
         own = own_ref[pl.ds(s * 33, 32), :]
+        lane = lanes_of((16, 128))
+        adds = []
+        for f in range(2):
+            cell_y, tile, after, offset, odd = landing(info_ref, 2 * s + f)
+            low = jnp.where(odd == 0, offset, 256)
+            part_inside = (lane >= low) & (lane < low + 32)
+            part_beyond = lane < jnp.where(odd == 0, offset - 96, 0)
+            inside = (lane >= offset) & (lane < offset + 32)
+            beyond = lane < offset - 96
+            start = pl.multiple_of(odd * 16, 16)
+            for r in range(2):
+                row = (cell_y + r) & 31
+                turned = pltpu.roll(own, (offset + 128 - (64 * f + 32 * r)) & 127, 1)
+                top, rest = turned[0:16], turned[16:32]
+                adds.append((row, tile, start, jnp.where(inside, top, 0.0)))
+                adds.append((row, after, start, jnp.where(beyond, top, 0.0)))
+                adds.append((row, tile, 16, jnp.where(part_inside, rest, 0.0)))
+                adds.append((row, after, 16, jnp.where(part_beyond, rest, 0.0)))
+        for row, tile, start, value in adds:
+            out_ref[row, tile, pl.ds(start, 16), :] += value
+        return carry
+
+    lax.fori_loop(0, 16, source, 0, unroll=4)
+
+
+def past_kernel(info_ref, past_ref, in_ref, out_ref):
+    out_ref[...] = in_ref[...]
+
+    def source(s, carry):
         past = past_ref[pl.ds(s * 17, 16), :]
         lane = lanes_of((16, 128))
         adds = []
         for f in range(2):
-            for first, piece in ((0, own), (32, past)):
-                number = first + 2 * s + f
-                odd = info_ref[number, 0] & 1
-                cell_y = info_ref[number, 1]
-                cell_z = info_ref[number, 2]
-                tile = cell_z >> 3
-                after = (tile + 1) & 3
-                offset = (cell_z & 7) * 16
-                kept = odd == 1 if first else odd == 0
-                low = jnp.where(kept, offset, 256)
-                part_inside = (lane >= low) & (lane < low + 32)
-                part_beyond = lane < jnp.where(kept, offset - 96, 0)
-                inside = (lane >= offset) & (lane < offset + 32)
-                beyond = lane < offset - 96
-                for r in range(2):
-                    row = (cell_y + r) & 31
-                    turned = pltpu.roll(piece, (offset + 128 - (64 * f + 32 * r)) & 127, 1)
-                    if first:
-                        adds.append((row, tile, 0, jnp.where(part_inside, turned, 0.0)))
-                        adds.append((row, after, 0, jnp.where(part_beyond, turned, 0.0)))
-                    else:
-                        start = pl.multiple_of(odd * 16, 16)
-                        top, rest = turned[0:16], turned[16:32]
-                        adds.append((row, tile, start, jnp.where(inside, top, 0.0)))
-                        adds.append((row, after, start, jnp.where(beyond, top, 0.0)))
-                        adds.append((row, tile, 16, jnp.where(part_inside, rest, 0.0)))
-                        adds.append((row, after, 16, jnp.where(part_beyond, rest, 0.0)))
-        for row, tile, start, value in adds:
-            out_ref[row, tile, pl.ds(start, 16), :] += value
+            cell_y, tile, after, offset, odd = landing(info_ref, 2 * s + f)
+            low = jnp.where(odd == 1, offset, 256)
+            inside = (lane >= low) & (lane < low + 32)
+            beyond = lane < jnp.where(odd == 1, offset - 96, 0)
+            for r in range(2):
+                row = (cell_y + r) & 31
+                turned = pltpu.roll(past, (offset + 128 - (64 * f + 32 * r)) & 127, 1)
+                adds.append((row, tile, jnp.where(inside, turned, 0.0)))
+                adds.append((row, after, jnp.where(beyond, turned, 0.0)))
+        for row, tile, value in adds:
+            out_ref[row, tile, 0:16, :] += value
         return carry
 
     lax.fori_loop(0, 16, source, 0, unroll=4)
 
 
-def deposits(info, own, past):
+def own_deposits(info, own):
     return pl.pallas_call(
-        deposit_kernel,
+        own_kernel,
+        in_specs=[pl.BlockSpec(memory_space=pltpu.SMEM), pl.BlockSpec(memory_space=pltpu.VMEM)],
+        out_specs=[pl.BlockSpec(memory_space=pltpu.VMEM)] * 2,
+        out_shape=[
+            jax.ShapeDtypeStruct((32, 4, 32, 128), F32),
+            jax.ShapeDtypeStruct((8, 128), F32),
+        ],
+        compiler_params=pltpu.CompilerParams(vmem_limit_bytes=VMEM_LIMIT),
+        name="own_deposits",
+    )(info, own)
+
+
+def past_deposits(info, past, region):
+    return pl.pallas_call(
+        past_kernel,
         in_specs=[
             pl.BlockSpec(memory_space=pltpu.SMEM),
             pl.BlockSpec(memory_space=pltpu.VMEM),
             pl.BlockSpec(memory_space=pltpu.VMEM),
         ],
-        out_specs=[pl.BlockSpec(memory_space=pltpu.VMEM)] * 2,
-        out_shape=[
-            jax.ShapeDtypeStruct((32, 4, 32, 128), F32),
-            jax.ShapeDtypeStruct((8, 128), F32),
-        ],
+        out_specs=pl.BlockSpec(memory_space=pltpu.VMEM),
+        out_shape=jax.ShapeDtypeStruct((32, 4, 32, 128), F32),
+        input_output_aliases={2: 0},
         compiler_params=pltpu.CompilerParams(vmem_limit_bytes=VMEM_LIMIT),
-        name="deposits",
-    )(info, own, past)
+        name="past_deposits",
+    )(info, past, region)
 
 
 def forward_kernel(back_ref, held_ref, table_ref, cell_ref, total_ref, out_ref, turned_ref):
@@ -543,10 +572,10 @@
     coeffs = orbitals.reshape(16, 256, 32)
     own = traded(densities(frag_info, coeffs).reshape(16, 1, 4224), "grp")
     past = along_frag(own[:, :, 2048:], 1)
-    info = jnp.concatenate([own[:, 0, 4096:4112], past[:, 0, 2048:2064]])
-    info = info.astype(jnp.int32).reshape(64, 8)
-    own, past = own.reshape(528, 128), past.reshape(272, 128)
-    region, cell = deposits(info, own, past)
+    info = own[:, 0, 4096:4112].astype(jnp.int32).reshape(32, 8)
+    past_info = past[:, 0, 2048:2064].astype(jnp.int32).reshape(32, 8)
+    region, cell = own_deposits(info, own.reshape(528, 128))
+    region = past_deposits(past_info, past.reshape(272, 128), region)
     held = traded(region.reshape(16, 256, 128), "grp").reshape(128, 32, 128)
     total_density, spectrum = forward_z(background, held, tables, cell)
     spectrum = traded(spectrum.reshape(256, 1, 2176), BOTH).reshape(4352, 128)

time: 178 us -> 176 us (0.989)
  waiting for transfers between devices: 2.02 us -> 0.01 us
    ppermute x1, waiting for transfers between devices: 2.02 us -> 0.01 us  [along_frag(): return lax.ppermute(block, 'frag', route)]
    pallas_call x1 -> x2, Pallas kernels: 2.93 us -> 3.9 us  [the longest x1 2.1 us: own_deposits(): pl.pallas_call(own_kernel, in_specs=[pl.BlockSpec(memory_space=pltpu.SMEM...]
  transfers between devices with their start and end apart: 1 -> 1, of which waited for: 1 -> 0; matrix products, arithmetic and copies ran while one was open for 0% -> 0% of each run, Pallas kernels for 0% -> 1%
where the time goes in v8:
time: 176 us
  blocking collectives  148 us (84%)
  Pallas kernels  23.4 us (13%)
  starting transfers between devices  3.65 us (2%)
    all_to_all x5, blocking collectives, traded(): return lax.all_to_all(block, axis, split_axis=0, concat_axis=0, tiled=True)  148 us
    pallas_call x1, Pallas kernels, solve_planes(): pl.pallas_call(planes_kernel, grid=(2,), in_specs=[pl.BlockSpec(memory_sp...  6.77 us
    pallas_call x1, Pallas kernels, densities(): pl.pallas_call(density_kernel, in_specs=[pl.BlockSpec(memory_space=pltpu....  6.41 us
    ppermute x1, starting transfers between devices, along_frag(): return lax.ppermute(block, 'frag', route)  3.65 us
  transfers between devices with their start and end apart: 1, of which 0 were waited for; matrix products, arithmetic and copies ran while one was open for 0% of the time, Pallas kernels for 1%

profile of v8, /device:TPU:1, one launch (start us, length us, event | category | flops | bytes accessed | tf_op | source)
XLA Modules:
  0.0 176.2 jit_solution(10881277459394251317)
XLA Ops:
  0.6 6.4 %densities.1 = f32[528,128]{1,0:T(8,128)} custom-call(s32[2,8]{1,0:T(2,128)} %info_ref.1, bf16[16,256,32]{2,1,0:T(8,128)(2,1)} %bitcast.25, bf16[4,2,256,1024]{3,2,1,0:T(8,128)(2,1)} %constant.19.clone.planes_ref, bf16[2,2,512,256]{3,2,1,0:T(8,128)(2,1)} %constant.20.clone.depths_ref), custom_call_target="tpu_custom_call" | custom-call | tf_op jit(solution)/shard_map/densities/pallas_call | solution.py:193
  7.1 15.2 %all_to_all.25 = f32[16,1,4224]{2,1,0:T(1,128)S(1)} all-to-all(f32[16,1,4224]{2,1,0:T(1,128)} %bitcast.24), channel_id=1, replica_groups=mesh['frag'=16,'grp'=16] {'grp'}, dimensions={0} | all-to-all | bytes 540672 | tf_op jit(solution)/shard_map/all_to_all | solution.py:565
  22.3 3.7 %collective-permute-start = (f32[16,1,2176]{2,1,0:T(1,128)S(1)}, f32[16,1,2176]{2,1,0:T(1,128)S(1)}, u32[]{:S(2)}, u32[]{:S(2)}) collective-permute-start(f32[16,1,2176]{2,1,0:T(1,128)S(1)} %slice.12), channel_id=1, source_target_pairs={{0,16},{16,32},{32,48},{48,64},{64,80},{80,96},{96,112},{112,128},... | collective-permute-start | bytes 417800 | tf_op jit(solution)/shard_map/ppermute | solution.py:561
  26.0 0.1 convert_element_type.17.info_ref
  26.0 2.1 %own_deposits.1 = (f32[32,4,32,128]{3,2,1,0:T(8,128)S(1)}, f32[8,128]{1,0:T(8,128)S(1)}) custom-call(s32[32,8]{1,0:T(8,128)S(1)} %convert_element_type.17.info_ref, f32[528,128]{1,0:T(8,128)S(1)} %bitcast.20), custom_call_target="tpu_custom_call" | custom-call | tf_op jit(solution)/shard_map/own_deposits/pallas_call | solution.py:290
  28.1 0.0 collective-permute-done
  28.2 0.1 convert_element_type.15.info_ref
  28.3 1.8 %past_deposits.1 = f32[32,4,32,128]{3,2,1,0:T(8,128)S(1)} custom-call(s32[32,8]{1,0:T(8,128)S(1)} %convert_element_type.15.info_ref, f32[272,128]{1,0:T(8,128)S(1)} %bitcast.23, f32[32,4,32,128]{3,2,1,0:T(8,128)S(1)} %get-tuple-element.9.in_ref), custom_call_target="tpu_custom_call", output_to_operand_aliasing={{}: (2, {})} | custom-call | tf_op jit(solution)/shard_map/past_deposits/pallas_call | solution.py:304
  30.1 0.0 copy-start
  30.1 0.0 copy-start.1
  30.1 27.8 %all_to_all.26 = f32[16,256,128]{2,1,0:T(8,128)S(1)} all-to-all(f32[16,256,128]{2,1,0:T(8,128)S(1)} %bitcast.17), channel_id=1, replica_groups=mesh['frag'=16,'grp'=16] {'grp'}, dimensions={0} | all-to-all | bytes 4194304 | tf_op jit(solution)/shard_map/all_to_all | solution.py:565
  57.9 0.0 copy-done
  57.9 0.0 copy-done.1
  57.9 3.0 %forward_z.1 = (f32[32,32,512]{2,1,0:T(8,128)}, f32[4352,128]{1,0:T(8,128)S(1)}) custom-call(f32[32,32,512]{2,1,0:T(8,128)S(1)} %copy-done.1, f32[128,32,128]{2,1,0:T(8,128)S(1)} %bitcast.18, bf16[10,256,256]{2,1,0:T(8,128)(2,1)S(1)} %copy-done, f32[8,128]{1,0:T(8,128)S(1)} %get-tuple-element.10.cell_ref), custom_call_target="tpu_custom_call" | custom-call | tf_op jit(solution)/shard_map/forward_z/pallas_call | solution.py:349
  60.8 0.0 copy-start.2
  60.8 68.7 %all_to_all.27 = f32[256,1,2176]{2,1,0:T(1,128)S(1)} all-to-all(f32[256,1,2176]{2,1,0:T(1,128)S(1)} %bitcast.19), channel_id=1, replica_groups=mesh['frag'=16,'grp'=16] {'frag','grp'}, dimensions={0} | all-to-all | bytes 4456448 | tf_op jit(solution)/shard_map/all_to_all | solution.py:565
  129.6 0.0 copy-done.2
  129.6 6.8 %solve_planes.1 = f32[768,128]{1,0:T(8,128)S(1)} custom-call(s32[1]{0:T(128)} %bitcast.place_ref, f32[4352,128]{1,0:T(8,128)S(1)} %bitcast.16, bf16[10,256,256]{2,1,0:T(8,128)(2,1)S(1)} %copy-done, bf16[2,576,512]{2,1,0:T(8,128)(2,1)S(1)} %copy-done.2), custom_call_target="tpu_custom_call" | custom-call | tf_op jit(solution)/shard_map/solve_planes/pallas_call | solution.py:446
  136.4 0.0 copy-start.3
  136.4 25.8 %all_to_all.28 = f32[256,1,384]{2,1,0:T(1,128)S(1)} all-to-all(f32[256,1,384]{2,1,0:T(1,128)S(1)} %bitcast.22), channel_id=1, replica_groups=mesh['frag'=16,'grp'=16] {'frag','grp'}, dimensions={0} | all-to-all | bytes 786432 | tf_op jit(solution)/shard_map/all_to_all | solution.py:565
  162.2 1.8 %boxes.1 = f32[16,32,128]{2,1,0:T(8,128)S(1)} custom-call(s32[32,8]{1,0:T(8,128)S(1)} %convert_element_type.17.info_ref, f32[768,128]{1,0:T(8,128)S(1)} %bitcast.21, bf16[10,256,256]{2,1,0:T(8,128)(2,1)S(1)} %copy-done), custom_call_target="tpu_custom_call" | custom-call | tf_op jit(solution)/shard_map/boxes/pallas_call | solution.py:511
  164.0 10.6 %all_to_all.29.in_ref = f32[16,32,128]{2,1,0:T(8,128)S(1)} all-to-all(f32[16,32,128]{2,1,0:T(8,128)S(1)} %boxes.1), channel_id=1, replica_groups=mesh['frag'=16,'grp'=16] {'grp'}, dimensions={0} | all-to-all | bytes 524288 | tf_op jit(solution)/shard_map/all_to_all | solution.py:565
  174.6 0.0 copy-done.3
  174.6 1.5 lay_out.1
  (3 shorter events, 0.1 us)
Async XLA Ops:
  22.3 5.9 %collective-permute-start = (f32[16,1,2176]{2,1,0:T(1,128)S(1)}, f32[16,1,2176]{2,1,0:T(1,128)S(1)}, u32[]{:S(2)}, u32[]{:S(2)}) collective-permute-start(f32[16,1,2176]{2,1,0:T(1,128)S(1)} %slice.12), channel_id=1, source_target_pairs={{0,16},{16,32},{32,48},{48,64},{64,80},{80,96},{96,112},{112,128},... | collective-permute-start | bytes 417800 | tf_op jit(solution)/shard_map/ppermute | solution.py:561
  30.1 27.8 %copy-start = (bf16[10,256,256]{2,1,0:T(8,128)(2,1)S(1)}, bf16[10,256,256]{2,1,0:T(8,128)(2,1)}, u32[]{:S(2)}) copy-start(bf16[10,256,256]{2,1,0:T(8,128)(2,1)} %constant.17.clone.table_ref.tables_ref) | copy-start | bytes 3932164
  30.1 27.8 %copy-start.1 = (f32[32,32,512]{2,1,0:T(8,128)S(1)}, f32[32,32,512]{2,1,0:T(8,128)}, u32[]{:S(2)}) copy-start(f32[32,32,512]{2,1,0:T(8,128)} %back_ref.1) | copy-start | bytes 6291460
  60.8 68.7 %copy-start.2 = (bf16[2,576,512]{2,1,0:T(8,128)(2,1)S(1)}, bf16[2,576,512]{2,1,0:T(8,128)(2,1)}, u32[]{:S(2)}) copy-start(bf16[2,576,512]{2,1,0:T(8,128)(2,1)} %constant.18.clone.window_ref) | copy-start | bytes 3538948
  136.4 38.3 %copy-start.3 = (s32[2,8]{1,0:T(2,128)S(1)}, s32[2,8]{1,0:T(2,128)}, u32[]{:S(2)}) copy-start(s32[2,8]{1,0:T(2,128)} %info_ref.1) | copy-start | bytes 196

commit v9 on v8

--- a/solution.py
+++ b/solution.py
@@ -213,16 +213,11 @@
 
 
 def first_cell(info_ref):
-    def touched(number):
-        cell = info_ref[number, 1]
-        return cell >> 1, ((cell + info_ref[number, 4] - 1) & 31) >> 1
-
-    first, last = touched(0)
-    shared = jnp.int32(1)
+    root = info_ref[0, 1]
+    lowest = jnp.int32(0)
     for number in range(1, 32):
-        one, other = touched(number)
-        shared = shared * ((one == first) | (other == first)).astype(jnp.int32)
-    return (2 * jnp.where(shared == 1, first, last) + 31) & 31
+        lowest = jnp.minimum(lowest, ((info_ref[number, 1] - root + 16) & 31) - 16)
+    return (root + lowest) & 31
 
 
 def landing(info_ref, number):
@@ -363,7 +358,7 @@
             jax.ShapeDtypeStruct((32, 32, 512), F32),
             jax.ShapeDtypeStruct((4352, 128), F32),
         ],
-        scratch_shapes=[pltpu.VMEM((4, 8 * PITCH, 128), F32)],
+        scratch_shapes=[pltpu.VMEM((4, 9 * PITCH, 128), F32)],
         compiler_params=pltpu.CompilerParams(vmem_limit_bytes=VMEM_LIMIT),
         name="forward_z",
     )(background, held, table, cell)

time: 176 us -> 176 us (level)
  no operation moved by 1% of the time
where the time goes in v9:
time: 176 us
  blocking collectives  148 us (84%)
  Pallas kernels  23.3 us (13%)
  starting transfers between devices  3.65 us (2%)
    all_to_all x5, blocking collectives, traded(): return lax.all_to_all(block, axis, split_axis=0, concat_axis=0, tiled=True)  148 us
    pallas_call x1, Pallas kernels, solve_planes(): pl.pallas_call(planes_kernel, grid=(2,), in_specs=[pl.BlockSpec(memory_sp...  6.78 us
    pallas_call x1, Pallas kernels, densities(): pl.pallas_call(density_kernel, in_specs=[pl.BlockSpec(memory_space=pltpu....  6.41 us
    ppermute x1, starting transfers between devices, along_frag(): return lax.ppermute(block, 'frag', route)  3.65 us
  transfers between devices with their start and end apart: 1, of which 0 were waited for; matrix products, arithmetic and copies ran while one was open for 0% of the time, Pallas kernels for 1%

profile of v9, /device:TPU:1, one launch (start us, length us, event | category | flops | bytes accessed | tf_op | source)
XLA Modules:
  0.0 176.1 jit_solution(2146496586685373398)
XLA Ops:
  0.6 6.4 %densities.1 = f32[528,128]{1,0:T(8,128)} custom-call(s32[2,8]{1,0:T(2,128)} %info_ref.1, bf16[16,256,32]{2,1,0:T(8,128)(2,1)} %bitcast.25, bf16[4,2,256,1024]{3,2,1,0:T(8,128)(2,1)} %constant.19.clone.planes_ref, bf16[2,2,512,256]{3,2,1,0:T(8,128)(2,1)} %constant.20.clone.depths_ref), custom_call_target="tpu_custom_call" | custom-call | tf_op jit(solution)/shard_map/densities/pallas_call | solution.py:193
  7.1 15.2 %all_to_all.25 = f32[16,1,4224]{2,1,0:T(1,128)S(1)} all-to-all(f32[16,1,4224]{2,1,0:T(1,128)} %bitcast.24), channel_id=1, replica_groups=mesh['frag'=16,'grp'=16] {'grp'}, dimensions={0} | all-to-all | bytes 540672 | tf_op jit(solution)/shard_map/all_to_all | solution.py:560
  22.3 3.7 %collective-permute-start = (f32[16,1,2176]{2,1,0:T(1,128)S(1)}, f32[16,1,2176]{2,1,0:T(1,128)S(1)}, u32[]{:S(2)}, u32[]{:S(2)}) collective-permute-start(f32[16,1,2176]{2,1,0:T(1,128)S(1)} %slice.12), channel_id=1, source_target_pairs={{0,16},{16,32},{32,48},{48,64},{64,80},{80,96},{96,112},{112,128},... | collective-permute-start | bytes 417800 | tf_op jit(solution)/shard_map/ppermute | solution.py:556
  26.0 0.1 convert_element_type.17.info_ref
  26.0 2.1 %own_deposits.1 = (f32[32,4,32,128]{3,2,1,0:T(8,128)S(1)}, f32[8,128]{1,0:T(8,128)S(1)}) custom-call(s32[32,8]{1,0:T(8,128)S(1)} %convert_element_type.17.info_ref, f32[528,128]{1,0:T(8,128)S(1)} %bitcast.20), custom_call_target="tpu_custom_call" | custom-call | tf_op jit(solution)/shard_map/own_deposits/pallas_call | solution.py:285
  28.1 0.0 collective-permute-done
  28.2 0.1 convert_element_type.15.info_ref
  28.3 1.8 %past_deposits.1 = f32[32,4,32,128]{3,2,1,0:T(8,128)S(1)} custom-call(s32[32,8]{1,0:T(8,128)S(1)} %convert_element_type.15.info_ref, f32[272,128]{1,0:T(8,128)S(1)} %bitcast.23, f32[32,4,32,128]{3,2,1,0:T(8,128)S(1)} %get-tuple-element.9.in_ref), custom_call_target="tpu_custom_call", output_to_operand_aliasing={{}: (2, {})} | custom-call | tf_op jit(solution)/shard_map/past_deposits/pallas_call | solution.py:299
  30.1 0.0 copy-start
  30.1 0.0 copy-start.1
  30.1 27.8 %all_to_all.26 = f32[16,256,128]{2,1,0:T(8,128)S(1)} all-to-all(f32[16,256,128]{2,1,0:T(8,128)S(1)} %bitcast.17), channel_id=1, replica_groups=mesh['frag'=16,'grp'=16] {'grp'}, dimensions={0} | all-to-all | bytes 4194304 | tf_op jit(solution)/shard_map/all_to_all | solution.py:560
  57.9 0.0 copy-done
  57.9 0.0 copy-done.1
  57.9 2.9 %forward_z.1 = (f32[32,32,512]{2,1,0:T(8,128)}, f32[4352,128]{1,0:T(8,128)S(1)}) custom-call(f32[32,32,512]{2,1,0:T(8,128)S(1)} %copy-done.1, f32[128,32,128]{2,1,0:T(8,128)S(1)} %bitcast.18, bf16[10,256,256]{2,1,0:T(8,128)(2,1)S(1)} %copy-done, f32[8,128]{1,0:T(8,128)S(1)} %get-tuple-element.10.cell_ref), custom_call_target="tpu_custom_call" | custom-call | tf_op jit(solution)/shard_map/forward_z/pallas_call | solution.py:344
  60.8 0.0 copy-start.2
  60.8 68.7 %all_to_all.27 = f32[256,1,2176]{2,1,0:T(1,128)S(1)} all-to-all(f32[256,1,2176]{2,1,0:T(1,128)S(1)} %bitcast.19), channel_id=1, replica_groups=mesh['frag'=16,'grp'=16] {'frag','grp'}, dimensions={0} | all-to-all | bytes 4456448 | tf_op jit(solution)/shard_map/all_to_all | solution.py:560
  129.5 0.0 copy-done.2
  129.5 6.8 %solve_planes.1 = f32[768,128]{1,0:T(8,128)S(1)} custom-call(s32[1]{0:T(128)} %bitcast.place_ref, f32[4352,128]{1,0:T(8,128)S(1)} %bitcast.16, bf16[10,256,256]{2,1,0:T(8,128)(2,1)S(1)} %copy-done, bf16[2,576,512]{2,1,0:T(8,128)(2,1)S(1)} %copy-done.2), custom_call_target="tpu_custom_call" | custom-call | tf_op jit(solution)/shard_map/solve_planes/pallas_call | solution.py:441
  136.3 0.0 copy-start.3
  136.3 25.8 %all_to_all.28 = f32[256,1,384]{2,1,0:T(1,128)S(1)} all-to-all(f32[256,1,384]{2,1,0:T(1,128)S(1)} %bitcast.22), channel_id=1, replica_groups=mesh['frag'=16,'grp'=16] {'frag','grp'}, dimensions={0} | all-to-all | bytes 786432 | tf_op jit(solution)/shard_map/all_to_all | solution.py:560
  162.1 1.8 %boxes.1 = f32[16,32,128]{2,1,0:T(8,128)S(1)} custom-call(s32[32,8]{1,0:T(8,128)S(1)} %convert_element_type.17.info_ref, f32[768,128]{1,0:T(8,128)S(1)} %bitcast.21, bf16[10,256,256]{2,1,0:T(8,128)(2,1)S(1)} %copy-done), custom_call_target="tpu_custom_call" | custom-call | tf_op jit(solution)/shard_map/boxes/pallas_call | solution.py:506
  163.9 10.6 %all_to_all.29.in_ref = f32[16,32,128]{2,1,0:T(8,128)S(1)} all-to-all(f32[16,32,128]{2,1,0:T(8,128)S(1)} %boxes.1), channel_id=1, replica_groups=mesh['frag'=16,'grp'=16] {'grp'}, dimensions={0} | all-to-all | bytes 524288 | tf_op jit(solution)/shard_map/all_to_all | solution.py:560
  174.5 0.0 copy-done.3
  174.5 1.5 lay_out.1
  (3 shorter events, 0.1 us)
Async XLA Ops:
  22.3 5.9 %collective-permute-start = (f32[16,1,2176]{2,1,0:T(1,128)S(1)}, f32[16,1,2176]{2,1,0:T(1,128)S(1)}, u32[]{:S(2)}, u32[]{:S(2)}) collective-permute-start(f32[16,1,2176]{2,1,0:T(1,128)S(1)} %slice.12), channel_id=1, source_target_pairs={{0,16},{16,32},{32,48},{48,64},{64,80},{80,96},{96,112},{112,128},... | collective-permute-start | bytes 417800 | tf_op jit(solution)/shard_map/ppermute | solution.py:556
  30.1 27.8 %copy-start = (bf16[10,256,256]{2,1,0:T(8,128)(2,1)S(1)}, bf16[10,256,256]{2,1,0:T(8,128)(2,1)}, u32[]{:S(2)}) copy-start(bf16[10,256,256]{2,1,0:T(8,128)(2,1)} %constant.17.clone.table_ref.tables_ref) | copy-start | bytes 3932164
  30.1 27.8 %copy-start.1 = (f32[32,32,512]{2,1,0:T(8,128)S(1)}, f32[32,32,512]{2,1,0:T(8,128)}, u32[]{:S(2)}) copy-start(f32[32,32,512]{2,1,0:T(8,128)} %back_ref.1) | copy-start | bytes 6291460
  60.8 68.7 %copy-start.2 = (bf16[2,576,512]{2,1,0:T(8,128)(2,1)S(1)}, bf16[2,576,512]{2,1,0:T(8,128)(2,1)}, u32[]{:S(2)}) copy-start(bf16[2,576,512]{2,1,0:T(8,128)(2,1)} %constant.18.clone.window_ref) | copy-start | bytes 3538948
  136.3 38.3 %copy-start.3 = (s32[2,8]{1,0:T(2,128)S(1)}, s32[2,8]{1,0:T(2,128)}, u32[]{:S(2)}) copy-start(s32[2,8]{1,0:T(2,128)} %info_ref.1) | copy-start | bytes 196

commit v10 on v9

--- a/solution.py
+++ b/solution.py
@@ -132,19 +132,27 @@
     depth_ref,
     sems,
 ):
-    orbitals_copy = pltpu.make_async_copy(source_ref, orbitals_ref, sems.at[4])
+    orbitals_copy = pltpu.make_async_copy(source_ref, orbitals_ref, sems.at[6])
     orbitals_copy.start()
     copies = []
     for f in range(2):
         pair = 2 * info_ref[f, 4] + info_ref[f, 5] - 3
-        copies.append(pltpu.make_async_copy(planes_ref.at[pair], plane_ref.at[f], sems.at[2 * f]))
         copies.append(
             pltpu.make_async_copy(
-                depths_ref.at[info_ref[f, 3] - 1], depth_ref.at[f], sems.at[2 * f + 1]
+                depths_ref.at[info_ref[f, 3] - 1], depth_ref.at[f], sems.at[3 * f]
             )
         )
-    copies[0].start()
-    copies[1].start()
+        for half in range(2):
+            columns = pl.ds(512 * half, 512)
+            copies.append(
+                pltpu.make_async_copy(
+                    planes_ref.at[pair, :, :, columns],
+                    plane_ref.at[f, :, :, columns],
+                    sems.at[3 * f + 1 + half],
+                )
+            )
+    for copy in copies[:3]:
+        copy.start()
     orbitals_copy.wait()
     for a in range(16):
         coeff_ref[a] = jnp.transpose(orbitals_ref[a].astype(F32)).astype(BF16)
@@ -152,12 +160,13 @@
         count = info_ref[f, 7]
         scale = 2.0 * info_ref[f, 6].astype(F32)
         coeffs = coeff_ref[:, 16 * f : 16 * f + 16, :].reshape(256, 256)
-        copies[2 * f].wait()
-        copies[2 * f + 1].wait()
-        if f == 0:
-            copies[2].start()
-            copies[3].start()
+        copies[3 * f].wait()
         for part in range(4):
+            if part % 2 == 0:
+                copies[3 * f + 1 + part // 2].wait()
+            if f == 0 and part == 2:
+                for copy in copies[3:]:
+                    copy.start()
             columns = slice(part * 256, (part + 1) * 256)
             flat = jnp.dot(coeffs, plane_ref[f, 1, :, columns], preferred_element_type=F32)
             flat += jnp.dot(coeffs, plane_ref[f, 0, :, columns], preferred_element_type=F32)
@@ -205,7 +214,7 @@
             pltpu.VMEM((16, 32, 256), BF16),
             pltpu.VMEM((2, 2, 256, 1024), BF16),
             pltpu.VMEM((2, 2, 512, 256), BF16),
-            pltpu.SemaphoreType.DMA((5,)),
+            pltpu.SemaphoreType.DMA((7,)),
         ],
         compiler_params=pltpu.CompilerParams(vmem_limit_bytes=56 * 1024 * 1024),
         name="densities",

time: 176 us -> 177 us (level)
  no operation moved by 1% of the time
where the time goes in v10:
time: 177 us
  blocking collectives  148 us (84%)
  Pallas kernels  24 us (14%)
  starting transfers between devices  3.66 us (2%)
    all_to_all x5, blocking collectives, traded(): return lax.all_to_all(block, axis, split_axis=0, concat_axis=0, tiled=True)  148 us
    pallas_call x1, Pallas kernels, densities(): pl.pallas_call(density_kernel, in_specs=[pl.BlockSpec(memory_space=pltpu....  7.08 us
    pallas_call x1, Pallas kernels, solve_planes(): pl.pallas_call(planes_kernel, grid=(2,), in_specs=[pl.BlockSpec(memory_sp...  6.78 us
    ppermute x1, starting transfers between devices, along_frag(): return lax.ppermute(block, 'frag', route)  3.66 us
  transfers between devices with their start and end apart: 1, of which 0 were waited for; matrix products, arithmetic and copies ran while one was open for 0% of the time, Pallas kernels for 1%

profile of v10, /device:TPU:1, one launch (start us, length us, event | category | flops | bytes accessed | tf_op | source)
XLA Modules:
  0.0 176.8 jit_solution(1442001727259141632)
XLA Ops:
  0.6 7.1 %densities.1 = f32[528,128]{1,0:T(8,128)} custom-call(s32[2,8]{1,0:T(2,128)} %info_ref.1, bf16[16,256,32]{2,1,0:T(8,128)(2,1)} %bitcast.25, bf16[4,2,256,1024]{3,2,1,0:T(8,128)(2,1)} %constant.19.clone.planes_ref, bf16[2,2,512,256]{3,2,1,0:T(8,128)(2,1)} %constant.20.clone.depths_ref), custom_call_target="tpu_custom_call" | custom-call | tf_op jit(solution)/shard_map/densities/pallas_call | solution.py:202
  7.7 15.2 %all_to_all.25 = f32[16,1,4224]{2,1,0:T(1,128)S(1)} all-to-all(f32[16,1,4224]{2,1,0:T(1,128)} %bitcast.24), channel_id=1, replica_groups=mesh['frag'=16,'grp'=16] {'grp'}, dimensions={0} | all-to-all | bytes 540672 | tf_op jit(solution)/shard_map/all_to_all | solution.py:569
  22.9 3.7 %collective-permute-start = (f32[16,1,2176]{2,1,0:T(1,128)S(1)}, f32[16,1,2176]{2,1,0:T(1,128)S(1)}, u32[]{:S(2)}, u32[]{:S(2)}) collective-permute-start(f32[16,1,2176]{2,1,0:T(1,128)S(1)} %slice.12), channel_id=1, source_target_pairs={{0,16},{16,32},{32,48},{48,64},{64,80},{80,96},{96,112},{112,128},... | collective-permute-start | bytes 417800 | tf_op jit(solution)/shard_map/ppermute | solution.py:565
  26.6 0.1 convert_element_type.17.info_ref
  26.7 2.1 %own_deposits.1 = (f32[32,4,32,128]{3,2,1,0:T(8,128)S(1)}, f32[8,128]{1,0:T(8,128)S(1)}) custom-call(s32[32,8]{1,0:T(8,128)S(1)} %convert_element_type.17.info_ref, f32[528,128]{1,0:T(8,128)S(1)} %bitcast.20), custom_call_target="tpu_custom_call" | custom-call | tf_op jit(solution)/shard_map/own_deposits/pallas_call | solution.py:294
  28.8 0.0 collective-permute-done
  28.9 0.1 convert_element_type.15.info_ref
  28.9 1.8 %past_deposits.1 = f32[32,4,32,128]{3,2,1,0:T(8,128)S(1)} custom-call(s32[32,8]{1,0:T(8,128)S(1)} %convert_element_type.15.info_ref, f32[272,128]{1,0:T(8,128)S(1)} %bitcast.23, f32[32,4,32,128]{3,2,1,0:T(8,128)S(1)} %get-tuple-element.9.in_ref), custom_call_target="tpu_custom_call", output_to_operand_aliasing={{}: (2, {})} | custom-call | tf_op jit(solution)/shard_map/past_deposits/pallas_call | solution.py:308
  30.7 0.0 copy-start
  30.7 0.0 copy-start.1
  30.8 27.8 %all_to_all.26 = f32[16,256,128]{2,1,0:T(8,128)S(1)} all-to-all(f32[16,256,128]{2,1,0:T(8,128)S(1)} %bitcast.17), channel_id=1, replica_groups=mesh['frag'=16,'grp'=16] {'grp'}, dimensions={0} | all-to-all | bytes 4194304 | tf_op jit(solution)/shard_map/all_to_all | solution.py:569
  58.5 0.0 copy-done
  58.5 0.0 copy-done.1
  58.5 2.9 %forward_z.1 = (f32[32,32,512]{2,1,0:T(8,128)}, f32[4352,128]{1,0:T(8,128)S(1)}) custom-call(f32[32,32,512]{2,1,0:T(8,128)S(1)} %copy-done.1, f32[128,32,128]{2,1,0:T(8,128)S(1)} %bitcast.18, bf16[10,256,256]{2,1,0:T(8,128)(2,1)S(1)} %copy-done, f32[8,128]{1,0:T(8,128)S(1)} %get-tuple-element.10.cell_ref), custom_call_target="tpu_custom_call" | custom-call | tf_op jit(solution)/shard_map/forward_z/pallas_call | solution.py:353
  61.4 0.0 copy-start.2
  61.4 68.8 %all_to_all.27 = f32[256,1,2176]{2,1,0:T(1,128)S(1)} all-to-all(f32[256,1,2176]{2,1,0:T(1,128)S(1)} %bitcast.19), channel_id=1, replica_groups=mesh['frag'=16,'grp'=16] {'frag','grp'}, dimensions={0} | all-to-all | bytes 4456448 | tf_op jit(solution)/shard_map/all_to_all | solution.py:569
  130.2 0.0 copy-done.2
  130.2 6.8 %solve_planes.1 = f32[768,128]{1,0:T(8,128)S(1)} custom-call(s32[1]{0:T(128)} %bitcast.place_ref, f32[4352,128]{1,0:T(8,128)S(1)} %bitcast.16, bf16[10,256,256]{2,1,0:T(8,128)(2,1)S(1)} %copy-done, bf16[2,576,512]{2,1,0:T(8,128)(2,1)S(1)} %copy-done.2), custom_call_target="tpu_custom_call" | custom-call | tf_op jit(solution)/shard_map/solve_planes/pallas_call | solution.py:450
  137.0 0.0 copy-start.3
  137.0 25.8 %all_to_all.28 = f32[256,1,384]{2,1,0:T(1,128)S(1)} all-to-all(f32[256,1,384]{2,1,0:T(1,128)S(1)} %bitcast.22), channel_id=1, replica_groups=mesh['frag'=16,'grp'=16] {'frag','grp'}, dimensions={0} | all-to-all | bytes 786432 | tf_op jit(solution)/shard_map/all_to_all | solution.py:569
  162.8 1.8 %boxes.1 = f32[16,32,128]{2,1,0:T(8,128)S(1)} custom-call(s32[32,8]{1,0:T(8,128)S(1)} %convert_element_type.17.info_ref, f32[768,128]{1,0:T(8,128)S(1)} %bitcast.21, bf16[10,256,256]{2,1,0:T(8,128)(2,1)S(1)} %copy-done), custom_call_target="tpu_custom_call" | custom-call | tf_op jit(solution)/shard_map/boxes/pallas_call | solution.py:515
  164.6 10.6 %all_to_all.29.in_ref = f32[16,32,128]{2,1,0:T(8,128)S(1)} all-to-all(f32[16,32,128]{2,1,0:T(8,128)S(1)} %boxes.1), channel_id=1, replica_groups=mesh['frag'=16,'grp'=16] {'grp'}, dimensions={0} | all-to-all | bytes 524288 | tf_op jit(solution)/shard_map/all_to_all | solution.py:569
  175.2 0.0 copy-done.3
  175.2 1.5 lay_out.1
  (3 shorter events, 0.1 us)
Async XLA Ops:
  22.9 5.9 %collective-permute-start = (f32[16,1,2176]{2,1,0:T(1,128)S(1)}, f32[16,1,2176]{2,1,0:T(1,128)S(1)}, u32[]{:S(2)}, u32[]{:S(2)}) collective-permute-start(f32[16,1,2176]{2,1,0:T(1,128)S(1)} %slice.12), channel_id=1, source_target_pairs={{0,16},{16,32},{32,48},{48,64},{64,80},{80,96},{96,112},{112,128},... | collective-permute-start | bytes 417800 | tf_op jit(solution)/shard_map/ppermute | solution.py:565
  30.7 27.8 %copy-start = (bf16[10,256,256]{2,1,0:T(8,128)(2,1)S(1)}, bf16[10,256,256]{2,1,0:T(8,128)(2,1)}, u32[]{:S(2)}) copy-start(bf16[10,256,256]{2,1,0:T(8,128)(2,1)} %constant.17.clone.table_ref.tables_ref) | copy-start | bytes 3932164
  30.7 27.8 %copy-start.1 = (f32[32,32,512]{2,1,0:T(8,128)S(1)}, f32[32,32,512]{2,1,0:T(8,128)}, u32[]{:S(2)}) copy-start(f32[32,32,512]{2,1,0:T(8,128)} %back_ref.1) | copy-start | bytes 6291460
  61.4 68.8 %copy-start.2 = (bf16[2,576,512]{2,1,0:T(8,128)(2,1)S(1)}, bf16[2,576,512]{2,1,0:T(8,128)(2,1)}, u32[]{:S(2)}) copy-start(bf16[2,576,512]{2,1,0:T(8,128)(2,1)} %constant.18.clone.window_ref) | copy-start | bytes 3538948
  137.0 38.3 %copy-start.3 = (s32[2,8]{1,0:T(2,128)S(1)}, s32[2,8]{1,0:T(2,128)}, u32[]{:S(2)}) copy-start(s32[2,8]{1,0:T(2,128)} %info_ref.1) | copy-start | bytes 196
